TPU v7x, 32 devices: a whole 2x2x4 slice. The times are simulated.
32 devices in a mesh: seq: 4 (over z), rows: 8 (over y, x, core).
Axes of the slice: x: 2, y: 2, z: 4, core: 2. Of those that a mesh axis runs over, the one named last changes fastest.
Arguments:
- tokens: bfloat16 [8, 1024, 1536], P('rows', 'seq'), may hold values from -6 to 6
- resets: int32 [8, 1024], P('rows', 'seq'), may hold values from 0 to 1, as said below
- norm_gain: bfloat16 [1536], P('rows'), may hold values from 0.5 to 1.5
- in_proj: bfloat16 [1536, 6144], P('rows'), may hold values from -0.15625 to 0.15625
- x_proj: bfloat16 [3072, 128], P('rows'), may hold values from -0.3125 to 0.3125
- dt_proj: bfloat16 [96, 3072], P(None, 'rows'), may hold values from -0.625 to 0.625
- conv_weight: bfloat16 [4, 3072], P(None, 'rows'), may hold values from -3 to 3
- conv_bias: bfloat16 [3072], P('rows'), may hold values from -3 to 3
- dt_bias: bfloat16 [3072], P('rows'), may hold values from -6 to -2
- a_log: bfloat16 [16, 3072], P(None, 'rows'), may hold values from -4.59375 to 2.796875
- out_proj: bfloat16 [3072, 1536], P('rows'), may hold values from -0.109375 to 0.109375
- cotangent: bfloat16 [8, 1024, 1536], P('rows', 'seq'), may hold values from -6 to 6
Outputs:
- block_out: bfloat16 [8, 1024, 1536], P('rows', 'seq')
- d_tokens: bfloat16 [8, 1024, 1536], P('rows', 'seq')
- d_norm_gain: float32 [1536], P('rows')
- d_in_proj: float32 [1536, 6144], P('rows')
- d_x_proj: float32 [3072, 128], P('rows')
- d_dt_proj: float32 [96, 3072], P(None, 'rows')
- d_conv_weight: float32 [4, 3072], P(None, 'rows')
- d_conv_bias: float32 [3072], P('rows')
- d_dt_bias: float32 [3072], P('rows')
- d_a_log: float32 [16, 3072], P(None, 'rows')
- d_out_proj: float32 [3072, 1536], P('rows')
Inputs may be any that keep to these rules, and one draw needn't show every extreme that they name: `resets`: each packed row holds either one item of 1024 tokens or four items of 256 tokens; a 1 marks an item's first token, so every row starts with 1, and some row holds a single item in every draw.
All inputs are finite; a program needn't handle non-finite values.
Results may differ from a plain program's by a relative error of at most 0.019.
Values may be sent and summed in bfloat16 or wider, within the bound.
A program may use at most 256 MiB of HBM per device.

v0:
```python
import math

import jax
import jax.numpy as jnp
from jax import lax
from jax.sharding import PartitionSpec as P

D = 1536
E = 3072
R = 96
NS = 16
KC = 4
RD = 1


epsilon = 1e-05


def from_behind(value, axis, steps):
    count = lax.axis_size(axis)
    first, last = (max(0, -steps), min(count, count - steps))
    return lax.ppermute(value, axis, [(source, source + steps) for source in range(first, last)])


def carried_in(x, axis, combine, identity, reverse):
    count, place = (lax.axis_size(axis), lax.axis_index(axis))
    everything = jax.tree.map(
        lambda part, kind: lax.all_gather(part.astype(kind), axis), x, (jnp.bfloat16, jnp.bfloat16)
    )
    start = jax.tree.map(
        lambda part, zero: jnp.broadcast_to(jnp.asarray(zero, part.dtype), part.shape), x, identity
    )

    def step(k, before):
        at = count - 1 - k if reverse else k
        reached = at > place if reverse else at < place
        new = combine(
            before, jax.tree.map(lambda part, own: part[at].astype(own.dtype), everything, x)
        )
        return jax.tree.map(lambda a, b: jnp.where(reached, a, b), new, before)

    return lax.fori_loop(0, count, step, start)


def shortened(x):
    return jax.tree.map(lambda a: a.astype(jnp.bfloat16) if a.dtype == jnp.float32 else a, x)


def to_blocks(values, block_len):
    layout = values.shape
    pieces = values.reshape((layout[0], layout[1] // block_len, block_len) + layout[2:])
    return jnp.moveaxis(pieces, 1, 0)


def from_blocks(values):
    joined = jnp.moveaxis(values, 0, 1)
    layout = joined.shape
    return joined.reshape((layout[0], layout[1] * layout[2]) + layout[3:])


def combine_carry(earlier, later):
    return (later[0] + later[1] * earlier[0], earlier[1] * later[1])


def forward_states(
    initial, step_size, inputs, b_coef, c_coef, alive, decay_rate, block_len, want_out
):

    def advance(carried, pieces):
        step_delta, step_input, step_b, step_c, step_alive = pieces
        entering = carried
        outputs = []
        for offset in range(block_len):
            decay_now = (
                jnp.exp(step_delta[:, offset, None, :] * decay_rate[None])
                * step_alive[:, offset, None, None]
            )
            carried = (
                decay_now * carried
                + (step_delta[:, offset] * step_input[:, offset])[:, None, :]
                * step_b[:, offset, :, None]
            )
            if want_out:
                outputs.append(jnp.sum(carried * step_c[:, offset, :, None], axis=1))
        if want_out:
            return (carried, (entering, jnp.stack(outputs, axis=1)))
        return (carried, None)

    pieces = (
        to_blocks(step_size, block_len),
        to_blocks(inputs, block_len),
        to_blocks(b_coef, block_len),
        to_blocks(c_coef, block_len),
        to_blocks(alive, block_len),
    )
    return lax.scan(advance, initial, pieces)


def reverse_decay(initial, step_size, c_coef, grad_y, alive, decay_rate, block_len):

    def reverse_retreat(running, pieces):
        step_delta, step_c, step_grad, step_alive = pieces
        for offset in reversed(range(block_len)):
            running = running + step_c[:, offset, :, None] * step_grad[:, offset, None, :]
            running = (
                running
                * jnp.exp(step_delta[:, offset, None, :] * decay_rate[None])
                * step_alive[:, offset, None, None]
            )
        return (running, None)

    pieces = (
        to_blocks(step_size, block_len),
        to_blocks(c_coef, block_len),
        to_blocks(grad_y, block_len),
        to_blocks(alive, block_len),
    )
    result, unused = lax.scan(reverse_retreat, initial, pieces, reverse=True)
    return result


def backward_states(
    incoming, block_starts, step_size, inputs, b_coef, c_coef, grad_y, alive, decay_rate, block_len
):

    def backward_retreat(running, pieces):
        grad_state, rate_sum = running
        entering, step_delta, step_input, step_b, step_c, step_grad, step_alive = pieces
        states = []
        decays = []
        current = entering
        for offset in range(block_len):
            decay_now = (
                jnp.exp(step_delta[:, offset, None, :] * decay_rate[None])
                * step_alive[:, offset, None, None]
            )
            current = (
                decay_now * current
                + (step_delta[:, offset] * step_input[:, offset])[:, None, :]
                * step_b[:, offset, :, None]
            )
            states.append(current)
            decays.append(decay_now)
        grad_delta_list = [None] * block_len
        grad_input_list = [None] * block_len
        grad_b_list = [None] * block_len
        grad_c_list = [None] * block_len
        for offset in reversed(range(block_len)):
            grad_state = grad_state + step_c[:, offset, :, None] * step_grad[:, offset, None, :]
            before = states[offset - 1] if offset > 0 else entering
            grad_c_list[offset] = jnp.sum(states[offset] * step_grad[:, offset, None, :], axis=2)
            weighted = grad_state * before * decays[offset]
            rate_sum = rate_sum + weighted * step_delta[:, offset, None, :]
            along_b = jnp.sum(grad_state * step_b[:, offset, :, None], axis=1)
            grad_delta_list[offset] = (
                jnp.sum(weighted * decay_rate[None], axis=1) + along_b * step_input[:, offset]
            )
            grad_input_list[offset] = along_b * step_delta[:, offset]
            grad_b_list[offset] = jnp.sum(
                grad_state * (step_delta[:, offset] * step_input[:, offset])[:, None, :], axis=2
            )
            grad_state = grad_state * decays[offset]
        stacked = (
            jnp.stack(grad_delta_list, axis=1),
            jnp.stack(grad_input_list, axis=1),
            jnp.stack(grad_b_list, axis=1),
            jnp.stack(grad_c_list, axis=1),
        )
        return ((grad_state, rate_sum), stacked)

    pieces = (
        block_starts,
        to_blocks(step_size, block_len),
        to_blocks(inputs, block_len),
        to_blocks(b_coef, block_len),
        to_blocks(c_coef, block_len),
        to_blocks(grad_y, block_len),
        to_blocks(alive, block_len),
    )
    return lax.scan(backward_retreat, (incoming, jnp.zeros_like(incoming)), pieces, reverse=True)


def local(
    tokens,
    resets,
    norm_gain,
    in_proj,
    x_proj,
    dt_proj,
    conv_weight,
    conv_bias,
    dt_bias,
    a_log,
    out_proj,
    cotangent,
):
    (
        gain_full,
        in_proj_full,
        x_proj_full,
        dt_proj_full,
        conv_weight_full,
        conv_bias_full,
        dt_bias_full,
        a_log_full,
        out_proj_full,
    ) = (
        lax.all_gather(norm_gain, "rows", axis=0, tiled=True),
        lax.all_gather(in_proj, "rows", axis=0, tiled=True),
        lax.all_gather(x_proj, "rows", axis=0, tiled=True),
        lax.all_gather(dt_proj, "rows", axis=1, tiled=True),
        lax.all_gather(conv_weight, "rows", axis=1, tiled=True),
        lax.all_gather(conv_bias, "rows", axis=0, tiled=True),
        lax.all_gather(dt_bias, "rows", axis=0, tiled=True),
        lax.all_gather(a_log, "rows", axis=1, tiled=True),
        lax.all_gather(out_proj, "rows", axis=0, tiled=True),
    )
    local_len = tokens.shape[1]
    tok_count = RD * local_len
    block_len = math.gcd(local_len, 16)
    flat_in = tokens.reshape(tok_count, D).astype(jnp.float32)
    inv_rms = lax.rsqrt(jnp.mean(flat_in * flat_in, axis=1, keepdims=True) + epsilon)
    gain_vec = gain_full.astype(jnp.float32)
    normed = (flat_in * inv_rms * gain_vec).astype(jnp.bfloat16)
    mixed_proj = jnp.dot(normed, in_proj_full, preferred_element_type=jnp.float32)
    conv_in = mixed_proj[:, :E].astype(jnp.bfloat16).reshape(RD, local_len, E)
    gate_pre = mixed_proj[:, E:].reshape(RD, local_len, E)
    left_rim = from_behind(conv_in[:, local_len - (KC - 1) :], "seq", 1)
    extended = jnp.concatenate([left_rim, conv_in], axis=1)
    kernel = conv_weight_full.astype(jnp.float32)
    conv_pre = conv_bias_full.astype(jnp.float32) + sum(
        (
            kernel[offset] * extended[:, offset : offset + local_len].astype(jnp.float32)
            for offset in range(KC)
        )
    )
    conv_out = jax.nn.silu(conv_pre).astype(jnp.bfloat16)
    flat_conv = conv_out.reshape(tok_count, E)
    projected = jnp.dot(flat_conv, x_proj_full, preferred_element_type=jnp.float32)
    rank_part = projected[:, :R].astype(jnp.bfloat16)
    b_coef = projected[:, R : R + NS].reshape(RD, local_len, NS)
    c_coef = projected[:, R + NS :].reshape(RD, local_len, NS)
    step_pre = jnp.dot(
        rank_part, dt_proj_full, preferred_element_type=jnp.float32
    ) + dt_bias_full.astype(jnp.float32)
    step_size = jax.nn.softplus(step_pre).reshape(RD, local_len, E)
    decay_rate = -jnp.exp(a_log_full.astype(jnp.float32))
    alive = (1 - resets).astype(jnp.float32)
    conv_float = conv_out.astype(jnp.float32)
    zeros_state = jnp.zeros((RD, NS, E), jnp.float32)
    ones_state = jnp.ones((RD, NS, E), jnp.float32)
    local_end, unused_ys = forward_states(
        zeros_state, step_size, conv_float, b_coef, c_coef, alive, decay_rate, block_len, False
    )
    no_reset = jnp.prod(alive, axis=1)
    through = (
        jnp.exp(decay_rate[None] * jnp.sum(step_size, axis=1)[:, None, :]) * no_reset[:, None, None]
    )
    carry_in, unused_product = carried_in(
        (local_end, through), "seq", combine_carry, (zeros_state, ones_state), False
    )
    final_state, (block_starts, scan_out) = forward_states(
        carry_in, step_size, conv_float, b_coef, c_coef, alive, decay_rate, block_len, True
    )
    scan_y = from_blocks(scan_out)
    gate_sig = jax.nn.sigmoid(gate_pre)
    gate_act = gate_pre * gate_sig
    gated = (scan_y * gate_act).astype(jnp.bfloat16).reshape(tok_count, E)
    branch = jnp.dot(gated, out_proj_full, preferred_element_type=jnp.float32)
    block_out = (flat_in + branch).astype(jnp.bfloat16).reshape(RD, local_len, D)
    flat_cot = cotangent.reshape(tok_count, D)
    grad_out_proj = lax.dot_general(
        gated, flat_cot, (((0,), (0,)), ((), ())), preferred_element_type=jnp.float32
    )
    grad_gated = lax.dot_general(
        flat_cot, out_proj_full, (((1,), (1,)), ((), ())), preferred_element_type=jnp.float32
    ).reshape(RD, local_len, E)
    grad_y = grad_gated * gate_act
    grad_gate_pre = grad_gated * scan_y * gate_sig * (1.0 + gate_pre * (1.0 - gate_sig))
    local_back = reverse_decay(zeros_state, step_size, c_coef, grad_y, alive, decay_rate, block_len)
    carry_back, unused_back = carried_in(
        (local_back, through), "seq", combine_carry, (zeros_state, ones_state), True
    )
    (unused_state, rate_total), (delta_blocks, input_blocks, b_blocks, c_blocks) = backward_states(
        carry_back,
        block_starts,
        step_size,
        conv_float,
        b_coef,
        c_coef,
        grad_y,
        alive,
        decay_rate,
        block_len,
    )
    grad_delta = from_blocks(delta_blocks)
    grad_input_scan = from_blocks(input_blocks)
    grad_b = from_blocks(b_blocks).reshape(tok_count, NS)
    grad_c = from_blocks(c_blocks).reshape(tok_count, NS)
    grad_a_log = jnp.sum(rate_total, axis=0) * decay_rate
    grad_step_pre = grad_delta.reshape(tok_count, E) * jax.nn.sigmoid(step_pre)
    grad_dt_bias = jnp.sum(grad_step_pre, axis=0)
    low_step = grad_step_pre.astype(jnp.bfloat16)
    grad_dt_proj = lax.dot_general(
        rank_part, low_step, (((0,), (0,)), ((), ())), preferred_element_type=jnp.float32
    )
    grad_rank = lax.dot_general(
        low_step, dt_proj_full, (((1,), (1,)), ((), ())), preferred_element_type=jnp.float32
    )
    grad_projected = jnp.concatenate([grad_rank, grad_b, grad_c], axis=1).astype(jnp.bfloat16)
    grad_x_proj = lax.dot_general(
        flat_conv, grad_projected, (((0,), (0,)), ((), ())), preferred_element_type=jnp.float32
    )
    back_conv = lax.dot_general(
        grad_projected, x_proj_full, (((1,), (1,)), ((), ())), preferred_element_type=jnp.float32
    ).reshape(RD, local_len, E)
    grad_conv_out = back_conv + grad_input_scan
    conv_sig = jax.nn.sigmoid(conv_pre)
    grad_conv_pre = grad_conv_out * conv_sig * (1.0 + conv_pre * (1.0 - conv_sig))
    grad_conv_bias = jnp.sum(grad_conv_pre, axis=(0, 1))
    ext_float = extended.astype(jnp.float32)
    grad_kernel = jnp.stack(
        [
            jnp.sum(grad_conv_pre * ext_float[:, offset : offset + local_len], axis=(0, 1))
            for offset in range(KC)
        ]
    )
    grad_ext = sum(
        (
            jnp.pad(kernel[offset] * grad_conv_pre, ((0, 0), (offset, KC - 1 - offset), (0, 0)))
            for offset in range(KC)
        )
    )
    right_rim = from_behind(shortened(grad_ext[:, : KC - 1]), "seq", -1)
    grad_conv_in = grad_ext[:, KC - 1 :] + jnp.pad(
        right_rim, ((0, 0), (local_len - (KC - 1), 0), (0, 0))
    )
    grad_mixed = jnp.concatenate(
        [grad_conv_in.reshape(tok_count, E), grad_gate_pre.reshape(tok_count, E)], axis=1
    ).astype(jnp.bfloat16)
    grad_in_proj = lax.dot_general(
        normed, grad_mixed, (((0,), (0,)), ((), ())), preferred_element_type=jnp.float32
    )
    grad_normed = lax.dot_general(
        grad_mixed, in_proj_full, (((1,), (1,)), ((), ())), preferred_element_type=jnp.float32
    )
    grad_gain = jnp.sum(grad_normed * flat_in * inv_rms, axis=0)
    grad_hat = grad_normed * gain_vec
    grad_norm_in = inv_rms * (
        grad_hat
        - flat_in * (inv_rms * inv_rms) * jnp.mean(grad_hat * flat_in, axis=1, keepdims=True)
    )
    d_tokens = (
        (flat_cot.astype(jnp.float32) + grad_norm_in).astype(jnp.bfloat16).reshape(RD, local_len, D)
    )
    partial_rows = (
        lax.psum_scatter(
            grad_gain.astype(jnp.bfloat16), "rows", scatter_dimension=0, tiled=True
        ).astype(jnp.float32),
        lax.psum_scatter(
            grad_in_proj.astype(jnp.bfloat16), "rows", scatter_dimension=0, tiled=True
        ).astype(jnp.float32),
        lax.psum_scatter(
            grad_x_proj.astype(jnp.bfloat16), "rows", scatter_dimension=0, tiled=True
        ).astype(jnp.float32),
        lax.psum_scatter(
            grad_dt_proj.astype(jnp.bfloat16), "rows", scatter_dimension=1, tiled=True
        ).astype(jnp.float32),
        lax.psum_scatter(
            grad_kernel.astype(jnp.bfloat16), "rows", scatter_dimension=1, tiled=True
        ).astype(jnp.float32),
        lax.psum_scatter(
            grad_conv_bias.astype(jnp.bfloat16), "rows", scatter_dimension=0, tiled=True
        ).astype(jnp.float32),
        lax.psum_scatter(
            grad_dt_bias.astype(jnp.bfloat16), "rows", scatter_dimension=0, tiled=True
        ).astype(jnp.float32),
        lax.psum_scatter(
            grad_a_log.astype(jnp.bfloat16), "rows", scatter_dimension=1, tiled=True
        ).astype(jnp.float32),
        lax.psum_scatter(
            grad_out_proj.astype(jnp.bfloat16), "rows", scatter_dimension=0, tiled=True
        ).astype(jnp.float32),
    )
    summed = (
        lax.psum(partial_rows[0].astype(jnp.bfloat16), "seq").astype(jnp.float32),
        lax.psum(partial_rows[1].astype(jnp.bfloat16), "seq").astype(jnp.float32),
        lax.psum(partial_rows[2].astype(jnp.bfloat16), "seq").astype(jnp.float32),
        lax.psum(partial_rows[3].astype(jnp.bfloat16), "seq").astype(jnp.float32),
        lax.psum(partial_rows[4].astype(jnp.bfloat16), "seq").astype(jnp.float32),
        lax.psum(partial_rows[5].astype(jnp.bfloat16), "seq").astype(jnp.float32),
        lax.psum(partial_rows[6].astype(jnp.bfloat16), "seq").astype(jnp.float32),
        lax.psum(partial_rows[7].astype(jnp.bfloat16), "seq").astype(jnp.float32),
        lax.psum(partial_rows[8].astype(jnp.bfloat16), "seq").astype(jnp.float32),
    )
    return (
        block_out,
        d_tokens,
        summed[0],
        summed[1],
        summed[2],
        summed[3],
        summed[4],
        summed[5],
        summed[6],
        summed[7],
        summed[8],
    )


def solution(mesh):
    in_specs = (
        P("rows", "seq", None),
        P("rows", "seq"),
        P("rows"),
        P("rows", None),
        P("rows", None),
        P(None, "rows"),
        P(None, "rows"),
        P("rows"),
        P("rows"),
        P(None, "rows"),
        P("rows", None),
        P("rows", "seq", None),
    )
    out_specs = (
        P("rows", "seq", None),
        P("rows", "seq", None),
        P("rows"),
        P("rows", None),
        P("rows", None),
        P(None, "rows"),
        P(None, "rows"),
        P("rows"),
        P("rows"),
        P(None, "rows"),
        P("rows", None),
    )
    return jax.shard_map(local, mesh=mesh, in_specs=in_specs, out_specs=out_specs, check_vma=False)
```

profile of v0, /device:TPU:0, one launch (start us, length us, event | category | flops | bytes accessed | tf_op | source)
XLA Modules:
  0.0 3366.4 jit_solution(9667583338308296708)
XLA Ops:
  10.4 15.2 all-reduce.5
  34.4 14.5 all_gather.52
  77.6 36.5 %all-gather.8.cloned.1.call-done = bf16[1536,6144]{1,0:T(8,128)(2,1)} async-done(((bf16[192,6144]{1,0:T(8,128)(2,1)}), bf16[1536,6144]{1,0:T(8,128)(2,1)}) %all-gather.8.cloned.1.call-update) | async-done | bytes 18874384 | tf_op jit(solution)/shard_map/all_gather | solution.py:209
  149.3 218.8 %while.96 = (s32[]{:T(128)}, f32[1,16,3072]{2,1,0:T(8,128)S(1)}, f32[16,1,16,3072]{3,2,1,0:T(8,128)}, f32[16,3072]{1,0:T(8,128)S(1)}, f32[16,1,16]{2,1,0:T(1,128...) while((s32[]{:T(128)}, f32[1,16,3072]{2,1,0:T(8,128)S(1)}, ...), condition=%wide.region_2.3_spmd.clone, body=%wide.region_1.2_spmd.clone.sunk | while | flops 4030467 | bytes 2745787 | solution.py:96
  368.1 15.3 all-gather
  383.4 15.1 all-gather.1
  403.7 360.2 %while.95 = (s32[]{:T(128)}, f32[1,16,3072]{2,1,0:T(8,128)S(1)}, f32[16,1,16,3072]{3,2,1,0:T(8,128)}, f32[16,1,16,3072]{3,2,1,0:T(8,128)}, f32[16,1,16,3072]{3,2...) while((s32[]{:T(128)}, f32[1,16,3072]{2,1,0:T(8,128)S(1)}, ...), condition=%wide.region_24.25_spmd, body=%wide.region_7.24_spmd.sunk | while | flops 7471106 | bytes 8416237 | solution.py:96
  408.1 11.0 multiply_reduce_fusion.80
  430.6 11.0 multiply_reduce_fusion.80
  453.1 11.0 multiply_reduce_fusion.80
  475.6 11.0 multiply_reduce_fusion.80
  498.1 11.0 multiply_reduce_fusion.80
  520.6 11.0 multiply_reduce_fusion.80
  543.1 11.0 multiply_reduce_fusion.80
  565.6 11.0 multiply_reduce_fusion.80
  588.1 11.0 multiply_reduce_fusion.80
  610.6 11.0 multiply_reduce_fusion.80
  655.6 11.0 multiply_reduce_fusion.80
  700.7 11.0 multiply_reduce_fusion.80
  723.3 11.0 multiply_reduce_fusion.80
  745.8 11.0 multiply_reduce_fusion.80
  764.0 13.0 fusion.307
  776.9 229.4 %while.98 = (s32[]{:T(128)}, f32[1,16,3072]{2,1,0:T(8,128)S(1)}, f32[16,1,16,16]{3,2,1,0:T(8,128)}, f32[16,1,16,3072]{3,2,1,0:T(8,128)}, f32[16,1,16,3072]{3,2,1...) while((s32[]{:T(128)}, f32[1,16,3072]{2,1,0:T(8,128)S(1)}, ...), condition=%wide.region_26.27_spmd.clone, body=%wide.region_25.26_spmd.clone.sunk | while | flops 3981316 | bytes 2561487 | solution.py:118
  1006.3 14.7 all-gather.2
  1026.9 1814.7 %while.100 = (s32[]{:T(128)}, f32[1,16,3072]{2,1,0:T(8,128)S(1)}, f32[1,16,3072]{2,1,0:T(8,128)}, f32[16,1,16,3072]{3,2,1,0:T(8,128)}, f32[16,1,16,3072]{3,2,1,0...) while((s32[]{:T(128)}, f32[1,16,3072]{2,1,0:T(8,128)S(1)}, ...), condition=%wide.region_94.95_spmd.clone, body=%wide.region_29.94_spmd.clone.sunk | while | flops 39271940 | bytes 29261224 | solution.py:180
  1036.6 12.3 multiply_reduce_fusion.87
  1080.0 12.7 fusion.401
  1150.0 12.3 multiply_reduce_fusion.87
  1193.4 12.8 fusion.401
  1263.4 12.3 multiply_reduce_fusion.87
  1306.8 12.8 fusion.401
  1376.9 12.3 multiply_reduce_fusion.87
  1420.3 12.8 fusion.401
  1490.3 12.3 multiply_reduce_fusion.87
  1533.6 12.8 fusion.401
  1603.6 12.3 multiply_reduce_fusion.87
  1647.0 12.8 fusion.401
  1717.0 12.3 multiply_reduce_fusion.87
  1760.4 12.8 fusion.401
  1830.4 12.3 multiply_reduce_fusion.87
  1873.8 12.8 fusion.401
  1943.8 12.3 multiply_reduce_fusion.87
  1987.2 12.8 fusion.401
  2057.3 12.3 multiply_reduce_fusion.87
  2100.7 12.8 fusion.401
  2170.6 12.3 multiply_reduce_fusion.87
  2214.0 12.8 fusion.401
  2284.1 12.3 multiply_reduce_fusion.87
  2327.5 12.8 fusion.401
  2397.4 12.3 multiply_reduce_fusion.87
  2440.8 12.8 fusion.401
  2510.8 12.3 multiply_reduce_fusion.87
  2554.2 12.8 fusion.401
  2624.2 12.3 multiply_reduce_fusion.87
  2667.6 12.8 fusion.401
  2737.6 12.3 multiply_reduce_fusion.87
  2781.0 12.8 fusion.401
  2891.8 29.5 reduce-scatter.15.cloned.1.call-done
  2921.3 79.9 %reduce-scatter.17.cloned.1.call-done = bf16[384,1536]{1,0:T(8,128)(2,1)} async-done(((bf16[3072,1536]{1,0:T(8,128)(2,1)}), bf16[384,1536]{1,0:T(8,128)(2,1)}) %reduce-scatter.17.cloned.1.call-update) | async-done | bytes 1179664 | tf_op jit(solution)/shard_map/reduce_scatter | solution.py:381
  3001.1 129.6 %reduce-scatter.13.cloned.1.call-done = bf16[192,6144]{1,0:T(8,128)(2,1)} async-done(((bf16[1536,6144]{1,0:T(8,128)(2,1)}), bf16[192,6144]{1,0:T(8,128)(2,1)}) %reduce-scatter.13.cloned.1.call-update) | async-done | bytes 2359312 | tf_op jit(solution)/shard_map/reduce_scatter | solution.py:360
  3149.0 22.9 all-reduce.9
  3176.0 31.6 reduce-scatter.23.cloned.1.call-done
  3208.6 19.5 all-reduce.10
  3231.1 120.8 %all-reduce.14.cloned.1.call-done = (bf16[192,6144]{1,0:T(8,128)(2,1)}, bf16[384,128]{1,0:T(8,128)(2,1)}, bf16[96,384]{1,0:T(8,128)(2,1)}, bf16[384,1536]{1,0:T(8,128)(2,1)}) async-done(((bf16[192,6144]{1,0:T(8,128)(2,1)}, bf16[384,128]{1,0:T(8,128)(2,1)}, bf16[96,384]{1,0:T(8,128)(2,1)}, bf16[384,1536]{1,0:T(8,128)(2,1)}), (bf16[192,6144]{1,0:T(8,128)(2,1)}, bf16[384,128]{1,0:T(8,128)(2,1)}, ...) | async-done | bytes 3710992 | tf_op jit(solution)/shard_map/psum | solution.py:387
  (5200 shorter events, 2205.1 us)
Async XLA Ops:
  7.2 51.8 %copy-start.163 = (bf16[4,384]{1,0:T(4,128)(2,1)S(1)}, bf16[4,384]{1,0:T(4,128)(2,1)}, u32[]{:S(2)}) copy-start(bf16[4,384]{1,0:T(4,128)(2,1)} %param.30) | copy-start | bytes 9220
  7.3 60.2 %copy-start.166 = (bf16[384]{0:T(512)(128)(2,1)S(1)}, bf16[384]{0:T(512)(128)(2,1)}, u32[]{:S(2)}) copy-start(bf16[384]{0:T(512)(128)(2,1)} %param.31) | copy-start | bytes 2308
  7.3 68.9 %copy-start.167 = (s32[1,256]{1,0:T(1,128)S(1)}, s32[1,256]{1,0:T(1,128)}, u32[]{:S(2)}) copy-start(s32[1,256]{1,0:T(1,128)} %param.25) | copy-start | bytes 3076
  7.3 106.8 %all-gather.8.cloned.1.call-start = ((), (), s32[]{:S(2)}) async-start(), calls=%async_computation.6 | async-start | bytes 21233664 | tf_op jit(solution)/shard_map/all_gather | solution.py:209
  8.0 756.0 %all-gather.10.cloned.1.call-start = ((), (), s32[]{:S(2)}) async-start(), calls=%async_computation.7 | async-start | bytes 10616832 | tf_op jit(solution)/shard_map/all_gather | solution.py:216
  8.8 2881.4 %reduce-scatter.19.cloned.1.call-start = ((), (), s32[]{:S(2)}) async-start(), calls=%async_computation.11 | async-start | bytes 884736
  25.6 97.6 %copy-start.113 = (f32[1536]{0:T(1024)}, f32[1536]{0:T(1024)S(1)}, u32[]{:S(2)}) copy-start(f32[1536]{0:T(1024)S(1)} %convert_element_type.252) | copy-start | bytes 18436
  26.5 96.7 %copy-start.157 = (f32[256]{0:T(256)}, f32[256]{0:T(256)S(1)}, u32[]{:S(2)}) copy-start(f32[256]{0:T(256)S(1)} %get-tuple-element.1601) | copy-start | bytes 3076
  48.9 94.0 %copy-start.67 = (bf16[96,3072]{1,0:T(8,128)(2,1)}, bf16[96,3072]{1,0:T(8,128)(2,1)S(1)}, u32[]{:S(2)}) copy-start(bf16[96,3072]{1,0:T(8,128)(2,1)S(1)} %all_gather.52) | copy-start | bytes 1769476
  59.0 81.0 %copy-start.23 = (bf16[3072,128]{1,0:T(8,128)(2,1)}, bf16[3072,128]{1,0:T(8,128)(2,1)S(1)}, u32[]{:S(2)}) copy-start(bf16[3072,128]{1,0:T(8,128)(2,1)S(1)} %all_gather.51) | copy-start | bytes 2359300
  67.5 69.2 %copy-start.149 = (f32[1,3072]{1,0:T(1,128)}, f32[1,3072]{1,0:T(1,128)S(1)}, u32[]{:S(2)}) copy-start(f32[1,3072]{1,0:T(1,128)S(1)} %get-tuple-element.1596) | copy-start | bytes 36868
  67.5 69.2 %copy-start.151 = (f32[1,3072]{1,0:T(1,128)}, f32[1,3072]{1,0:T(1,128)S(1)}, u32[]{:S(2)}) copy-start(f32[1,3072]{1,0:T(1,128)S(1)} %get-tuple-element.1597) | copy-start | bytes 36868
  67.5 69.2 %copy-start.153 = (f32[1,3072]{1,0:T(1,128)}, f32[1,3072]{1,0:T(1,128)S(1)}, u32[]{:S(2)}) copy-start(f32[1,3072]{1,0:T(1,128)S(1)} %get-tuple-element.1598) | copy-start | bytes 36868
  67.5 69.2 %copy-start.155 = (f32[1,3072]{1,0:T(1,128)}, f32[1,3072]{1,0:T(1,128)S(1)}, u32[]{:S(2)}) copy-start(f32[1,3072]{1,0:T(1,128)S(1)} %get-tuple-element.1599) | copy-start | bytes 36868
  123.5 13.2 collective-permute-start
  403.7 360.3 %copy-start.19 = (bf16[1,256,1536]{2,1,0:T(8,128)(2,1)S(1)}, bf16[1,256,1536]{2,1,0:T(8,128)(2,1)}, u32[]{:S(2)}) copy-start(bf16[1,256,1536]{2,1,0:T(8,128)(2,1)} %param.35) | copy-start | bytes 2359300
  1030.4 46.6 %copy-start.14 = (f32[1,1,3072]{2,1,0:T(1,128)}, f32[1,1,3072]{2,1,0:T(1,128)S(1)}, u32[]{:S(2)}) copy-start(f32[1,1,3072]{2,1,0:T(1,128)S(1)} %get-tuple-element.2688) | copy-start | bytes 36868 | tf_op jit(solution)/shard_map/while
  1031.2 45.9 %copy-start.103 = (f32[16]{0:T(128)}, f32[16]{0:T(128)S(1)}, u32[]{:S(2)}) copy-start(f32[16]{0:T(128)S(1)} %get-tuple-element.2595) | copy-start | bytes 196 | tf_op jit(solution)/shard_map/while
  1031.2 45.9 %copy-start.123 = (f32[16]{0:T(128)}, f32[16]{0:T(128)S(1)}, u32[]{:S(2)}) copy-start(f32[16]{0:T(128)S(1)} %get-tuple-element.2689) | copy-start | bytes 196 | tf_op jit(solution)/shard_map/while
  1143.7 46.6 %copy-start.14 = (f32[1,1,3072]{2,1,0:T(1,128)}, f32[1,1,3072]{2,1,0:T(1,128)S(1)}, u32[]{:S(2)}) copy-start(f32[1,1,3072]{2,1,0:T(1,128)S(1)} %get-tuple-element.2688) | copy-start | bytes 36868 | tf_op jit(solution)/shard_map/while
  1144.5 45.9 %copy-start.103 = (f32[16]{0:T(128)}, f32[16]{0:T(128)S(1)}, u32[]{:S(2)}) copy-start(f32[16]{0:T(128)S(1)} %get-tuple-element.2595) | copy-start | bytes 196 | tf_op jit(solution)/shard_map/while
  1144.5 45.8 %copy-start.123 = (f32[16]{0:T(128)}, f32[16]{0:T(128)S(1)}, u32[]{:S(2)}) copy-start(f32[16]{0:T(128)S(1)} %get-tuple-element.2689) | copy-start | bytes 196 | tf_op jit(solution)/shard_map/while
  1257.2 46.6 %copy-start.14 = (f32[1,1,3072]{2,1,0:T(1,128)}, f32[1,1,3072]{2,1,0:T(1,128)S(1)}, u32[]{:S(2)}) copy-start(f32[1,1,3072]{2,1,0:T(1,128)S(1)} %get-tuple-element.2688) | copy-start | bytes 36868 | tf_op jit(solution)/shard_map/while
  1258.0 45.8 %copy-start.103 = (f32[16]{0:T(128)}, f32[16]{0:T(128)S(1)}, u32[]{:S(2)}) copy-start(f32[16]{0:T(128)S(1)} %get-tuple-element.2595) | copy-start | bytes 196 | tf_op jit(solution)/shard_map/while
  1258.0 45.8 %copy-start.123 = (f32[16]{0:T(128)}, f32[16]{0:T(128)S(1)}, u32[]{:S(2)}) copy-start(f32[16]{0:T(128)S(1)} %get-tuple-element.2689) | copy-start | bytes 196 | tf_op jit(solution)/shard_map/while
  1370.6 46.6 %copy-start.14 = (f32[1,1,3072]{2,1,0:T(1,128)}, f32[1,1,3072]{2,1,0:T(1,128)S(1)}, u32[]{:S(2)}) copy-start(f32[1,1,3072]{2,1,0:T(1,128)S(1)} %get-tuple-element.2688) | copy-start | bytes 36868 | tf_op jit(solution)/shard_map/while
  1371.4 45.9 %copy-start.103 = (f32[16]{0:T(128)}, f32[16]{0:T(128)S(1)}, u32[]{:S(2)}) copy-start(f32[16]{0:T(128)S(1)} %get-tuple-element.2595) | copy-start | bytes 196 | tf_op jit(solution)/shard_map/while
  1371.4 45.8 %copy-start.123 = (f32[16]{0:T(128)}, f32[16]{0:T(128)S(1)}, u32[]{:S(2)}) copy-start(f32[16]{0:T(128)S(1)} %get-tuple-element.2689) | copy-start | bytes 196 | tf_op jit(solution)/shard_map/while
  1484.0 46.6 %copy-start.14 = (f32[1,1,3072]{2,1,0:T(1,128)}, f32[1,1,3072]{2,1,0:T(1,128)S(1)}, u32[]{:S(2)}) copy-start(f32[1,1,3072]{2,1,0:T(1,128)S(1)} %get-tuple-element.2688) | copy-start | bytes 36868 | tf_op jit(solution)/shard_map/while
  1484.8 45.8 %copy-start.103 = (f32[16]{0:T(128)}, f32[16]{0:T(128)S(1)}, u32[]{:S(2)}) copy-start(f32[16]{0:T(128)S(1)} %get-tuple-element.2595) | copy-start | bytes 196 | tf_op jit(solution)/shard_map/while
  1484.8 45.8 %copy-start.123 = (f32[16]{0:T(128)}, f32[16]{0:T(128)S(1)}, u32[]{:S(2)}) copy-start(f32[16]{0:T(128)S(1)} %get-tuple-element.2689) | copy-start | bytes 196 | tf_op jit(solution)/shard_map/while
  1597.4 46.6 %copy-start.14 = (f32[1,1,3072]{2,1,0:T(1,128)}, f32[1,1,3072]{2,1,0:T(1,128)S(1)}, u32[]{:S(2)}) copy-start(f32[1,1,3072]{2,1,0:T(1,128)S(1)} %get-tuple-element.2688) | copy-start | bytes 36868 | tf_op jit(solution)/shard_map/while
  1710.8 46.6 %copy-start.14 = (f32[1,1,3072]{2,1,0:T(1,128)}, f32[1,1,3072]{2,1,0:T(1,128)S(1)}, u32[]{:S(2)}) copy-start(f32[1,1,3072]{2,1,0:T(1,128)S(1)} %get-tuple-element.2688) | copy-start | bytes 36868 | tf_op jit(solution)/shard_map/while
  1711.6 45.8 %copy-start.103 = (f32[16]{0:T(128)}, f32[16]{0:T(128)S(1)}, u32[]{:S(2)}) copy-start(f32[16]{0:T(128)S(1)} %get-tuple-element.2595) | copy-start | bytes 196 | tf_op jit(solution)/shard_map/while
  1711.6 45.8 %copy-start.123 = (f32[16]{0:T(128)}, f32[16]{0:T(128)S(1)}, u32[]{:S(2)}) copy-start(f32[16]{0:T(128)S(1)} %get-tuple-element.2689) | copy-start | bytes 196 | tf_op jit(solution)/shard_map/while
  1824.2 46.6 %copy-start.14 = (f32[1,1,3072]{2,1,0:T(1,128)}, f32[1,1,3072]{2,1,0:T(1,128)S(1)}, u32[]{:S(2)}) copy-start(f32[1,1,3072]{2,1,0:T(1,128)S(1)} %get-tuple-element.2688) | copy-start | bytes 36868 | tf_op jit(solution)/shard_map/while
  1825.0 45.8 %copy-start.103 = (f32[16]{0:T(128)}, f32[16]{0:T(128)S(1)}, u32[]{:S(2)}) copy-start(f32[16]{0:T(128)S(1)} %get-tuple-element.2595) | copy-start | bytes 196 | tf_op jit(solution)/shard_map/while
  1825.0 45.8 %copy-start.123 = (f32[16]{0:T(128)}, f32[16]{0:T(128)S(1)}, u32[]{:S(2)}) copy-start(f32[16]{0:T(128)S(1)} %get-tuple-element.2689) | copy-start | bytes 196 | tf_op jit(solution)/shard_map/while
  1937.6 46.6 %copy-start.14 = (f32[1,1,3072]{2,1,0:T(1,128)}, f32[1,1,3072]{2,1,0:T(1,128)S(1)}, u32[]{:S(2)}) copy-start(f32[1,1,3072]{2,1,0:T(1,128)S(1)} %get-tuple-element.2688) | copy-start | bytes 36868 | tf_op jit(solution)/shard_map/while
  1938.4 45.8 %copy-start.103 = (f32[16]{0:T(128)}, f32[16]{0:T(128)S(1)}, u32[]{:S(2)}) copy-start(f32[16]{0:T(128)S(1)} %get-tuple-element.2595) | copy-start | bytes 196 | tf_op jit(solution)/shard_map/while
  1938.4 45.8 %copy-start.123 = (f32[16]{0:T(128)}, f32[16]{0:T(128)S(1)}, u32[]{:S(2)}) copy-start(f32[16]{0:T(128)S(1)} %get-tuple-element.2689) | copy-start | bytes 196 | tf_op jit(solution)/shard_map/while
  2051.0 46.6 %copy-start.14 = (f32[1,1,3072]{2,1,0:T(1,128)}, f32[1,1,3072]{2,1,0:T(1,128)S(1)}, u32[]{:S(2)}) copy-start(f32[1,1,3072]{2,1,0:T(1,128)S(1)} %get-tuple-element.2688) | copy-start | bytes 36868 | tf_op jit(solution)/shard_map/while
  2051.8 45.9 %copy-start.103 = (f32[16]{0:T(128)}, f32[16]{0:T(128)S(1)}, u32[]{:S(2)}) copy-start(f32[16]{0:T(128)S(1)} %get-tuple-element.2595) | copy-start | bytes 196 | tf_op jit(solution)/shard_map/while
  2051.8 45.9 %copy-start.123 = (f32[16]{0:T(128)}, f32[16]{0:T(128)S(1)}, u32[]{:S(2)}) copy-start(f32[16]{0:T(128)S(1)} %get-tuple-element.2689) | copy-start | bytes 196 | tf_op jit(solution)/shard_map/while
  2164.4 46.5 %copy-start.14 = (f32[1,1,3072]{2,1,0:T(1,128)}, f32[1,1,3072]{2,1,0:T(1,128)S(1)}, u32[]{:S(2)}) copy-start(f32[1,1,3072]{2,1,0:T(1,128)S(1)} %get-tuple-element.2688) | copy-start | bytes 36868 | tf_op jit(solution)/shard_map/while
  2277.8 46.6 %copy-start.14 = (f32[1,1,3072]{2,1,0:T(1,128)}, f32[1,1,3072]{2,1,0:T(1,128)S(1)}, u32[]{:S(2)}) copy-start(f32[1,1,3072]{2,1,0:T(1,128)S(1)} %get-tuple-element.2688) | copy-start | bytes 36868 | tf_op jit(solution)/shard_map/while
  2278.6 45.9 %copy-start.103 = (f32[16]{0:T(128)}, f32[16]{0:T(128)S(1)}, u32[]{:S(2)}) copy-start(f32[16]{0:T(128)S(1)} %get-tuple-element.2595) | copy-start | bytes 196 | tf_op jit(solution)/shard_map/while
  2278.6 45.8 %copy-start.123 = (f32[16]{0:T(128)}, f32[16]{0:T(128)S(1)}, u32[]{:S(2)}) copy-start(f32[16]{0:T(128)S(1)} %get-tuple-element.2689) | copy-start | bytes 196 | tf_op jit(solution)/shard_map/while
  2391.2 46.6 %copy-start.14 = (f32[1,1,3072]{2,1,0:T(1,128)}, f32[1,1,3072]{2,1,0:T(1,128)S(1)}, u32[]{:S(2)}) copy-start(f32[1,1,3072]{2,1,0:T(1,128)S(1)} %get-tuple-element.2688) | copy-start | bytes 36868 | tf_op jit(solution)/shard_map/while
  2392.0 45.8 %copy-start.103 = (f32[16]{0:T(128)}, f32[16]{0:T(128)S(1)}, u32[]{:S(2)}) copy-start(f32[16]{0:T(128)S(1)} %get-tuple-element.2595) | copy-start | bytes 196 | tf_op jit(solution)/shard_map/while
  2504.6 46.6 %copy-start.14 = (f32[1,1,3072]{2,1,0:T(1,128)}, f32[1,1,3072]{2,1,0:T(1,128)S(1)}, u32[]{:S(2)}) copy-start(f32[1,1,3072]{2,1,0:T(1,128)S(1)} %get-tuple-element.2688) | copy-start | bytes 36868 | tf_op jit(solution)/shard_map/while
  2505.4 45.8 %copy-start.103 = (f32[16]{0:T(128)}, f32[16]{0:T(128)S(1)}, u32[]{:S(2)}) copy-start(f32[16]{0:T(128)S(1)} %get-tuple-element.2595) | copy-start | bytes 196 | tf_op jit(solution)/shard_map/while
  2505.4 45.8 %copy-start.123 = (f32[16]{0:T(128)}, f32[16]{0:T(128)S(1)}, u32[]{:S(2)}) copy-start(f32[16]{0:T(128)S(1)} %get-tuple-element.2689) | copy-start | bytes 196 | tf_op jit(solution)/shard_map/while
  2618.0 46.6 %copy-start.14 = (f32[1,1,3072]{2,1,0:T(1,128)}, f32[1,1,3072]{2,1,0:T(1,128)S(1)}, u32[]{:S(2)}) copy-start(f32[1,1,3072]{2,1,0:T(1,128)S(1)} %get-tuple-element.2688) | copy-start | bytes 36868 | tf_op jit(solution)/shard_map/while
  2618.8 45.8 %copy-start.103 = (f32[16]{0:T(128)}, f32[16]{0:T(128)S(1)}, u32[]{:S(2)}) copy-start(f32[16]{0:T(128)S(1)} %get-tuple-element.2595) | copy-start | bytes 196 | tf_op jit(solution)/shard_map/while
  2618.8 45.8 %copy-start.123 = (f32[16]{0:T(128)}, f32[16]{0:T(128)S(1)}, u32[]{:S(2)}) copy-start(f32[16]{0:T(128)S(1)} %get-tuple-element.2689) | copy-start | bytes 196 | tf_op jit(solution)/shard_map/while
  2731.4 46.6 %copy-start.14 = (f32[1,1,3072]{2,1,0:T(1,128)}, f32[1,1,3072]{2,1,0:T(1,128)S(1)}, u32[]{:S(2)}) copy-start(f32[1,1,3072]{2,1,0:T(1,128)S(1)} %get-tuple-element.2688) | copy-start | bytes 36868 | tf_op jit(solution)/shard_map/while
  2849.5 71.8 %reduce-scatter.15.cloned.1.call-start = ((), (), s32[]{:S(2)}) async-start(), calls=%async_computation.9 | async-start | bytes 884736 | tf_op jit(solution)/shard_map/reduce_scatter | solution.py:363
  2853.0 148.2 %reduce-scatter.17.cloned.1.call-start = ((), (), s32[]{:S(2)}) async-start(), calls=%async_computation.10 | async-start | bytes 10616832 | tf_op jit(solution)/shard_map/reduce_scatter | solution.py:381
  2859.8 271.0 %reduce-scatter.13.cloned.1.call-start = ((), (), s32[]{:S(2)}) async-start(), calls=%async_computation.8 | async-start | bytes 21233664 | tf_op jit(solution)/shard_map/reduce_scatter | solution.py:360
  2870.2 5.9 collective-permute-start.1
  2885.8 289.3 %reduce-scatter.21.cloned.1.call-start = ((), (), s32[]{:S(2)}) async-start(), calls=%async_computation.12 | async-start | bytes 884736
  2887.2 320.5 %reduce-scatter.23.cloned.1.call-start = ((), (), s32[]{:S(2)}) async-start(), calls=%async_computation.13 | async-start | bytes 884736
  2888.5 463.4 %all-reduce.14.cloned.1.call-start = ((), (), s32[]{:S(2)}) async-start(), calls=%async_computation.14 | async-start | bytes 7421952 | tf_op jit(solution)/shard_map/psum | solution.py:387
  (1871 other events, 44250.0 us)
Sparse Core Ops, SparseCore 0:
  10.0 104.0 all-gather.7
  116.0 59.1 all-gather.9
  2849.6 33.0 reduce-scatter.18
  2886.3 34.9 reduce-scatter.14
  2924.6 76.4 reduce-scatter.16
  3004.6 126.1 reduce-scatter.12
  3134.5 35.0 reduce-scatter.20
  3172.7 34.9 reduce-scatter.22
  3210.9 140.9 all-reduce.13
where the time goes:
time: 3410 us; the launch traced here: 3370 us
  other arithmetic  2310 us (68%)
  waiting for transfers between devices  434 us (13%)
  local copies, waits for them, and re-layouts  336 us (10%)
  blocking collectives  162 us (5%)
  matrix products  72.6 us (2%)
    reduce_sum x112, other arithmetic, backward_retreat(): jnp.sum(weighted * decay_rate[None], axis=1)  606 us
    reduce_sum x96, other arithmetic, backward_retreat(): jnp.sum(grad_state * (step_delta[:, offset] * step_input[:, offset])[:, N...  470 us
    reduce_sum x80, other arithmetic, advance(): outputs.append(jnp.sum(carried * step_c[:, offset, :, None], axis=1))  272 us
    add x16, other arithmetic, backward_retreat(): rate_sum = rate_sum + weighted * step_delta[:, offset, None, :]  205 us
    squeeze x272, local copies, waits for them, and re-layouts, forward_states(): return lax.scan(advance, initial, pieces)  185 us
    mul x16, other arithmetic, reverse_retreat(): running * jnp.exp(step_delta[:, offset, None, :] * decay_rate[None])  175 us
    add x16, other arithmetic, advance(): decay_now * carried  173 us
    add x16, other arithmetic, backward_retreat(): decay_now * current  169 us

commit v1 on v0

v1 whole, which is shorter than its diff:
```python
import functools
import math

import jax
import jax.numpy as jnp
from jax import lax
from jax.experimental import pallas as pl
from jax.experimental.pallas import tpu as pltpu
from jax.sharding import PartitionSpec as P

D = 1536
E = 3072
R = 96
NS = 16
KC = 4
ITEM = 256

epsilon = 1e-05
LOG2E = 1.4426950408889634
LN2 = 0.6931471805599453
MIB = 2**20


LANES = 128


def pad_lanes(lanes):
    return -(-lanes // LANES) * LANES


def selector(wide):
    row = lax.broadcasted_iota(jnp.int32, (256, 2 * NS * wide), 0) % 128
    col = lax.broadcasted_iota(jnp.int32, (256, 2 * NS * wide), 1) // wide
    return (row == col + R).astype(jnp.bfloat16)


def spread(proj, sel_ref):
    high = proj.astype(jnp.bfloat16)
    low = (proj - high.astype(jnp.float32)).astype(jnp.bfloat16)
    return jnp.dot(
        jnp.concatenate([high, low], axis=1), sel_ref[...], preferred_element_type=jnp.float32
    )


def load_blocks(sources, targets, sems):
    copies = []
    for i, (source, target) in enumerate(zip(sources, targets)):
        for b in range(target.shape[0]):
            lanes = pl.ds(b * LANES, LANES)
            copies.append(pltpu.make_async_copy(source.at[:, lanes], target.at[b], sems.at[i, b]))
    for copy in copies:
        copy.start()
    return copies


def store_blocks(sources, targets, sems):
    copies = []
    for i, (source, target) in enumerate(zip(sources, targets)):
        for b in range(source.shape[0]):
            lanes = pl.ds(b * LANES, LANES)
            copies.append(pltpu.make_async_copy(source.at[b], target.at[:, lanes], sems.at[i, b]))
    for copy in copies:
        copy.start()
    return copies


def ends_kernel(
    nr, tt, ct, uu, delta_in, x_in, gy_in, proj_ref, a_ref, out_ref, sel, bc, delta_ref, x_ref, gy_ref, sems
):
    el = a_ref.shape[1]
    half = NS // 2
    copies = load_blocks((delta_in, x_in, gy_in), (delta_ref, x_ref, gy_ref), sems)
    sel[...] = selector(LANES)
    out_ref[0] = jnp.zeros((NS, nr, el), jnp.float32)
    out_ref[1] = jnp.ones((NS, nr, el), jnp.float32)
    out_ref[2] = jnp.zeros((NS, nr, el), jnp.float32)
    for copy in copies:
        copy.wait()

    def chunk(c, none):
        rows = pl.multiple_of(c * (ct * nr), ct * nr)
        bc[...] = spread(proj_ref[pl.ds(rows, ct * nr), :], sel)
        for b in range(el // LANES):
            lanes = slice(b * LANES, (b + 1) * LANES)
            for n0 in range(0, NS, half):
                ns = range(n0, n0 + half)
                rate = [jnp.broadcast_to(a_ref[n : n + 1, lanes], (nr, LANES)) for n in ns]

                def steps(s, carried):
                    state, through, back = (list(v) for v in carried)
                    for u in range(uu):
                        at = s * uu + u
                        here = pl.ds(c * ct + at, nr, stride=tt)
                        delta = delta_ref[b, here, :]
                        gy = gy_ref[b, here, :]
                        du = delta * x_ref[b, here, :]
                        near = pl.ds(pl.multiple_of(at * nr, nr), nr)
                        for i, n in enumerate(ns):
                            b_at, c_at = n * LANES, (NS + n) * LANES
                            decay = jnp.exp2(delta * rate[i])
                            state[i] = decay * state[i] + du * bc[near, b_at : b_at + LANES]
                            through[i] = through[i] * decay
                            back[i] = back[i] + through[i] * (gy * bc[near, c_at : c_at + LANES])
                    return tuple(state), tuple(through), tuple(back)

                start = tuple(tuple(out_ref[k, n, :, lanes] for n in ns) for k in range(3))
                last = lax.fori_loop(0, ct // uu, steps, start)
                for k in range(3):
                    for i, n in enumerate(ns):
                        out_ref[k, n, :, lanes] = last[k][i]
        return none

    lax.fori_loop(0, tt // ct, chunk, 0)


def scan_ends(delta, x, gy, proj, rate, nr, tt):
    el = rate.shape[1]
    ct = math.gcd(tt, 32)
    here = pl.BlockSpec(memory_space=pltpu.VMEM)
    away = pl.BlockSpec(memory_space=pl.ANY)
    blocks = pltpu.VMEM((el // LANES, nr * tt, LANES), jnp.float32)
    return pl.pallas_call(
        functools.partial(ends_kernel, nr, tt, ct, min(8, ct)),
        in_specs=[away] * 3 + [here] * 2,
        out_specs=here,
        out_shape=jax.ShapeDtypeStruct((3, NS, nr, el), jnp.float32),
        scratch_shapes=[
            pltpu.VMEM((256, 2 * NS * LANES), jnp.bfloat16),
            pltpu.VMEM((ct * nr, 2 * NS * LANES), jnp.float32),
            blocks,
            blocks,
            blocks,
            pltpu.SemaphoreType.DMA((3, el // LANES)),
        ],
        compiler_params=pltpu.CompilerParams(vmem_limit_bytes=56 * MIB),
        name="scan_ends",
    )(delta, x, gy, proj, rate)


def main_kernel(
    nr, tt, ct, uu,
    delta_in, x_in, gy_in, proj_ref, a_ref, carry_ref,
    y_out, gdelta_out, gx_out, gbc_ref, grate_ref,
    sel, bc, hist, prod, state_ref, fold, delta_ref, x_ref, gy_ref, y_ref, gdelta_ref, gx_ref, sems, out_sems,
):
    el = a_ref.shape[1]
    blocks = el // LANES
    copies = load_blocks((delta_in, x_in, gy_in), (delta_ref, x_ref, gy_ref), sems)
    sel[...] = selector(LANES)
    fold_row = lax.broadcasted_iota(jnp.int32, fold.shape, 0) // LANES
    fold_col = lax.broadcasted_iota(jnp.int32, fold.shape, 1)
    fold[...] = (fold_row + R == fold_col).astype(jnp.bfloat16)
    state_ref[...] = carry_ref[0]

    def enter(p):
        return pl.ds(2 * p * nr, 2 * nr)

    def keep(b, t, state):
        for p in range(NS // 2):
            both = jnp.concatenate([state[2 * p], state[2 * p + 1]], axis=0)
            hist[b, t, enter(p), :] = both.astype(jnp.bfloat16)

    for b in range(blocks):
        keep(b, 0, [carry_ref[0, n, :, b * LANES : (b + 1) * LANES] for n in range(NS)])
    for copy in copies:
        copy.wait()

    def forward(c, none):
        rows = pl.multiple_of(c * (ct * nr), ct * nr)
        bc[...] = spread(proj_ref[pl.ds(rows, ct * nr), :], sel)
        for b in range(blocks):
            lanes = slice(b * LANES, (b + 1) * LANES)
            rate = [jnp.broadcast_to(a_ref[n : n + 1, lanes], (nr, LANES)) for n in range(NS)]

            def steps(s, carried):
                state = list(carried)
                for u in range(uu):
                    at = s * uu + u
                    t = c * ct + at
                    here = pl.ds(t, nr, stride=tt)
                    delta = delta_ref[b, here, :]
                    du = delta * x_ref[b, here, :]
                    near = pl.ds(pl.multiple_of(at * nr, nr), nr)
                    y = None
                    for n in range(NS):
                        b_at, c_at = n * LANES, (NS + n) * LANES
                        decay = jnp.exp2(delta * rate[n])
                        state[n] = decay * state[n] + du * bc[near, b_at : b_at + LANES]
                        term = state[n] * bc[near, c_at : c_at + LANES]
                        y = term if y is None else y + term
                    keep(b, t + 1, state)
                    y_ref[b, here, :] = y
                return tuple(state)

            start = tuple(state_ref[n, :, lanes] for n in range(NS))
            last = lax.fori_loop(0, ct // uu, steps, start)
            for n in range(NS):
                state_ref[n, :, lanes] = last[n]
        return none

    lax.fori_loop(0, tt // ct, forward, 0)
    y_copies = store_blocks((y_ref,), (y_out,), out_sems.at[pl.ds(0, 1)])

    state_ref[...] = carry_ref[1]
    grate_ref[...] = jnp.zeros_like(grate_ref)

    def backward(k, none):
        c = tt // ct - 1 - k
        rows = pl.multiple_of(c * (ct * nr), ct * nr)
        bc[...] = spread(proj_ref[pl.ds(rows, ct * nr), :], sel)
        for b in range(blocks):
            lanes = slice(b * LANES, (b + 1) * LANES)
            for first in (True, False):
                ns = range(0, NS // 2) if first else range(NS // 2, NS)
                pairs = range(ns[0] // 2, ns[-1] // 2 + 1)
                rate = [jnp.broadcast_to(a_ref[n : n + 1, lanes], (nr, LANES)) for n in ns]

                def steps(s, carried):
                    grad, total, after = (list(v) for v in carried)
                    for u in reversed(range(uu)):
                        at = (ct // uu - 1 - s) * uu + u
                        t = c * ct + at
                        here = pl.ds(t, nr, stride=tt)
                        delta = delta_ref[b, here, :]
                        x = x_ref[b, here, :]
                        gy = gy_ref[b, here, :]
                        du = delta * x
                        near = pl.ds(pl.multiple_of(at * nr, nr), nr)
                        along_rate = along_b = None
                        for p in pairs:
                            pair = hist[b, t, enter(p), :].astype(jnp.float32)
                            for n, before in ((2 * p, pair[:nr]), (2 * p + 1, pair[nr:])):
                                i = n - ns[0]
                                to_b_at = slice(n * LANES, (n + 1) * LANES)
                                to_c_at = slice((NS + n) * LANES, (NS + n + 1) * LANES)
                                decay = jnp.exp2(delta * rate[i])
                                grad[i] = grad[i] + gy * bc[near, to_c_at]
                                to_c = after[i] * gy
                                to_b = grad[i] * du
                                if b > 0:
                                    to_c = to_c + prod[near, to_c_at]
                                    to_b = to_b + prod[near, to_b_at]
                                prod[near, to_c_at] = to_c
                                prod[near, to_b_at] = to_b
                                term_b = grad[i] * bc[near, to_b_at]
                                along_b = term_b if along_b is None else along_b + term_b
                                grad[i] = grad[i] * decay
                                weighted = grad[i] * before
                                total[i] = total[i] + weighted * delta
                                term = weighted * rate[i]
                                along_rate = term if along_rate is None else along_rate + term
                                after[i] = before
                        gdelta = along_rate * LN2 + along_b * x
                        gx = along_b * delta
                        if not first:
                            gdelta = gdelta + gdelta_ref[b, here, :]
                            gx = gx + gx_ref[b, here, :]
                        gdelta_ref[b, here, :] = gdelta
                        gx_ref[b, here, :] = gx
                    return tuple(grad), tuple(total), tuple(after)

                after = []
                for p in pairs:
                    pair = hist[b, (c + 1) * ct, enter(p), :].astype(jnp.float32)
                    after += [pair[:nr], pair[nr:]]
                start = (
                    tuple(state_ref[n, :, lanes] for n in ns),
                    tuple(grate_ref[n, :, lanes] for n in ns),
                    tuple(after),
                )
                grad, total, unused = lax.fori_loop(0, ct // uu, steps, start)
                for i, n in enumerate(ns):
                    state_ref[n, :, lanes] = grad[i]
                    grate_ref[n, :, lanes] = total[i]
        gbc_ref[pl.ds(rows, ct * nr), :] = jnp.dot(
            prod[...].astype(jnp.bfloat16), fold[...], preferred_element_type=jnp.float32
        )
        return none

    lax.fori_loop(0, tt // ct, backward, 0)
    late = store_blocks((gdelta_ref, gx_ref), (gdelta_out, gx_out), out_sems.at[pl.ds(1, 2)])
    for copy in y_copies + late:
        copy.wait()


def scan_main(delta, x, gy, proj, rate, carry, nr, tt):
    el = rate.shape[1]
    ct = math.gcd(tt, 32)
    here = pl.BlockSpec(memory_space=pltpu.VMEM)
    away = pl.BlockSpec(memory_space=pl.ANY)
    full = jax.ShapeDtypeStruct((nr * tt, el), jnp.float32)
    blocks = pltpu.VMEM((el // LANES, nr * tt, LANES), jnp.float32)
    return pl.pallas_call(
        functools.partial(main_kernel, nr, tt, ct, min(8, ct)),
        in_specs=[away] * 3 + [here] * 3,
        out_specs=[away] * 3 + [here] * 2,
        out_shape=[
            full,
            full,
            full,
            jax.ShapeDtypeStruct((tt * nr, LANES), jnp.float32),
            jax.ShapeDtypeStruct((NS, nr, el), jnp.float32),
        ],
        scratch_shapes=[
            pltpu.VMEM((256, 2 * NS * LANES), jnp.bfloat16),
            pltpu.VMEM((ct * nr, 2 * NS * LANES), jnp.float32),
            pltpu.VMEM((el // LANES, tt + 1, NS * nr, LANES), jnp.bfloat16),
            pltpu.VMEM((ct * nr, 2 * NS * LANES), jnp.float32),
            pltpu.VMEM((NS, nr, el), jnp.float32),
            pltpu.VMEM((2 * NS * LANES, LANES), jnp.bfloat16),
        ]
        + [blocks] * 6
        + [
            pltpu.SemaphoreType.DMA((3, el // LANES)),
            pltpu.SemaphoreType.DMA((3, el // LANES)),
        ],
        compiler_params=pltpu.CompilerParams(vmem_limit_bytes=63 * MIB),
        name="scan_main",
    )(delta, x, gy, proj, rate, carry)


MESH = pl.DeviceIdType.MESH


def greet(devices):
    barrier = pltpu.get_barrier_semaphore()
    for device in devices:
        pl.semaphore_signal(barrier, inc=1, device_id=device, device_id_type=MESH)
    pl.semaphore_wait(barrier, len(devices))


def remote(source, target, send, recv, device):
    copy = pltpu.make_async_remote_copy(
        src_ref=source, dst_ref=target, send_sem=send, recv_sem=recv, device_id=device, device_id_type=MESH
    )
    copy.start()
    return copy


def row_peers(size):
    me = lax.axis_index("rows")
    half = size // 2
    mine = me // 2
    return me, me % 2, me + 1 - 2 * (me % 2), [lax.rem(mine + k, half) for k in range(half)]


def sum_rows(size, part_of, part, near, total, mail, far, out, sems, use):
    me, parity, partner, others = row_peers(size)
    place = lax.axis_index("seq")
    half = size // 2
    greet([(place, partner)] + [(place, 2 * j + parity) for j in others[1:]])
    first = []
    for j in range(half):
        block = 2 * j + 1 - parity
        part[block] = part_of(block).astype(jnp.bfloat16)
        first.append(
            remote(part.at[block], near.at[j], sems.at[0, j], sems.at[1, j], (place, partner))
        )
    for j in range(half):
        total[j] = part_of(2 * j + parity)
    for copy in first:
        copy.wait()
    second = []
    for k in list(range(1, half)) + [0]:
        j = others[k]
        total[j] = total[j] + near[j].astype(jnp.float32)
        if k:
            mail[j] = total[j].astype(jnp.bfloat16)
            target = (place, 2 * j + parity)
            second.append(remote(mail.at[j], far.at[k], sems.at[2, k], sems.at[3, k], target))
    mine = others[0]
    done = total[mine]
    for k in range(1, half):
        second[k - 1].wait()
        done = done + far[k].astype(jnp.float32)
    out[me] = done.astype(jnp.bfloat16)
    third = []
    for k in range(1, half):
        target = (place, 2 * others[k] + parity)
        third.append(remote(out.at[me], out.at[me], sems.at[4, k], sems.at[5, k], target))
    fourth = [remote(out.at[me], out.at[me], sems.at[6, 0], sems.at[7, 0], (place, partner))]
    use(me)
    for k in range(1, half):
        block = 2 * others[half - k] + parity
        here = pltpu.make_async_remote_copy(
            src_ref=out.at[me], dst_ref=out.at[block], send_sem=sems.at[4, k], recv_sem=sems.at[5, k],
            device_id=(place, partner), device_id_type=MESH,
        )
        here.wait_recv()
        fourth.append(
            remote(out.at[block], out.at[block], sems.at[6, k], sems.at[7, k], (place, partner))
        )
        use(block)
    for k in range(half):
        block = 2 * others[(half - k) % half] + 1 - parity
        here = pltpu.make_async_remote_copy(
            src_ref=out.at[me], dst_ref=out.at[block], send_sem=sems.at[6, k], recv_sem=sems.at[7, k],
            device_id=(place, partner), device_id_type=MESH,
        )
        here.wait_recv()
        use(block)
    for copy in third + fourth:
        copy.wait_send()


def sum_scratch(size, tt):
    half = size // 2
    return [
        pltpu.VMEM((size, tt, LANES), jnp.bfloat16),
        pltpu.VMEM((half, tt, LANES), jnp.bfloat16),
        pltpu.VMEM((half, tt, LANES), jnp.float32),
        pltpu.VMEM((half, tt, LANES), jnp.bfloat16),
        pltpu.VMEM((half, tt, LANES), jnp.bfloat16),
        pltpu.VMEM((size, tt, LANES), jnp.bfloat16),
        pltpu.SemaphoreType.DMA((8, half)),
    ]


def project_kernel(
    size, conv_ref, x_proj_ref, dt_ref, bias_ref, proj_ref, delta_ref, rank_ref,
    part, near, total, mail, far, out, sems,
):
    tt = conv_ref.shape[1]

    def part_of(p):
        return jnp.dot(conv_ref[p], x_proj_ref[...], preferred_element_type=jnp.float32)

    def use(p):
        block = out[p]
        rank_ref[p] = block
        proj_ref[pl.ds(p, tt, stride=size), :] = block.astype(jnp.float32)
        step = jnp.dot(block, dt_ref[...], preferred_element_type=jnp.float32) + bias_ref[...]
        delta_ref[p] = jnp.maximum(step, 0.0) + jnp.log1p(jnp.exp(-jnp.abs(step)))

    sum_rows(size, part_of, part, near, total, mail, far, out, sems, use)


def project(conv_out, x_proj, dt_pad, bias):
    size, tt, el = conv_out.shape
    here = pl.BlockSpec(memory_space=pltpu.VMEM)
    return pl.pallas_call(
        functools.partial(project_kernel, size),
        in_specs=[here] * 4,
        out_specs=[here] * 3,
        out_shape=[
            jax.ShapeDtypeStruct((tt * size, LANES), jnp.float32),
            jax.ShapeDtypeStruct((size, tt, el), jnp.float32),
            jax.ShapeDtypeStruct((size, tt, LANES), jnp.bfloat16),
        ],
        scratch_shapes=sum_scratch(size, tt),
        compiler_params=pltpu.CompilerParams(
            vmem_limit_bytes=40 * MIB, collective_id=0, has_side_effects=True
        ),
        name="project",
    )(conv_out, x_proj, dt_pad, bias)


def back_project_kernel(
    size, low_ref, dt_ref, gbc_ref, out_ref, part, near, total, mail, far, out, sems
):
    tt = low_ref.shape[1]

    def part_of(p):
        ranks = lax.dot_general(
            low_ref[p], dt_ref[...], (((1,), (1,)), ((), ())), preferred_element_type=jnp.float32
        )
        return ranks + gbc_ref[pl.ds(p, tt, stride=size), :]

    def use(p):
        out_ref[p] = out[p]

    sum_rows(size, part_of, part, near, total, mail, far, out, sems, use)


def back_project(low_step, dt_pad, gbc):
    size, tt, unused_el = low_step.shape
    here = pl.BlockSpec(memory_space=pltpu.VMEM)
    return pl.pallas_call(
        functools.partial(back_project_kernel, size),
        in_specs=[here] * 3,
        out_specs=here,
        out_shape=jax.ShapeDtypeStruct((size, tt, LANES), jnp.bfloat16),
        scratch_shapes=sum_scratch(size, tt),
        compiler_params=pltpu.CompilerParams(
            vmem_limit_bytes=40 * MIB, collective_id=1, has_side_effects=True
        ),
        name="back_project",
    )(low_step, dt_pad, gbc)


def carry_kernel(seq, ends_ref, alive_ref, out_ref, mail, land, sems):
    place = lax.axis_index("seq")
    me = lax.axis_index("rows")
    barrier = pltpu.get_barrier_semaphore()
    alive = alive_ref[...][None]

    for step, there in ((-1, place > 0), (1, place < seq - 1)):

        @pl.when(there)
        def _(step=step):
            pl.semaphore_signal(barrier, inc=1, device_id=(place + step, me), device_id_type=MESH)

    pl.semaphore_wait(barrier, (place > 0).astype(jnp.int32) + (place < seq - 1).astype(jnp.int32))

    def hop(way):
        first, last, step = ((0, seq - 1, 1), (seq - 1, 0, -1))[way]
        target = (jnp.clip(place + step, 0, seq - 1), me)
        copy = pltpu.make_async_remote_copy(
            src_ref=mail.at[way], dst_ref=land.at[way], send_sem=sems.at[way, 0], recv_sem=sems.at[way, 1],
            device_id=target, device_id_type=MESH,
        )

        @pl.when(place == first)
        def _():
            out_ref[way] = jnp.zeros_like(out_ref[way])

        @pl.when(place != first)
        def _():
            copy.wait_recv()
            entering = land[way].astype(jnp.float32)
            out_ref[way] = entering * alive if way == 0 else entering

        @pl.when(place != last)
        def _():
            if way == 0:
                leaving = ends_ref[0] + ends_ref[1] * out_ref[0]
            else:
                leaving = (ends_ref[2] + ends_ref[1] * out_ref[1]) * alive
            mail[way] = leaving.astype(jnp.bfloat16)
            copy.start()

    def finish(way):
        last, step = ((seq - 1, 1), (0, -1))[way]
        target = (jnp.clip(place + step, 0, seq - 1), me)

        @pl.when(place != last)
        def _():
            pltpu.make_async_remote_copy(
                src_ref=mail.at[way], dst_ref=land.at[way], send_sem=sems.at[way, 0],
                recv_sem=sems.at[way, 1], device_id=target, device_id_type=MESH,
            ).wait_send()

    @pl.when(place < seq // 2)
    def _():
        hop(0)
        hop(1)

    @pl.when(place >= seq // 2)
    def _():
        hop(1)
        hop(0)

    finish(0)
    finish(1)


def exchange_carry(ends, alive, seq):
    here = pl.BlockSpec(memory_space=pltpu.VMEM)
    shape = ends.shape[1:]
    return pl.pallas_call(
        functools.partial(carry_kernel, seq),
        in_specs=[here] * 2,
        out_specs=here,
        out_shape=jax.ShapeDtypeStruct((2,) + shape, jnp.float32),
        scratch_shapes=[
            pltpu.VMEM((2,) + shape, jnp.bfloat16),
            pltpu.VMEM((2,) + shape, jnp.bfloat16),
            pltpu.SemaphoreType.DMA((2, 2)),
        ],
        compiler_params=pltpu.CompilerParams(
            vmem_limit_bytes=40 * MIB, collective_id=2, has_side_effects=True
        ),
        name="exchange_carry",
    )(ends, alive)


def flip(place, mask):
    for k in range(mask.bit_length()):
        bit = 1 << k
        if mask & bit:
            place = place + bit * (1 - 2 * (lax.div(place, bit) % 2))
    return place


def bit_orders(size):
    rest = [1 << k for k in range(1, size.bit_length() - 1)]
    cut = max(1, len(rest) // 2)
    return [1] + rest, [1] + rest[cut:] + rest[:cut]


def masks_of(bits):
    masks = [0]
    for bit in bits:
        masks = masks + [m | bit for m in masks]
    return masks


def gather_kernel(size, count, *refs):
    sources, outs, (local_sem, send, recv) = refs[:count], refs[count : 2 * count], refs[2 * count :]
    me, place = lax.axis_index("rows"), lax.axis_index("seq")
    greet([(place, flip(me, 1 << k)) for k in range(size.bit_length() - 1)])
    started = []
    kept = []
    for i in range(count):
        copy = pltpu.make_async_copy(sources[i], outs[i].at[me], local_sem.at[i])
        copy.start()
        kept.append(copy)

    def cut(i, h, ref):
        width = outs[i].shape[-1] // 2
        return ref.at[:, pl.ds(h * width, width)]

    def slot(i, h, m):
        return (i, h, m)

    def push(i, h, m, bit):
        source = sources[i] if m == 0 else outs[i].at[flip(me, m)]
        key = slot(i, h, m | bit)
        started.append(
            remote(
                cut(i, h, source), cut(i, h, outs[i].at[flip(me, m)]), send.at[key], recv.at[key],
                (place, flip(me, bit)),
            )
        )

    def arrived(i, h, m):
        key = slot(i, h, m)
        block = cut(i, h, outs[i].at[flip(me, m)])
        pltpu.make_async_remote_copy(
            src_ref=block, dst_ref=block, send_sem=send.at[key], recv_sem=recv.at[key],
            device_id=(place, flip(me, 1)), device_id_type=MESH,
        ).wait_recv()

    orders = [order[1:] + order[:1] for order in bit_orders(size)]
    steps = len(orders[0])
    for i in range(count):
        for h in range(2):
            push(i, h, 0, orders[h][0])
    for i in range(count):
        for h in range(2):
            push(i, h, 0, 1)
    for i in range(count):
        for k in range(1, steps):
            for h in range(2):
                order = orders[h]
                old = masks_of(order[: k - 1])
                if k < steps - 1:
                    for m in old:
                        push(i, h, m, order[k])
                for m in old:
                    fresh = m | order[k - 1]
                    arrived(i, h, fresh)
                    if k < steps - 1:
                        push(i, h, fresh, order[k])
                    push(i, h, fresh, 1)
    for i in range(count):
        for h in range(2):
            for m in masks_of(orders[h][:-1]):
                arrived(i, h, m | 1)
    for copy in started:
        copy.wait_send()
    for copy in kept:
        copy.wait()


def gather_rows(arrays, size):
    count = len(arrays)
    away = pl.BlockSpec(memory_space=pl.ANY)
    return pl.pallas_call(
        functools.partial(gather_kernel, size, count),
        in_specs=[away] * count,
        out_specs=[away] * count,
        out_shape=[jax.ShapeDtypeStruct((size,) + v.shape, v.dtype) for v in arrays],
        scratch_shapes=[
            pltpu.SemaphoreType.DMA((count,)),
            pltpu.SemaphoreType.DMA((count, 2, size)),
            pltpu.SemaphoreType.DMA((count, 2, size)),
        ],
        compiler_params=pltpu.CompilerParams(collective_id=3, has_side_effects=True),
        name="gather_rows",
    )(*arrays)


def by_tiles(rows, tile, body):
    def step(i, none):
        body(pl.ds(pl.multiple_of(i * tile, tile), tile))
        return none

    lax.fori_loop(0, rows // tile, step, 0)


def wait_for(ref, sem):
    pltpu.make_async_copy(ref, ref, sem).wait()


def greet_rows_and_seq(size, seq):
    me, place = lax.axis_index("rows"), lax.axis_index("seq")
    barrier = pltpu.get_barrier_semaphore()
    for mask in range(1, size):
        pl.semaphore_signal(barrier, inc=1, device_id=(place, flip(me, mask)), device_id_type=MESH)
    for step, there in ((-1, place > 0), (1, place < seq - 1)):

        @pl.when(there)
        def _(step=step):
            pl.semaphore_signal(barrier, inc=1, device_id=(place + step, me), device_id_type=MESH)

    near = (place > 0).astype(jnp.int32) + (place < seq - 1).astype(jnp.int32)
    pl.semaphore_wait(barrier, near + size - 1)


class RowScatter:
    def __init__(self, size, part, keep, land, mail, keep_sem, send, recv):
        self.size, self.part, self.keep, self.land, self.mail = size, part, keep, land, mail
        self.keep_sem, self.send, self.recv = keep_sem, send, recv
        self.me, self.place = lax.axis_index("rows"), lax.axis_index("seq")
        self.tt, self.width = part.shape[1], part.shape[2] // 2
        self.orders = bit_orders(size)
        self.steps = len(self.orders[0])
        self.started, self.local = [], []

    @staticmethod
    def scratch(size, tt, width):
        return [
            pltpu.VMEM((size // 2, tt, width), jnp.bfloat16),
            pltpu.VMEM((size - 1, tt, width), jnp.bfloat16),
            pltpu.VMEM((size // 2 - 1, tt, width), jnp.bfloat16),
            pltpu.SemaphoreType.DMA((size // 2,)),
            pltpu.SemaphoreType.DMA((2, size - 1)),
            pltpu.SemaphoreType.DMA((2, size - 1)),
        ]

    def free(self, h, k):
        return masks_of(self.orders[h][k + 1 :])

    def at(self, h, k, m):
        return sum(len(self.free(h, j)) for j in range(k)) + self.free(h, k).index(m)

    def cols(self, h):
        return pl.ds(h * self.width, self.width)

    def receive(self, h, k, m):
        slot = self.at(h, k, m)
        wait_for(self.land.at[slot, :, self.cols(h)], self.recv.at[h, slot])

    def partial_sum(self, h, k, m, rows):
        value = self.keep[m >> 1, rows, self.cols(h)].astype(jnp.float32)
        for j in range(k):
            value = value + self.land[self.at(h, j, m), rows, self.cols(h)].astype(jnp.float32)
        return value

    def start(self):
        for h in range(2):
            self.scatter(h, 0)
        for m in self.free(0, 0):
            copy = pltpu.make_async_copy(
                self.part.at[flip(self.me, m)], self.keep.at[m >> 1], self.keep_sem.at[m >> 1]
            )
            copy.start()
            self.local.append(copy)

    def step(self, k):
        if k == 1:
            for copy in self.local:
                copy.wait()
        for h in range(2):
            self.scatter(h, k)

    def scatter(self, h, k):
        bit = self.orders[h][k]
        for m in self.free(h, k):
            slot = self.at(h, k, m)
            if k == 0:
                source = self.part.at[flip(self.me, m | bit), :, self.cols(h)]
            else:
                for j in range(k):
                    self.receive(h, j, m | bit)
                box = slot - self.size // 2

                def fill(rows, m=m, box=box):
                    value = self.partial_sum(h, k, m | bit, rows)
                    self.mail[box, rows, self.cols(h)] = value.astype(jnp.bfloat16)

                by_tiles(self.tt, 32, fill)
                source = self.mail.at[box, :, self.cols(h)]
            self.started.append(
                remote(
                    source, self.land.at[slot, :, self.cols(h)], self.send.at[h, slot], self.recv.at[h, slot],
                    (self.place, flip(self.me, bit)),
                )
            )

    def finish(self, own):
        for h in range(2):
            for j in range(self.steps):
                self.receive(h, j, 0)

            def fill(rows, h=h):
                own[rows, self.cols(h)] = self.partial_sum(h, self.steps, 0, rows).astype(jnp.bfloat16)

            by_tiles(self.tt, 32, fill)

    def drain(self):
        for copy in self.started:
            copy.wait_send()


class SeqSum:
    def __init__(self, seq, held, land, mail, fill_sem, send, recv):
        self.seq, self.held, self.land, self.mail = seq, held, land, mail
        self.fill_sem, self.send, self.recv = fill_sem, send, recv
        self.me, self.place = lax.axis_index("rows"), lax.axis_index("seq")
        self.behind = (self.place, seq - 1 - self.place)
        self.chunks = held.shape[0]
        self.last_step = self.chunks + seq - 1

    @staticmethod
    def scratch(chunks, block):
        return [
            pltpu.VMEM((chunks,) + block, jnp.bfloat16),
            pltpu.VMEM((2, chunks) + block, jnp.bfloat16),
            pltpu.VMEM((2, chunks) + block, jnp.bfloat16),
            pltpu.SemaphoreType.DMA((chunks,)),
            pltpu.SemaphoreType.DMA((2, chunks)),
            pltpu.SemaphoreType.DMA((2, chunks)),
        ]

    def copy(self, n, way, source):
        target = (jnp.clip(self.place + 1 - 2 * way, 0, self.seq - 1), self.me)
        return pltpu.make_async_remote_copy(
            src_ref=source, dst_ref=self.land.at[way, n], send_sem=self.send.at[way, n],
            recv_sem=self.recv.at[way, n], device_id=target, device_id_type=MESH,
        )

    def hop(self, step, way):
        n = step - self.behind[way]

        @pl.when((n >= 0) & (n < self.chunks))
        def _():
            @pl.when(self.behind[way] == 0)
            def _():
                self.copy(n, way, self.held.at[n]).start()

            @pl.when(self.behind[way] > 0)
            def _():
                self.copy(n, way, self.held.at[n]).wait_recv()

                @pl.when(self.behind[way] < self.seq - 1)
                def _():
                    value = self.held[n].astype(jnp.float32) + self.land[way, n].astype(jnp.float32)
                    self.mail[way, n] = value.astype(jnp.bfloat16)
                    self.copy(n, way, self.mail.at[way, n]).start()

    def advance(self, step, total):
        first = step - jnp.minimum(self.behind[0], self.behind[1])

        @pl.when((first >= 0) & (first < self.chunks))
        def _():
            wait_for(self.held.at[first], self.fill_sem.at[first])

        self.hop(step, 0)
        self.hop(step, 1)
        n = step - jnp.maximum(self.behind[0], self.behind[1])

        @pl.when((n >= 0) & (n < self.chunks))
        def _():
            for ways, there in (
                ((1,), self.behind[0] == 0),
                ((0,), self.behind[1] == 0),
                ((0, 1), (self.behind[0] > 0) & (self.behind[1] > 0)),
            ):

                @pl.when(there)
                def _(ways=ways):
                    value = self.held[n].astype(jnp.float32)
                    for way in ways:
                        value = value + self.land[way, n].astype(jnp.float32)
                    total[n] = value.astype(jnp.bfloat16)

    def run(self, first, last, total):
        def body(step, none):
            self.advance(step, total)
            return none

        lax.fori_loop(first, last, body, 0)

    def drain(self):
        for way in range(2):

            @pl.when(self.behind[way] < self.seq - 1)
            def _(way=way):
                def sent(n, none):
                    self.copy(n, way, self.held.at[n]).wait_send()
                    return none

                lax.fori_loop(0, self.chunks, sent, 0)


def chunk_order(size):
    return sorted(range(size), key=lambda m: (m > 1, (m >> 1).bit_count(), m))


def tail_kernel(size, seq, *refs):
    branch, normed, weight, out_w, small = refs[:5]
    branch_own, normed_own, total = refs[5:8]
    scatter_a = RowScatter(size, branch, *refs[8:14])
    scatter_b = RowScatter(size, normed, *refs[14:20])
    held, land, mail, fill_sem, zsend, zrecv, swap_send = refs[20:]
    chain = SeqSum(seq, held, land, mail, fill_sem, zsend, zrecv)
    me, place = lax.axis_index("rows"), lax.axis_index("seq")
    rows, cols = held.shape[1:]
    greet_rows_and_seq(size, seq)
    scatter_a.start()
    n = 0
    for source in (out_w, small):
        for i in range(source.shape[0] // rows):
            for j in range(source.shape[1] // cols):
                piece = source.at[pl.ds(i * rows, rows), pl.ds(j * cols, cols)]
                pltpu.make_async_copy(piece, held.at[n], fill_sem.at[n]).start()
                n += 1
    sent = []
    for m in chunk_order(size):
        for i in range(weight.shape[1] // rows):
            piece = weight.at[flip(me, m), pl.ds(i * rows, rows), :]
            if m == 0:
                pltpu.make_async_copy(piece, held.at[n], fill_sem.at[n]).start()
            else:
                target = (place, flip(me, m))
                sent.append(remote(piece, held.at[n], swap_send.at[n], fill_sem.at[n], target))
            n += 1
    scatter_b.start()
    jobs = []
    for k in range(1, scatter_a.steps):
        jobs += [functools.partial(scatter_a.step, k), functools.partial(scatter_b.step, k)]
    jobs += [functools.partial(scatter_a.finish, branch_own), functools.partial(scatter_b.finish, normed_own)]
    done = 0
    for i, job in enumerate(jobs):
        upto = chain.last_step * (i + 1) // (len(jobs) + 1)
        chain.run(done, upto, total)
        done = upto
        job()
    chain.run(done, chain.last_step, total)
    scatter_a.drain()
    scatter_b.drain()
    for copy in sent:
        copy.wait_send()
    chain.drain()


def reduce_all(branch, normed, weight, out_w, small, size, seq):
    away = pl.BlockSpec(memory_space=pl.ANY)
    here = pl.BlockSpec(memory_space=pltpu.VMEM)
    tt, width = branch.shape[1:]
    share, cols = weight.shape[1:]
    rows = share // 2
    chunks = (weight.size + out_w.size + small.size) // (rows * cols)
    return pl.pallas_call(
        functools.partial(tail_kernel, size, seq),
        in_specs=[away] * 5,
        out_specs=[here] * 3,
        out_shape=[jax.ShapeDtypeStruct((tt, width), jnp.bfloat16)] * 2
        + [jax.ShapeDtypeStruct((chunks, rows, cols), jnp.bfloat16)],
        scratch_shapes=RowScatter.scratch(size, tt, width) * 2
        + SeqSum.scratch(chunks, (rows, cols))
        + [pltpu.SemaphoreType.DMA((chunks,))],
        compiler_params=pltpu.CompilerParams(
            vmem_limit_bytes=60 * MIB, collective_id=4, has_side_effects=True
        ),
        name="reduce_all",
    )(branch, normed, weight, out_w, small)


def from_behind(value, axis, steps):
    count = lax.axis_size(axis)
    first, last = (max(0, -steps), min(count, count - steps))
    return lax.ppermute(value, axis, [(source, source + steps) for source in range(first, last)])


def shortened(x):
    return x.astype(jnp.bfloat16)


def contract_rows(left, right):
    return lax.dot_general(left, right, (((0,), (0,)), ((), ())), preferred_element_type=jnp.float32)


def contract_cols(left, right):
    return lax.dot_general(left, right, (((1,), (1,)), ((), ())), preferred_element_type=jnp.float32)


def local(
    tokens, resets, norm_gain, in_proj, x_proj, dt_proj, conv_weight, conv_bias, dt_bias, a_log, out_proj,
    cotangent,
):
    size = lax.axis_size("rows")
    seq = lax.axis_size("seq")
    rd, tt, unused_d = tokens.shape
    nr = rd * size
    el = E // size
    count = nr * tt
    assert rd == 1 and ITEM % tt == 0 and nr % 8 == 0

    w_in = lax.all_to_all(
        in_proj.reshape(D // size, 2, size, el), "rows", split_axis=2, concat_axis=0, tiled=True
    ).reshape(D, 2 * el)
    share = D // size
    notes = jnp.zeros((16, -(-share // 256) * 256), jnp.bfloat16)
    notes = notes.at[0, :share].set(norm_gain).at[1, 0].set(1.0 - resets[0, 0].astype(jnp.bfloat16))
    all_tokens, all_cot, all_notes = gather_rows([tokens[0], cotangent[0], notes], size)
    all_tokens, all_cot = all_tokens.reshape(count, D), all_cot.reshape(count, D)
    gain = all_notes[:, 0, :share].reshape(D).astype(jnp.float32)
    alive = all_notes[:, 1, :1].astype(jnp.float32)

    flat = all_tokens.astype(jnp.float32)
    inv_all = lax.rsqrt(jnp.mean(flat * flat, axis=1, keepdims=True) + epsilon)
    normed = (flat * inv_all * gain).astype(jnp.bfloat16)
    mixed = jnp.dot(normed, w_in, preferred_element_type=jnp.float32)
    conv_in = mixed[:, :el].astype(jnp.bfloat16).reshape(nr, tt, el)
    gate_pre = mixed[:, el:]
    left_rim = from_behind(conv_in[:, tt - (KC - 1) :], "seq", 1)
    extended = jnp.concatenate([left_rim, conv_in], axis=1)
    taps = conv_weight.astype(jnp.float32)
    conv_pre = conv_bias.astype(jnp.float32) + sum(
        taps[k] * extended[:, k : k + tt].astype(jnp.float32) for k in range(KC)
    )
    conv_out = jax.nn.silu(conv_pre).astype(jnp.bfloat16).reshape(count, el)
    dt_pad = jnp.pad(dt_proj, ((0, LANES - R), (0, 0)))
    proj_t, step_size, rank_all = project(
        conv_out.reshape(nr, tt, el), x_proj, dt_pad, dt_bias.astype(jnp.float32)[None]
    )
    step_size = step_size.reshape(count, el)
    rank_part = rank_all.reshape(count, LANES)[:, :R]
    decay_rate = -jnp.exp(a_log.astype(jnp.float32))
    rate2 = decay_rate * LOG2E
    conv_float = conv_out.astype(jnp.float32)

    grad_gated = contract_cols(all_cot, out_proj)
    gate_sig = jax.nn.sigmoid(gate_pre)
    gate_act = gate_pre * gate_sig
    grad_y = grad_gated * gate_act

    wide = -(-el // LANES) * LANES
    extra = [(0, 0), (0, wide - el)]
    scanned = [jnp.pad(v, extra) for v in (step_size, conv_float, grad_y)]
    rate2 = jnp.pad(rate2, extra)
    ends = scan_ends(*scanned, proj_t, rate2, nr, tt)
    carry = exchange_carry(ends, alive, seq)
    scan_y, grad_delta, grad_input, grad_bc, grate = scan_main(
        *scanned, proj_t, rate2, carry, nr, tt
    )
    scan_y, grad_delta, grad_input = scan_y[:, :el], grad_delta[:, :el], grad_input[:, :el]
    grate = grate[:, :, :el]
    grad_a_log = jnp.sum(grate, axis=1) * decay_rate

    gated = (scan_y * gate_act).astype(jnp.bfloat16)
    branch = jnp.dot(gated, out_proj, preferred_element_type=jnp.float32).astype(jnp.bfloat16)
    grad_out_proj = contract_rows(gated, all_cot)
    grad_gate_pre = grad_gated * scan_y * gate_sig * (1.0 + gate_pre * (1.0 - gate_sig))

    grad_step_pre = grad_delta * -jnp.expm1(-step_size)
    grad_dt_bias = jnp.sum(grad_step_pre, axis=0)
    low_step = grad_step_pre.astype(jnp.bfloat16)
    grad_dt_proj = contract_rows(rank_part, low_step)
    grad_projected = back_project(low_step.reshape(nr, tt, el), dt_pad, grad_bc).reshape(count, LANES)
    grad_x_proj = contract_rows(conv_out, grad_projected)
    grad_conv_out = contract_cols(grad_projected, x_proj) + grad_input
    conv_sig = jax.nn.sigmoid(conv_pre).reshape(count, el)
    conv_flat = conv_pre.reshape(count, el)
    grad_conv_pre = (grad_conv_out * conv_sig * (1.0 + conv_flat * (1.0 - conv_sig))).reshape(nr, tt, el)
    grad_conv_bias = jnp.sum(grad_conv_pre, axis=(0, 1))
    grad_taps = jnp.stack(
        [
            jnp.sum(grad_conv_pre * extended[:, k : k + tt].astype(jnp.float32), axis=(0, 1))
            for k in range(KC)
        ]
    )
    grad_ext = sum(
        jnp.pad(taps[k] * grad_conv_pre, ((0, 0), (k, KC - 1 - k), (0, 0))) for k in range(KC)
    )
    right_rim = from_behind(shortened(grad_ext[:, : KC - 1]), "seq", -1)
    grad_conv_in = grad_ext[:, KC - 1 :] + jnp.pad(
        right_rim.astype(jnp.float32), ((0, 0), (tt - (KC - 1), 0), (0, 0))
    )
    grad_mixed = jnp.concatenate([grad_conv_in.reshape(count, el), grad_gate_pre], axis=1).astype(
        jnp.bfloat16
    )
    grad_in_proj = contract_rows(normed, grad_mixed).astype(jnp.bfloat16)
    grad_normed_part = contract_cols(grad_mixed, w_in).astype(jnp.bfloat16)
    small = jnp.concatenate(
        [grad_x_proj.T, grad_dt_proj, grad_taps, grad_conv_bias[None], grad_dt_bias[None], grad_a_log],
        axis=0,
    )
    piece = (share // 2, 2 * el)
    folded = shortened(small)
    folded = jnp.pad(folded, ((0, -folded.shape[0] % 2), (0, 0)))
    high = folded.shape[0] // 2
    folded = jnp.concatenate([folded[:high], folded[high:]], axis=1)
    folded = jnp.pad(folded, ((0, -high % piece[0]), (0, 0)))
    branch_own, grad_normed, summed = reduce_all(
        branch.reshape(nr, tt, D), grad_normed_part.reshape(nr, tt, D),
        grad_in_proj.reshape(size, share, 2 * el), shortened(grad_out_proj), folded, size, seq,
    )
    summed = summed.astype(jnp.float32)
    out_rows, out_cols = el // piece[0], D // piece[1]
    at = out_rows * out_cols
    sum_out = jnp.swapaxes(summed[:at].reshape(out_rows, out_cols, *piece), 1, 2).reshape(el, D)
    folded = summed[at : at + folded.shape[0] // piece[0]].reshape(folded.shape)
    small = jnp.concatenate([folded[:high, :el], folded[:high, el:]], axis=0)
    blocks = summed[-2 * size :].reshape(size, share, 2, el)
    me = lax.axis_index("rows")
    places = [chunk_order(size).index(m) for m in range(size)]
    order = jnp.array(places)[jnp.array(range(size)) ^ me]
    sum_in = jnp.moveaxis(blocks[order], 0, 2).reshape(share, 2 * E)
    block_out = (tokens.astype(jnp.float32) + branch_own[None].astype(jnp.float32)).astype(jnp.bfloat16)
    grad_normed = grad_normed[None].astype(jnp.float32)

    own = tokens.astype(jnp.float32)
    inv = lax.rsqrt(jnp.mean(own * own, axis=2, keepdims=True) + epsilon)
    gain_own = jnp.sum(in_proj.astype(jnp.float32) * sum_in, axis=1) / norm_gain.astype(jnp.float32)
    grad_hat = grad_normed * gain
    grad_norm_in = inv * (
        grad_hat - own * (inv * inv) * jnp.mean(grad_hat * own, axis=2, keepdims=True)
    )
    d_tokens = (cotangent.astype(jnp.float32) + grad_norm_in).astype(jnp.bfloat16)

    cuts = [128, R, KC, 1, 1, NS]
    parts = []
    at = 0
    for cut in cuts:
        parts.append(small[at : at + cut])
        at += cut
    return (
        block_out,
        d_tokens,
        gain_own,
        sum_in,
        parts[0].T,
        parts[1],
        parts[2],
        parts[3][0],
        parts[4][0],
        parts[5],
        sum_out,
    )


def solution(mesh):
    in_specs = (
        P("rows", "seq", None),
        P("rows", "seq"),
        P("rows"),
        P("rows", None),
        P("rows", None),
        P(None, "rows"),
        P(None, "rows"),
        P("rows"),
        P("rows"),
        P(None, "rows"),
        P("rows", None),
        P("rows", "seq", None),
    )
    out_specs = (
        P("rows", "seq", None),
        P("rows", "seq", None),
        P("rows"),
        P("rows", None),
        P("rows", None),
        P(None, "rows"),
        P(None, "rows"),
        P("rows"),
        P("rows"),
        P(None, "rows"),
        P("rows", None),
    )
    return jax.shard_map(local, mesh=mesh, in_specs=in_specs, out_specs=out_specs, check_vma=False)
```

time: 3410 us -> 544 us (0.16); the launches traced: 3370 us -> 536 us
  other arithmetic: 2310 us -> 37.8 us
  waiting for transfers between devices: 434 us -> 3.72 us
  Pallas kernels: 0 us -> 385 us
  local copies, waits for them, and re-layouts: 336 us -> 52.8 us
  blocking collectives: 162 us -> 0 us
    reduce_sum x369 -> x5, other arithmetic: 1510 us -> 7.61 us  [the longest x1 4.23 us: local(): inv_all = lax.rsqrt(jnp.mean(flat * flat, axis=1, keepdims=True) + epsilon)]
    add x97 -> x1, other arithmetic: 577 us -> 0.95 us  [local(): sum((jnp.pad(taps[k] * grad_conv_pre, ((0, 0), (k, KC - 1 - k), (0, 0)))...]
    pallas_call x0 -> x7, Pallas kernels: none -> 385 us  [the longest x1 129 us: reduce_all(): pl.pallas_call(functools.partial(tail_kernel, size, seq), in_specs=[away]...]
    reduce_scatter x3 -> x0, waiting for transfers between devices: 239 us -> none  [the longest x1 130 us: local(): lax.psum_scatter(grad_in_proj.astype(jnp.bfloat16), 'rows', scatter_dimen...]
    mul x145 -> x2, other arithmetic: 192 us -> 3.93 us  [the longest x1 3.31 us: local(): taps[k] * grad_conv_pre]
    squeeze x272 -> x0, local copies, waits for them, and re-layouts: 185 us -> none  [forward_states(): return lax.scan(advance, initial, pieces)]
    psum x1 -> x0, waiting for transfers between devices: 121 us -> none  [local(): lax.psum(partial_rows[1].astype(jnp.bfloat16), 'seq').astype(jnp.float32)]
    all_gather x9 -> x0, blocking collectives: 104 us -> none  [the longest x3 45.1 us: carried_in(): lax.all_gather(part.astype(kind), axis)]
where the time goes in v1:
time: 544 us; the launch traced here: 536 us
  Pallas kernels  385 us (71%)
  local copies, waits for them, and re-layouts  52.8 us (10%)
  matrix products  43.5 us (8%)
  other arithmetic  37.8 us (7%)
  starting transfers between devices  10.9 us (2%)
    pallas_call x1, Pallas kernels, reduce_all(): pl.pallas_call(functools.partial(tail_kernel, size, seq), in_specs=[away]...  129 us
    pallas_call x1, Pallas kernels, scan_main(): pl.pallas_call(functools.partial(main_kernel, nr, tt, ct, min(8, ct)), in...  90.8 us
    pallas_call x1, Pallas kernels, gather_rows(): pl.pallas_call(functools.partial(gather_kernel, size, count), in_specs=[a...  84.5 us
    pallas_call x1, Pallas kernels, scan_ends(): pl.pallas_call(functools.partial(ends_kernel, nr, tt, ct, min(8, ct)), in...  36.3 us
    unnamed x94, local copies, waits for them, and re-layouts  17 us
    pallas_call x1, Pallas kernels, project(): pl.pallas_call(functools.partial(project_kernel, size), in_specs=[here] *...  16 us
    dot_general x3, matrix products, contract_cols(): lax.dot_general(left, right, (((1,), (1,)), ((), ())), preferred_element_...  16 us
    pallas_call x1, Pallas kernels, back_project(): pl.pallas_call(functools.partial(back_project_kernel, size), in_specs=[he...  14.6 us
  transfers between devices with their start and end apart: 3, of which 1 were waited for; matrix products, arithmetic and copies ran while one was open for 4% of the time, Pallas kernels for 16%

profile of v1, /device:TPU:0, one launch (start us, length us, event | category | flops | bytes accessed | tf_op | source)
XLA Modules:
  0.0 536.2 jit_solution(13211307492553525734)
XLA Ops:
  0.6 2.2 copy.42
  2.8 3.2 copy.32
  6.1 5.3 all-to-all-start
  11.4 0.5 slice.172
  12.7 0.6 copy-done.31
  13.3 84.5 %gather_rows.1 = (bf16[8,256,1536]{2,1,0:T(8,128)(2,1)}, bf16[8,256,1536]{2,1,0:T(8,128)(2,1)}, bf16[8,16,256]{2,1,0:T(8,128)(2,1)}) custom-call(bf16[256,1536]{1,0:T(8,128)(2,1)} %bitcast.114, bf16[256,1536]{1,0:T(8,128)(2,1)} %bitcast.123, bf16[16,256]{1,0:T(8,128)(2,1)} %copy-done.31), custom_call_target="tpu_custom_call" | custom-call | tf_op jit(solution)/shard_map/gather_rows/pallas_call | solution.py:669
  97.8 0.7 slice_convert_fusion.2
  98.5 0.8 convert_reduce_fusion
  99.4 0.6 gather_fusion
  100.1 0.6 fusion.32.a_ref
  100.8 4.2 multiply_reduce_fusion
  105.4 4.1 multiply_convert_fusion
  109.5 4.2 fusion.1
  113.7 0.5 copy.43
  114.2 8.2 %fusion.41 = f32[2048,768]{1,0:T(8,128)S(1)} fusion(bf16[2048,1536]{1,0:T(8,128)(2,1)} %bitcast.120, bf16[1536,768]{1,0:T(8,128)(2,1)S(1)} %bitcast.124), kind=kOutput, calls=%fused_computation.106 | convolution fusion | flops 4831838208 | bytes 14942208 | tf_op jit(solution)/shard_map/dot_general | solution.py:1016
  122.7 4.2 collective-permute-start
  126.9 5.5 %fusion.29 = (f32[2048,384]{1,0:T(8,128)}, f32[2048,384]{1,0:T(8,128)}) fusion(f32[2048,768]{1,0:T(8,128)S(1)} %fusion.41, bf16[2048,1536]{1,0:T(8,128)(2,1)S(1)} %bitcast.140, bf16[384,1536]{1,0:T(8,128)(2,1)S(1)} %copy-done.37), kind=kOutput, calls=%fused_computation.75 | convolution fusion | flops 2419851264 | bytes 16908288 | tf_op jit(solution)/shard_map/dot_general | solution.py:987
  132.4 3.3 add_divide_fusion.1
  135.8 0.9 multiply_convert_fusion.3.conv_ref
  136.6 0.8 copy-done.12
  137.4 2.1 bitcast_convert_fusion.x_in
  139.5 16.0 %project.1 = (f32[2048,128]{1,0:T(8,128)S(1)}, f32[8,256,384]{2,1,0:T(8,128)S(1)}, bf16[8,256,128]{2,1,0:T(8,128)(2,1)S(1)}) custom-call(bf16[8,256,384]{2,1,0:T(8,128)(2,1)S(1)} %multiply_convert_fusion.3.conv_ref, bf16[384,128]{1,0:T(8,128)(2,1)S(1)} %copy-done.8, bf16[128,384]{1,0:T(8,128)(2,1)S(1)} %pad.40.dt_ref, f32[1,384]{1,0:T(1,128)S(1)} %reshape.282.bias_ref), custom_call_target="tpu_custom_call" | custom-call | tf_op jit(solution)/shard_map/project/pallas_call | solution.py:441
  155.6 1.7 copy-done
  157.3 1.0 copy-done.4
  158.3 36.3 %scan_ends.1.ends_ref = f32[3,16,8,384]{3,2,1,0:T(8,128)} custom-call(f32[2048,384]{1,0:T(8,128)} %bitcast.98, f32[2048,384]{1,0:T(8,128)} %bitcast_convert_fusion.x_in, f32[2048,384]{1,0:T(8,128)} %get-tuple-element.116.gy_in, f32[2048,128]{1,0:T(8,128)} %copy-done.4, f32[16,384]{1,0:T(8,128)} %fusion.32.a_ref), custom_call_target="tpu_custom_call" | custom-call | tf_op jit(solution)/shard_map/scan_ends/pallas_call | solution.py:122
  194.6 1.1 copy-done.5
  195.7 13.3 %exchange_carry.1.carry_ref = f32[2,16,8,384]{3,2,1,0:T(8,128)S(1)} custom-call(f32[3,16,8,384]{3,2,1,0:T(8,128)S(1)} %copy-done.5, f32[8,1]{1,0:T(8,128)S(1)} %bitcast.103), custom_call_target="tpu_custom_call" | custom-call | tf_op jit(solution)/shard_map/exchange_carry/pallas_call | solution.py:560
  209.0 0.7 copy-done.6
  209.8 90.8 %scan_main.1 = (f32[2048,384]{1,0:T(8,128)}, f32[2048,384]{1,0:T(8,128)}, f32[2048,384]{1,0:T(8,128)}, f32[2048,128]{1,0:T(8,128)}, f32[16,8,384]{2,1,0:T(8,128)}) custom-call(f32[2048,384]{1,0:T(8,128)} %bitcast.99, f32[2048,384]{1,0:T(8,128)} %bitcast_convert_fusion.x_in, f32[2048,384]{1,0:T(8,128)} %get-tuple-element.116.gy_in, f32[2048,128]{1,0:T(8,128)} %copy-done.4, ...), custom_call_target="tpu_custom_call" | custom-call | tf_op jit(solution)/shard_map/scan_main/pallas_call | solution.py:293
  300.6 4.5 multiply_convert_fusion.1
  305.1 6.6 %convolution_convert_fusion.3.refs_3_ = bf16[384,1536]{1,0:T(8,128)(2,1)} fusion(bf16[2048,384]{1,0:T(8,128)(2,1)S(1)} %get-tuple-element.101, bf16[2048,1536]{1,0:T(8,128)(2,1)} %bitcast.137), kind=kOutput, calls=%fused_computation.42 | convolution fusion | flops 2416508928 | bytes 9043968 | tf_op jit(solution)/shard_map/dot_general | solution.py:983
  311.7 5.2 convolution_convert_fusion.1
  317.0 1.3 fusion.24
  318.8 14.6 %back_project.1 = bf16[8,256,128]{2,1,0:T(8,128)(2,1)S(1)} custom-call(bf16[8,256,384]{2,1,0:T(8,128)(2,1)S(1)} %bitcast.100, bf16[128,384]{1,0:T(8,128)(2,1)S(1)} %pad.40.dt_ref, f32[2048,128]{1,0:T(8,128)S(1)} %copy-done.7), custom_call_target="tpu_custom_call" | custom-call | tf_op jit(solution)/shard_map/back_project/pallas_call | solution.py:478
  333.4 0.5 fusion.23
  334.0 3.2 fusion.8
  337.2 1.6 copy-done.14
  338.9 2.3 fusion.38
  341.6 3.3 broadcast_multiply_fusion.3
  345.0 1.0 pad_add_fusion
  345.9 1.4 collective-permute-start.1
  347.4 0.7 fusion.30.refs_4_
  348.1 3.7 collective-permute-done.1
  352.2 7.3 %convolution_convert_fusion = bf16[2048,1536]{1,0:T(8,128)(2,1)} fusion(bf16[1536,768]{1,0:T(8,128)(2,1)S(1)} %bitcast.125, bf16[2048,384]{1,0:T(8,128)(2,1)S(1)} %get-tuple-element.100, bf16[2048,384]{1,0:T(8,128)(2,1)S(1)} %bitcast.133), kind=kOutput, calls=%fused_computation.7 | convolution fusion | flops 4841275392 | bytes 11796480 | tf_op jit(solution)/shard_map/dot_general | solution.py:987
  359.5 6.5 %convolution_convert_fusion.2 = bf16[1536,768]{1,0:T(8,128)(2,1)} fusion(bf16[2048,1536]{1,0:T(8,128)(2,1)S(1)} %bitcast.119, bf16[2048,384]{1,0:T(8,128)(2,1)S(1)} %get-tuple-element.100, bf16[2048,384]{1,0:T(8,128)(2,1)S(1)} %bitcast.134), kind=kOutput, calls=%fused_computation.16 | convolution fusion | flops 4839309312 | bytes 11796480 | tf_op jit(solution)/shard_map/dot_general | solution.py:983
  366.0 129.3 %reduce_all.1 = (bf16[256,1536]{1,0:T(8,128)(2,1)}, bf16[256,1536]{1,0:T(8,128)(2,1)}, bf16[26,96,768]{2,1,0:T(8,128)(2,1)}) custom-call(bf16[8,256,1536]{2,1,0:T(8,128)(2,1)} %bitcast.121, bf16[8,256,1536]{2,1,0:T(8,128)(2,1)} %bitcast.122, bf16[8,192,768]{2,1,0:T(8,128)(2,1)} %bitcast.127, bf16[384,1536]{1,0:T(8,128)(2,1)} %convolution_convert_fusion.3.refs_3_, ...), custom_call_target="tpu_custom_call" | custom-call | tf_op jit(solution)/shard_map/reduce_all/pallas_call | solution.py:956
  495.3 1.0 slice.189
  496.4 0.6 slice_reduce_fusion
  497.0 0.6 slice.193
  497.6 0.6 slice.196
  498.2 0.7 slice.192
  498.9 1.5 slice.197
  500.4 2.7 slice.188
  503.6 0.8 copy.39
  504.4 1.8 copy.38
  506.2 1.6 copy.46
  507.7 6.7 %reshape.276 = f32[8,192,2,384]{3,2,1,0:T(2,128)} reshape(f32[16,96,768]{2,1,0:T(8,128)} %slice.188) | data formatting | bytes 9437184 | tf_op jit(solution)/shard_map/reshape | solution.py:1108
  514.5 9.4 %gather_fusion.1 = f32[8,192,2,384]{3,2,1,0:T(2,128)} fusion(f32[8,192,2,384]{3,2,1,0:T(2,128)} %reshape.276, s32[1024]{0:T(1024)S(1)} %pad_clamp_fusion), kind=kCustom, calls=%fused_computation.1 | custom fusion | bytes 9437216 | tf_op jit(solution)/shard_map/gather | solution.py:1112
  523.9 5.1 copy.37
  529.0 1.8 copy.45
  530.8 0.6 multiply_reduce_fusion.1
  531.4 1.8 copy-done.10
  533.2 0.6 convert_divide_fusion
  534.1 1.7 fusion.21
  (119 shorter events, 3.0 us)
Async XLA Ops:
  6.0 5.4 %copy-start.39 = (s32[1,256]{1,0:T(1,128)S(1)}, s32[1,256]{1,0:T(1,128)}, u32[]{:S(2)}) copy-start(s32[1,256]{1,0:T(1,128)} %param.19) | copy-start | bytes 3076
  6.0 6.5 %copy-start.35 = (bf16[192]{0:T(256)(128)(2,1)S(1)}, bf16[192]{0:T(256)(128)(2,1)}, u32[]{:S(2)}) copy-start(bf16[192]{0:T(256)(128)(2,1)} %param.20) | copy-start | bytes 1156
  6.0 93.2 %copy-start.34 = (bf16[384]{0:T(512)(128)(2,1)S(1)}, bf16[384]{0:T(512)(128)(2,1)}, u32[]{:S(2)}) copy-start(bf16[384]{0:T(512)(128)(2,1)} %param.26) | copy-start | bytes 2308
  6.0 93.3 %copy-start.33 = (bf16[384]{0:T(512)(128)(2,1)S(1)}, bf16[384]{0:T(512)(128)(2,1)}, u32[]{:S(2)}) copy-start(bf16[384]{0:T(512)(128)(2,1)} %param.25) | copy-start | bytes 2308
  6.1 94.0 %copy-start.32 = (bf16[4,384]{1,0:T(4,128)(2,1)S(1)}, bf16[4,384]{1,0:T(4,128)(2,1)}, u32[]{:S(2)}) copy-start(bf16[4,384]{1,0:T(4,128)(2,1)} %param.24) | copy-start | bytes 9220
  6.1 94.0 %copy-start.30 = (bf16[16,384]{1,0:T(8,128)(2,1)S(1)}, bf16[16,384]{1,0:T(8,128)(2,1)}, u32[]{:S(2)}) copy-start(bf16[16,384]{1,0:T(8,128)(2,1)} %param.27) | copy-start | bytes 36868
  6.1 94.6 %copy-start.29 = (bf16[96,384]{1,0:T(8,128)(2,1)S(1)}, bf16[96,384]{1,0:T(8,128)(2,1)}, u32[]{:S(2)}) copy-start(bf16[96,384]{1,0:T(8,128)(2,1)} %param.23) | copy-start | bytes 221188
  6.1 107.6 %all-to-all-start = ((bf16[192,2,8,384]{3,1,0,2:T(2,128)(2,1)}), bf16[192,2,8,384]{3,1,0,2:T(2,128)(2,1)S(1)}, u32[]{:S(2)}, u32[]{:S(2)}) async-start(bf16[192,2,8,384]{3,1,0,2:T(2,128)(2,1)} %copy.32), calls=%async_computation | async-start | bytes 4718592 | tf_op jit(solution)/shard_map/all_to_all | solution.py:1002
  12.7 0.6 copy-start.31
  100.8 4.6 copy-start.9
  113.7 13.2 %slice-start.2 = ((s8[6291456]{0:T(1024)(128)(4,1)}), s8[4194304]{0:T(1024)(128)(4,1)S(1)}, s32[]{:S(2)}) async-start(s8[6291456]{0:T(1024)(128)(4,1)} %bitcast.138), calls=%async_computation.3 | async-start | bytes 8388608
  114.2 8.3 %copy-start.25 = (bf16[192,8,2,384]{3,1,2,0:T(8,128)(2,1)}, bf16[192,8,2,384]{3,1,2,0:T(8,128)(2,1)S(1)}, u32[]{:S(2)}) copy-start(bf16[192,8,2,384]{3,1,2,0:T(8,128)(2,1)S(1)} %copy.43) | copy-start | bytes 7077892
  114.2 12.7 %slice-start.3 = ((s8[6291456]{0:T(1024)(128)(4,1)}), s8[2097152]{0:T(1024)(128)(4,1)S(1)}, s32[]{:S(2)}) async-start(s8[6291456]{0:T(1024)(128)(4,1)} %bitcast.138), calls=%async_computation.4 | async-start | bytes 4194304
  122.5 10.0 %copy-start.19 = (f32[2048,768]{1,0:T(8,128)}, f32[2048,768]{1,0:T(8,128)S(1)}, u32[]{:S(2)}) copy-start(f32[2048,768]{1,0:T(8,128)S(1)} %fusion.41) | copy-start | bytes 18874372
  122.5 4.5 copy-start.37
  122.7 9.8 %copy-start.17 = (bf16[2048,384]{1,0:T(8,128)(2,1)}, bf16[2048,384]{1,0:T(8,128)(2,1)S(1)}, u32[]{:S(2)}) copy-start(bf16[2048,384]{1,0:T(8,128)(2,1)S(1)} %slice.243) | copy-start | bytes 4718596
  122.7 9.7 %collective-permute-start = (bf16[8,3,384]{2,1,0:T(4,128)(2,1)S(1)}, bf16[8,3,384]{2,1,0:T(4,128)(2,1)S(1)}, u32[]{:S(2)}, u32[]{:S(2)}) collective-permute-start(bf16[8,3,384]{2,1,0:T(4,128)(2,1)S(1)} %slice.174), channel_id=1, source_target_pairs={{0,8},{8,16},{16,24},{1,9},{9,17},{17,25},{2,10},{10,18},{18,26},{... | collective-permute-start | bytes 55304 | tf_op jit(solution)/shard_map/ppermute | solution.py:975
  135.7 1.7 copy-start.12
  137.4 18.1 %copy-start.2 = (bf16[8,256,384]{2,1,0:T(8,128)(2,1)}, bf16[8,256,384]{2,1,0:T(8,128)(2,1)S(1)}, u32[]{:S(2)}) copy-start(bf16[8,256,384]{2,1,0:T(8,128)(2,1)S(1)} %multiply_convert_fusion.3.conv_ref) | copy-start | bytes 4718596
  137.4 2.1 copy-start.8
  155.5 1.7 copy-start
  157.3 1.0 copy-start.4
  194.6 1.1 copy-start.5
  209.0 0.7 copy-start.6
  305.1 6.6 %copy-start.38 = (bf16[384,1536]{1,0:T(8,128)(2,1)S(1)}, bf16[384,1536]{1,0:T(8,128)(2,1)}, u32[]{:S(2)}) copy-start(bf16[384,1536]{1,0:T(8,128)(2,1)} %param.28) | copy-start | bytes 3538948
  311.7 5.3 copy-start.1
  311.7 5.3 copy-start.24
  317.0 1.8 copy-start.7
  317.0 17.0 %copy-start.23 = (f32[8,256,384]{2,1,0:T(8,128)S(1)}, f32[8,256,384]{2,1,0:T(8,128)}, u32[]{:S(2)}) copy-start(f32[8,256,384]{2,1,0:T(8,128)} %get-tuple-element.98) | copy-start | bytes 9437188
  317.0 17.0 %copy-start.36 = (f32[2048,384]{1,0:T(8,128)S(1)}, f32[2048,384]{1,0:T(8,128)}, u32[]{:S(2)}) copy-start(f32[2048,384]{1,0:T(8,128)} %get-tuple-element.57) | copy-start | bytes 9437188
  318.3 15.1 %copy-start.3 = (bf16[8,256,384]{2,1,0:T(8,128)(2,1)S(1)}, bf16[8,256,384]{2,1,0:T(8,128)(2,1)}, u32[]{:S(2)}) copy-start(bf16[8,256,384]{2,1,0:T(8,128)(2,1)} %copy-done.2) | copy-start | bytes 4718596
  318.8 15.2 %copy-start.13 = (f32[8,256,384]{2,1,0:T(8,128)S(1)}, f32[8,256,384]{2,1,0:T(8,128)}, u32[]{:S(2)}) copy-start(f32[8,256,384]{2,1,0:T(8,128)} %copy-done.12) | copy-start | bytes 9437188
  318.8 15.2 %copy-start.18 = (bf16[2048,384]{1,0:T(8,128)(2,1)S(1)}, bf16[2048,384]{1,0:T(8,128)(2,1)}, u32[]{:S(2)}) copy-start(bf16[2048,384]{1,0:T(8,128)(2,1)} %copy-done.17) | copy-start | bytes 4718596
  337.2 1.7 copy-start.14
  337.2 4.0 copy-start.28
  345.9 6.3 %copy-start.26 = (bf16[192,8,2,384]{3,1,2,0:T(8,128)(2,1)S(1)}, bf16[192,8,2,384]{3,1,2,0:T(8,128)(2,1)}, u32[]{:S(2)}) copy-start(bf16[192,8,2,384]{3,1,2,0:T(8,128)(2,1)} %copy-done.25) | copy-start | bytes 7077892
  345.9 5.9 %collective-permute-start.1 = (bf16[8,3,384]{2,1,0:T(4,128)(2,1)S(1)}, bf16[8,3,384]{2,1,0:T(4,128)(2,1)S(1)}, u32[]{:S(2)}, u32[]{:S(2)}) collective-permute-start(bf16[8,3,384]{2,1,0:T(4,128)(2,1)S(1)} %slice.244), channel_id=1, source_target_pairs={{8,0},{16,8},{24,16},{9,1},{17,9},{25,17},{10,2},{18,10},{26,18},{... | collective-permute-start | bytes 55304 | tf_op jit(solution)/shard_map/ppermute | solution.py:975
  351.8 7.7 %slice-start = ((s8[6291456]{0:T(1024)(128)(4,1)}), s8[4194304]{0:T(1024)(128)(4,1)S(1)}, s32[]{:S(2)}) async-start(s8[6291456]{0:T(1024)(128)(4,1)} %bitcast.118), calls=%async_computation.1 | async-start | bytes 8388608
  352.2 7.3 %slice-start.1 = ((s8[6291456]{0:T(1024)(128)(4,1)}), s8[2097152]{0:T(1024)(128)(4,1)S(1)}, s32[]{:S(2)}) async-start(s8[6291456]{0:T(1024)(128)(4,1)} %bitcast.118), calls=%async_computation.2 | async-start | bytes 4194304
  496.4 4.0 copy-start.11
  500.4 2.7 copy-start.16
  500.4 2.7 copy-start.21
  528.9 1.8 copy-start.15
  530.8 2.4 copy-start.10
  530.8 3.0 copy-start.20
  530.8 3.0 copy-start.22
  530.8 3.3 copy-start.27

commit v2 on v1

--- a/solution.py
+++ b/solution.py
@@ -29,47 +29,32 @@
 
 
 def selector(wide):
-    row = lax.broadcasted_iota(jnp.int32, (256, 2 * NS * wide), 0) % 128
-    col = lax.broadcasted_iota(jnp.int32, (256, 2 * NS * wide), 1) // wide
+    row = lax.broadcasted_iota(jnp.int32, (LANES, 2 * NS * wide), 0)
+    col = lax.broadcasted_iota(jnp.int32, (LANES, 2 * NS * wide), 1) // wide
     return (row == col + R).astype(jnp.bfloat16)
 
 
 def spread(proj, sel_ref):
-    high = proj.astype(jnp.bfloat16)
-    low = (proj - high.astype(jnp.float32)).astype(jnp.bfloat16)
-    return jnp.dot(
-        jnp.concatenate([high, low], axis=1), sel_ref[...], preferred_element_type=jnp.float32
-    )
-
-
-def load_blocks(sources, targets, sems):
+    return jnp.dot(proj.astype(jnp.bfloat16), sel_ref[...], preferred_element_type=jnp.float32)
+
+
+def copy_all(sources, targets, sems):
     copies = []
     for i, (source, target) in enumerate(zip(sources, targets)):
-        for b in range(target.shape[0]):
-            lanes = pl.ds(b * LANES, LANES)
-            copies.append(pltpu.make_async_copy(source.at[:, lanes], target.at[b], sems.at[i, b]))
-    for copy in copies:
-        copy.start()
+        copies.append(pltpu.make_async_copy(source, target, sems.at[i]))
+        copies[-1].start()
     return copies
 
 
-def store_blocks(sources, targets, sems):
-    copies = []
-    for i, (source, target) in enumerate(zip(sources, targets)):
-        for b in range(source.shape[0]):
-            lanes = pl.ds(b * LANES, LANES)
-            copies.append(pltpu.make_async_copy(source.at[b], target.at[:, lanes], sems.at[i, b]))
-    for copy in copies:
-        copy.start()
-    return copies
-
-
 def ends_kernel(
-    nr, tt, ct, uu, delta_in, x_in, gy_in, proj_ref, a_ref, out_ref, sel, bc, delta_ref, x_ref, gy_ref, sems
+    seq, nr, tt, ct, uu, delta_in, x_in, gy_in, proj_ref, a_ref, alive_ref, carry_ref,
+    out_ref, mail, land, carry_sems, sel, bc, delta_ref, x_ref, gy_ref, sems,
 ):
     el = a_ref.shape[1]
+    carry = Carry(seq, out_ref, alive_ref, carry_ref, mail, land, carry_sems)
+    greet_seq(seq)
     half = NS // 2
-    copies = load_blocks((delta_in, x_in, gy_in), (delta_ref, x_ref, gy_ref), sems)
+    copies = copy_all((delta_in, x_in, gy_in), (delta_ref, x_ref, gy_ref), sems)
     sel[...] = selector(LANES)
     out_ref[0] = jnp.zeros((NS, nr, el), jnp.float32)
     out_ref[1] = jnp.ones((NS, nr, el), jnp.float32)
@@ -90,7 +75,7 @@
                     state, through, back = (list(v) for v in carried)
                     for u in range(uu):
                         at = s * uu + u
-                        here = pl.ds(c * ct + at, nr, stride=tt)
+                        here = pl.ds(pl.multiple_of((c * ct + at) * nr, nr), nr)
                         delta = delta_ref[b, here, :]
                         gy = gy_ref[b, here, :]
                         du = delta * x_ref[b, here, :]
@@ -111,30 +96,36 @@
         return none
 
     lax.fori_loop(0, tt // ct, chunk, 0)
-
-
-def scan_ends(delta, x, gy, proj, rate, nr, tt):
+    carry.both()
+    carry.drain()
+
+
+def scan_ends(delta, x, gy, proj, rate, alive, nr, tt, seq):
     el = rate.shape[1]
     ct = math.gcd(tt, 32)
     here = pl.BlockSpec(memory_space=pltpu.VMEM)
     away = pl.BlockSpec(memory_space=pl.ANY)
     blocks = pltpu.VMEM((el // LANES, nr * tt, LANES), jnp.float32)
     return pl.pallas_call(
-        functools.partial(ends_kernel, nr, tt, ct, min(8, ct)),
-        in_specs=[away] * 3 + [here] * 2,
+        functools.partial(ends_kernel, seq, nr, tt, ct, min(8, ct)),
+        in_specs=[away] * 3 + [here] * 3,
         out_specs=here,
-        out_shape=jax.ShapeDtypeStruct((3, NS, nr, el), jnp.float32),
-        scratch_shapes=[
-            pltpu.VMEM((256, 2 * NS * LANES), jnp.bfloat16),
+        out_shape=jax.ShapeDtypeStruct((2, NS, nr, el), jnp.float32),
+        scratch_shapes=[pltpu.VMEM((3, NS, nr, el), jnp.float32)]
+        + Carry.scratch((NS, nr, el))
+        + [
+            pltpu.VMEM((LANES, 2 * NS * LANES), jnp.bfloat16),
             pltpu.VMEM((ct * nr, 2 * NS * LANES), jnp.float32),
             blocks,
             blocks,
             blocks,
-            pltpu.SemaphoreType.DMA((3, el // LANES)),
+            pltpu.SemaphoreType.DMA((3,)),
         ],
-        compiler_params=pltpu.CompilerParams(vmem_limit_bytes=56 * MIB),
+        compiler_params=pltpu.CompilerParams(
+            vmem_limit_bytes=56 * MIB, collective_id=2, has_side_effects=True
+        ),
         name="scan_ends",
-    )(delta, x, gy, proj, rate)
+    )(delta, x, gy, proj, rate, alive)
 
 
 def main_kernel(
@@ -145,7 +136,7 @@
 ):
     el = a_ref.shape[1]
     blocks = el // LANES
-    copies = load_blocks((delta_in, x_in, gy_in), (delta_ref, x_ref, gy_ref), sems)
+    copies = copy_all((delta_in, x_in, gy_in), (delta_ref, x_ref, gy_ref), sems)
     sel[...] = selector(LANES)
     fold_row = lax.broadcasted_iota(jnp.int32, fold.shape, 0) // LANES
     fold_col = lax.broadcasted_iota(jnp.int32, fold.shape, 1)
@@ -177,7 +168,7 @@
                 for u in range(uu):
                     at = s * uu + u
                     t = c * ct + at
-                    here = pl.ds(t, nr, stride=tt)
+                    here = pl.ds(pl.multiple_of(t * nr, nr), nr)
                     delta = delta_ref[b, here, :]
                     du = delta * x_ref[b, here, :]
                     near = pl.ds(pl.multiple_of(at * nr, nr), nr)
@@ -199,7 +190,7 @@
         return none
 
     lax.fori_loop(0, tt // ct, forward, 0)
-    y_copies = store_blocks((y_ref,), (y_out,), out_sems.at[pl.ds(0, 1)])
+    y_copies = copy_all((y_ref,), (y_out,), out_sems.at[pl.ds(0, 1)])
 
     state_ref[...] = carry_ref[1]
     grate_ref[...] = jnp.zeros_like(grate_ref)
@@ -220,7 +211,7 @@
                     for u in reversed(range(uu)):
                         at = (ct // uu - 1 - s) * uu + u
                         t = c * ct + at
-                        here = pl.ds(t, nr, stride=tt)
+                        here = pl.ds(pl.multiple_of(t * nr, nr), nr)
                         delta = delta_ref[b, here, :]
                         x = x_ref[b, here, :]
                         gy = gy_ref[b, here, :]
@@ -278,7 +269,7 @@
         return none
 
     lax.fori_loop(0, tt // ct, backward, 0)
-    late = store_blocks((gdelta_ref, gx_ref), (gdelta_out, gx_out), out_sems.at[pl.ds(1, 2)])
+    late = copy_all((gdelta_ref, gx_ref), (gdelta_out, gx_out), out_sems.at[pl.ds(1, 2)])
     for copy in y_copies + late:
         copy.wait()
 
@@ -288,7 +279,7 @@
     ct = math.gcd(tt, 32)
     here = pl.BlockSpec(memory_space=pltpu.VMEM)
     away = pl.BlockSpec(memory_space=pl.ANY)
-    full = jax.ShapeDtypeStruct((nr * tt, el), jnp.float32)
+    full = jax.ShapeDtypeStruct((el // LANES, tt * nr, LANES), jnp.float32)
     blocks = pltpu.VMEM((el // LANES, nr * tt, LANES), jnp.float32)
     return pl.pallas_call(
         functools.partial(main_kernel, nr, tt, ct, min(8, ct)),
@@ -302,7 +293,7 @@
             jax.ShapeDtypeStruct((NS, nr, el), jnp.float32),
         ],
         scratch_shapes=[
-            pltpu.VMEM((256, 2 * NS * LANES), jnp.bfloat16),
+            pltpu.VMEM((LANES, 2 * NS * LANES), jnp.bfloat16),
             pltpu.VMEM((ct * nr, 2 * NS * LANES), jnp.float32),
             pltpu.VMEM((el // LANES, tt + 1, NS * nr, LANES), jnp.bfloat16),
             pltpu.VMEM((ct * nr, 2 * NS * LANES), jnp.float32),
@@ -311,8 +302,8 @@
         ]
         + [blocks] * 6
         + [
-            pltpu.SemaphoreType.DMA((3, el // LANES)),
-            pltpu.SemaphoreType.DMA((3, el // LANES)),
+            pltpu.SemaphoreType.DMA((3,)),
+            pltpu.SemaphoreType.DMA((3,)),
         ],
         compiler_params=pltpu.CompilerParams(vmem_limit_bytes=63 * MIB),
         name="scan_main",
@@ -358,11 +349,19 @@
         )
     for j in range(half):
         total[j] = part_of(2 * j + parity)
+    exchange_sums(size, near, total, mail, far, out, sems, use)
     for copy in first:
-        copy.wait()
+        copy.wait_send()
+
+
+def exchange_sums(size, near, total, mail, far, out, sems, use, between=None):
+    me, parity, partner, others = row_peers(size)
+    place = lax.axis_index("seq")
+    half = size // 2
     second = []
     for k in list(range(1, half)) + [0]:
         j = others[k]
+        wait_for(near.at[j], sems.at[1, j])
         total[j] = total[j] + near[j].astype(jnp.float32)
         if k:
             mail[j] = total[j].astype(jnp.bfloat16)
@@ -371,7 +370,7 @@
     mine = others[0]
     done = total[mine]
     for k in range(1, half):
-        second[k - 1].wait()
+        wait_for(far.at[k], sems.at[3, k])
         done = done + far[k].astype(jnp.float32)
     out[me] = done.astype(jnp.bfloat16)
     third = []
@@ -382,24 +381,18 @@
     use(me)
     for k in range(1, half):
         block = 2 * others[half - k] + parity
-        here = pltpu.make_async_remote_copy(
-            src_ref=out.at[me], dst_ref=out.at[block], send_sem=sems.at[4, k], recv_sem=sems.at[5, k],
-            device_id=(place, partner), device_id_type=MESH,
-        )
-        here.wait_recv()
+        wait_for(out.at[block], sems.at[5, k])
         fourth.append(
             remote(out.at[block], out.at[block], sems.at[6, k], sems.at[7, k], (place, partner))
         )
         use(block)
     for k in range(half):
         block = 2 * others[(half - k) % half] + 1 - parity
-        here = pltpu.make_async_remote_copy(
-            src_ref=out.at[me], dst_ref=out.at[block], send_sem=sems.at[6, k], recv_sem=sems.at[7, k],
-            device_id=(place, partner), device_id_type=MESH,
-        )
-        here.wait_recv()
+        wait_for(out.at[block], sems.at[7, k])
         use(block)
-    for copy in third + fourth:
+    if between:
+        between()
+    for copy in second + third + fourth:
         copy.wait_send()
 
 
@@ -414,45 +407,6 @@
         pltpu.VMEM((size, tt, LANES), jnp.bfloat16),
         pltpu.SemaphoreType.DMA((8, half)),
     ]
-
-
-def project_kernel(
-    size, conv_ref, x_proj_ref, dt_ref, bias_ref, proj_ref, delta_ref, rank_ref,
-    part, near, total, mail, far, out, sems,
-):
-    tt = conv_ref.shape[1]
-
-    def part_of(p):
-        return jnp.dot(conv_ref[p], x_proj_ref[...], preferred_element_type=jnp.float32)
-
-    def use(p):
-        block = out[p]
-        rank_ref[p] = block
-        proj_ref[pl.ds(p, tt, stride=size), :] = block.astype(jnp.float32)
-        step = jnp.dot(block, dt_ref[...], preferred_element_type=jnp.float32) + bias_ref[...]
-        delta_ref[p] = jnp.maximum(step, 0.0) + jnp.log1p(jnp.exp(-jnp.abs(step)))
-
-    sum_rows(size, part_of, part, near, total, mail, far, out, sems, use)
-
-
-def project(conv_out, x_proj, dt_pad, bias):
-    size, tt, el = conv_out.shape
-    here = pl.BlockSpec(memory_space=pltpu.VMEM)
-    return pl.pallas_call(
-        functools.partial(project_kernel, size),
-        in_specs=[here] * 4,
-        out_specs=[here] * 3,
-        out_shape=[
-            jax.ShapeDtypeStruct((tt * size, LANES), jnp.float32),
-            jax.ShapeDtypeStruct((size, tt, el), jnp.float32),
-            jax.ShapeDtypeStruct((size, tt, LANES), jnp.bfloat16),
-        ],
-        scratch_shapes=sum_scratch(size, tt),
-        compiler_params=pltpu.CompilerParams(
-            vmem_limit_bytes=40 * MIB, collective_id=0, has_side_effects=True
-        ),
-        name="project",
-    )(conv_out, x_proj, dt_pad, bias)
 
 
 def back_project_kernel(
@@ -488,90 +442,67 @@
     )(low_step, dt_pad, gbc)
 
 
-def carry_kernel(seq, ends_ref, alive_ref, out_ref, mail, land, sems):
-    place = lax.axis_index("seq")
-    me = lax.axis_index("rows")
-    barrier = pltpu.get_barrier_semaphore()
-    alive = alive_ref[...][None]
-
-    for step, there in ((-1, place > 0), (1, place < seq - 1)):
-
-        @pl.when(there)
-        def _(step=step):
-            pl.semaphore_signal(barrier, inc=1, device_id=(place + step, me), device_id_type=MESH)
-
-    pl.semaphore_wait(barrier, (place > 0).astype(jnp.int32) + (place < seq - 1).astype(jnp.int32))
-
-    def hop(way):
-        first, last, step = ((0, seq - 1, 1), (seq - 1, 0, -1))[way]
-        target = (jnp.clip(place + step, 0, seq - 1), me)
-        copy = pltpu.make_async_remote_copy(
-            src_ref=mail.at[way], dst_ref=land.at[way], send_sem=sems.at[way, 0], recv_sem=sems.at[way, 1],
-            device_id=target, device_id_type=MESH,
-        )
-
-        @pl.when(place == first)
-        def _():
-            out_ref[way] = jnp.zeros_like(out_ref[way])
-
-        @pl.when(place != first)
-        def _():
-            copy.wait_recv()
-            entering = land[way].astype(jnp.float32)
-            out_ref[way] = entering * alive if way == 0 else entering
-
-        @pl.when(place != last)
-        def _():
-            if way == 0:
-                leaving = ends_ref[0] + ends_ref[1] * out_ref[0]
-            else:
-                leaving = (ends_ref[2] + ends_ref[1] * out_ref[1]) * alive
-            mail[way] = leaving.astype(jnp.bfloat16)
-            copy.start()
-
-    def finish(way):
-        last, step = ((seq - 1, 1), (0, -1))[way]
-        target = (jnp.clip(place + step, 0, seq - 1), me)
-
-        @pl.when(place != last)
-        def _():
-            pltpu.make_async_remote_copy(
-                src_ref=mail.at[way], dst_ref=land.at[way], send_sem=sems.at[way, 0],
-                recv_sem=sems.at[way, 1], device_id=target, device_id_type=MESH,
-            ).wait_send()
-
-    @pl.when(place < seq // 2)
-    def _():
-        hop(0)
-        hop(1)
-
-    @pl.when(place >= seq // 2)
-    def _():
-        hop(1)
-        hop(0)
-
-    finish(0)
-    finish(1)
-
-
-def exchange_carry(ends, alive, seq):
-    here = pl.BlockSpec(memory_space=pltpu.VMEM)
-    shape = ends.shape[1:]
-    return pl.pallas_call(
-        functools.partial(carry_kernel, seq),
-        in_specs=[here] * 2,
-        out_specs=here,
-        out_shape=jax.ShapeDtypeStruct((2,) + shape, jnp.float32),
-        scratch_shapes=[
+class Carry:
+    def __init__(self, seq, ends, alive, out, mail, land, sems):
+        self.seq, self.ends, self.alive, self.out = seq, ends, alive, out
+        self.mail, self.land, self.sems = mail, land, sems
+        self.me, self.place = lax.axis_index("rows"), lax.axis_index("seq")
+
+    @staticmethod
+    def scratch(shape):
+        return [
             pltpu.VMEM((2,) + shape, jnp.bfloat16),
             pltpu.VMEM((2,) + shape, jnp.bfloat16),
             pltpu.SemaphoreType.DMA((2, 2)),
-        ],
-        compiler_params=pltpu.CompilerParams(
-            vmem_limit_bytes=40 * MIB, collective_id=2, has_side_effects=True
-        ),
-        name="exchange_carry",
-    )(ends, alive)
+        ]
+
+    def copy(self, way):
+        target = (jnp.clip(self.place + 1 - 2 * way, 0, self.seq - 1), self.me)
+        return pltpu.make_async_remote_copy(
+            src_ref=self.mail.at[way], dst_ref=self.land.at[way], send_sem=self.sems.at[way, 0],
+            recv_sem=self.sems.at[way, 1], device_id=target, device_id_type=MESH,
+        )
+
+    def hop(self, way):
+        first, last = ((0, self.seq - 1), (self.seq - 1, 0))[way]
+        alive = self.alive[...][None]
+
+        @pl.when(self.place == first)
+        def _():
+            self.out[way] = jnp.zeros_like(self.out[way])
+
+        @pl.when(self.place != first)
+        def _():
+            self.copy(way).wait_recv()
+            entering = self.land[way].astype(jnp.float32)
+            self.out[way] = entering * alive if way == 0 else entering
+
+        @pl.when(self.place != last)
+        def _():
+            if way == 0:
+                leaving = self.ends[0] + self.ends[1] * self.out[0]
+            else:
+                leaving = (self.ends[2] + self.ends[1] * self.out[1]) * alive
+            self.mail[way] = leaving.astype(jnp.bfloat16)
+            self.copy(way).start()
+
+    def both(self):
+        @pl.when(self.place < self.seq // 2)
+        def _():
+            self.hop(0)
+            self.hop(1)
+
+        @pl.when(self.place >= self.seq // 2)
+        def _():
+            self.hop(1)
+            self.hop(0)
+
+    def drain(self):
+        for way, last in ((0, self.seq - 1), (1, 0)):
+
+            @pl.when(self.place != last)
+            def _(way=way):
+                self.copy(way).wait_send()
 
 
 def flip(place, mask):
@@ -595,92 +526,6 @@
     return masks
 
 
-def gather_kernel(size, count, *refs):
-    sources, outs, (local_sem, send, recv) = refs[:count], refs[count : 2 * count], refs[2 * count :]
-    me, place = lax.axis_index("rows"), lax.axis_index("seq")
-    greet([(place, flip(me, 1 << k)) for k in range(size.bit_length() - 1)])
-    started = []
-    kept = []
-    for i in range(count):
-        copy = pltpu.make_async_copy(sources[i], outs[i].at[me], local_sem.at[i])
-        copy.start()
-        kept.append(copy)
-
-    def cut(i, h, ref):
-        width = outs[i].shape[-1] // 2
-        return ref.at[:, pl.ds(h * width, width)]
-
-    def slot(i, h, m):
-        return (i, h, m)
-
-    def push(i, h, m, bit):
-        source = sources[i] if m == 0 else outs[i].at[flip(me, m)]
-        key = slot(i, h, m | bit)
-        started.append(
-            remote(
-                cut(i, h, source), cut(i, h, outs[i].at[flip(me, m)]), send.at[key], recv.at[key],
-                (place, flip(me, bit)),
-            )
-        )
-
-    def arrived(i, h, m):
-        key = slot(i, h, m)
-        block = cut(i, h, outs[i].at[flip(me, m)])
-        pltpu.make_async_remote_copy(
-            src_ref=block, dst_ref=block, send_sem=send.at[key], recv_sem=recv.at[key],
-            device_id=(place, flip(me, 1)), device_id_type=MESH,
-        ).wait_recv()
-
-    orders = [order[1:] + order[:1] for order in bit_orders(size)]
-    steps = len(orders[0])
-    for i in range(count):
-        for h in range(2):
-            push(i, h, 0, orders[h][0])
-    for i in range(count):
-        for h in range(2):
-            push(i, h, 0, 1)
-    for i in range(count):
-        for k in range(1, steps):
-            for h in range(2):
-                order = orders[h]
-                old = masks_of(order[: k - 1])
-                if k < steps - 1:
-                    for m in old:
-                        push(i, h, m, order[k])
-                for m in old:
-                    fresh = m | order[k - 1]
-                    arrived(i, h, fresh)
-                    if k < steps - 1:
-                        push(i, h, fresh, order[k])
-                    push(i, h, fresh, 1)
-    for i in range(count):
-        for h in range(2):
-            for m in masks_of(orders[h][:-1]):
-                arrived(i, h, m | 1)
-    for copy in started:
-        copy.wait_send()
-    for copy in kept:
-        copy.wait()
-
-
-def gather_rows(arrays, size):
-    count = len(arrays)
-    away = pl.BlockSpec(memory_space=pl.ANY)
-    return pl.pallas_call(
-        functools.partial(gather_kernel, size, count),
-        in_specs=[away] * count,
-        out_specs=[away] * count,
-        out_shape=[jax.ShapeDtypeStruct((size,) + v.shape, v.dtype) for v in arrays],
-        scratch_shapes=[
-            pltpu.SemaphoreType.DMA((count,)),
-            pltpu.SemaphoreType.DMA((count, 2, size)),
-            pltpu.SemaphoreType.DMA((count, 2, size)),
-        ],
-        compiler_params=pltpu.CompilerParams(collective_id=3, has_side_effects=True),
-        name="gather_rows",
-    )(*arrays)
-
-
 def by_tiles(rows, tile, body):
     def step(i, none):
         body(pl.ds(pl.multiple_of(i * tile, tile), tile))
@@ -691,6 +536,18 @@
 
 def wait_for(ref, sem):
     pltpu.make_async_copy(ref, ref, sem).wait()
+
+
+def greet_seq(seq):
+    me, place = lax.axis_index("rows"), lax.axis_index("seq")
+    barrier = pltpu.get_barrier_semaphore()
+    for step, there in ((-1, place > 0), (1, place < seq - 1)):
+
+        @pl.when(there)
+        def _(step=step):
+            pl.semaphore_signal(barrier, inc=1, device_id=(place + step, me), device_id_type=MESH)
+
+    pl.semaphore_wait(barrier, (place > 0).astype(jnp.int32) + (place < seq - 1).astype(jnp.int32))
 
 
 def greet_rows_and_seq(size, seq):
@@ -706,6 +563,342 @@
 
     near = (place > 0).astype(jnp.int32) + (place < seq - 1).astype(jnp.int32)
     pl.semaphore_wait(barrier, near + size - 1)
+
+
+def crossed(place, mask, size):
+    out = 0
+    for k in range(size.bit_length() - 1):
+        bit = 1 << k
+        out = out + bit * lax.rem(lax.div(place, bit) + lax.div(mask, bit), 2)
+    return out
+
+
+class RowGather:
+    def __init__(self, size, source, out, own_sem, send, recv):
+        self.size, self.source, self.out, self.own_sem, self.send, self.recv = size, source, out, own_sem, send, recv
+        self.me, self.place = lax.axis_index("rows"), lax.axis_index("seq")
+        self.rows = source.shape[0] // 2
+        self.orders = [order[1:] for order in bit_orders(size)]
+        self.steps = len(self.orders[0])
+        self.started = []
+
+    @staticmethod
+    def sems(size):
+        return [pltpu.SemaphoreType.DMA((1,))] + [pltpu.SemaphoreType.DMA((2, size))] * 2
+
+    def half(self, h, m, ref=None):
+        ref = self.out.at[flip(self.me, m)] if ref is None else ref
+        return ref.at[pl.ds(h * self.rows, self.rows), :]
+
+    def push(self, h, m, bit):
+        source = self.half(h, m, self.source if m == 0 else None)
+        key = (h, m | bit)
+        self.started.append(
+            remote(
+                source, self.half(h, m), self.send.at[key], self.recv.at[key],
+                (self.place, flip(self.me, bit)),
+            )
+        )
+
+    def arrived(self, h, m):
+        wait_for(self.half(h, m), self.recv.at[h, m])
+
+    def start(self):
+        pltpu.make_async_copy(self.source, self.out.at[self.me], self.own_sem.at[0]).start()
+        for h in range(2):
+            self.push(h, 0, self.orders[h][0])
+        for h in range(2):
+            self.push(h, 0, 1)
+
+    def own(self):
+        wait_for(self.out.at[self.me], self.own_sem.at[0])
+
+    def step(self, k, use=None):
+        for h in range(2):
+            order = self.orders[h]
+            old = masks_of(order[:k])
+            if k + 1 < self.steps:
+                for m in old:
+                    self.push(h, m, order[k + 1])
+            for m in old:
+                fresh = m | order[k]
+                self.arrived(h, fresh)
+                if k + 1 < self.steps:
+                    self.push(h, fresh, order[k + 1])
+                self.push(h, fresh, 1)
+                if use:
+                    use(h, fresh)
+
+    def paired(self, use=None):
+        for m in masks_of(self.orders[0]):
+            for h in range(2):
+                self.arrived(h, m | 1)
+                if use:
+                    use(h, m | 1)
+
+    def drain(self):
+        for copy in self.started:
+            copy.wait_send()
+
+
+def front_kernel(size, seq, direct, *refs):
+    (tokens, cot, notes, w_local, out_w, x_w, dt_w, taps_ref, bias_ref, dt_bias_ref) = refs[:10]
+    (
+        normed_out, cot_out, w_out, x_out, delta_out, gy_out, pre_out, gate_out, gg_out, cext_out,
+        proj_ref, rank_ref, all_notes,
+    ) = refs[10:23]
+    (
+        tok, normed, cot_s, wc, wg, cext, pre, xb, x_s, delta_s, gy_s, gate_s, gg_s, gain_ref,
+    ) = refs[23:37]
+    token_sems, cot_sems = refs[37:40], refs[40:43]
+    part, near, total, mail, far, out, sems = refs[43:50]
+    note_send, note_recv, wc_send, wc_recv, wg_send, wg_recv, halo_send, halo_recv, out_sems = refs[50:]
+    me, parity, partner, others = row_peers(size)
+    place = lax.axis_index("seq")
+    tt, width = tokens.shape
+    share, el = wc.shape[1:]
+    blocks = el // LANES
+    half = size // 2
+    f32, bf16 = jnp.float32, jnp.bfloat16
+    tile = 32
+    stores = []
+
+    def put(source, target):
+        copy = pltpu.make_async_copy(source, target, out_sems.at[len(stores)])
+        copy.start()
+        stores.append(copy)
+
+    def piece(q, gate):
+        if direct:
+            at = pl.multiple_of(q * el, LANES) + gate * size * el
+            return w_local.at[:, pl.ds(at, el)]
+        return w_local.at[q, :, pl.ds(gate * el, el)]
+
+    def swap(gate, target, send, recv):
+        copies = []
+        for m in range(1, size):
+            q = flip(me, m)
+            copies.append(remote(piece(q, gate), target.at[me], send.at[m], recv.at[m], (place, q)))
+        pltpu.make_async_copy(piece(me, gate), target.at[me], recv.at[0]).start()
+        return copies
+
+    def swapped(target, recv):
+        for m in range(size):
+            wait_for(target.at[flip(me, m)], recv.at[m])
+
+    greet_rows_and_seq(size, seq)
+
+    sent = []
+    for m in range(1, size):
+        sent.append(remote(notes, all_notes.at[me], note_send.at[m], note_recv.at[m], (place, flip(me, m))))
+    pltpu.make_async_copy(notes, all_notes.at[me], note_recv.at[0]).start()
+    token_rows = RowGather(size, tokens, tok, *token_sems)
+    cot_rows = RowGather(size, cot, cot_s, *cot_sems)
+    token_rows.start()
+    sent += swap(0, wc, wc_send, wc_recv)
+
+    for m in range(size):
+        wait_for(all_notes.at[flip(me, m)], note_recv.at[m])
+    for p in range(size):
+        gain_ref[:, p * share : (p + 1) * share] = all_notes[p, 0:1, :share].astype(f32)
+
+    def norm(p, base, rows):
+        def body(span):
+            there = pl.ds(base + span.start, span.size)
+            x = tok[p, there, :].astype(f32)
+            inv = lax.rsqrt(jnp.mean(x * x, axis=1, keepdims=True) + epsilon)
+            normed[p, there, :] = (x * inv * gain_ref[...]).astype(bf16)
+
+        by_tiles(rows, 16, body)
+
+    def norm_half(h, m):
+        norm(flip(me, m), h * (tt // 2), tt // 2)
+
+    token_rows.own()
+    norm(me, 0, tt)
+    for k in range(token_rows.steps):
+        token_rows.step(k, norm_half)
+    cot_rows.start()
+    sent += swap(1, wg, wg_send, wg_recv)
+    token_rows.paired(norm_half)
+    swapped(wc, wc_recv)
+
+    @pl.when(place == 0)
+    def _():
+        cext[:, 0:16, :] = jnp.zeros((size, 16, el), bf16)
+
+    def halo(p, i):
+        there = cext.at[p, pl.ds(0, 16), :]
+        return pltpu.make_async_remote_copy(
+            src_ref=cext.at[p, pl.ds(tt, 16), :], dst_ref=there, send_sem=halo_send.at[i],
+            recv_sem=halo_recv.at[i], device_id=(jnp.minimum(place + 1, seq - 1), me), device_id_type=MESH,
+        )
+
+    def block_at(i):
+        return 2 * lax.rem(me // 2 + lax.rem(i, half), half) + lax.rem(parity + 1 + lax.div(i, half), 2)
+
+    def mix(i, none):
+        p = block_at(i)
+        weight = wc[...].reshape(size * share, el)
+        cext[p, 16:, :] = jnp.dot(normed[p], weight, preferred_element_type=f32).astype(bf16)
+
+        @pl.when(place < seq - 1)
+        def _():
+            halo(p, i).start()
+
+        return none
+
+    lax.fori_loop(0, size, mix, 0)
+    for p in range(size):
+        put(normed.at[p], normed_out.at[p])
+
+    def conv(i, none):
+        p = block_at(i)
+
+        @pl.when(place > 0)
+        def _():
+            halo(p, i).wait_recv()
+
+        def body(span):
+            ext = cext[p, pl.ds(span.start, tile + 16), :].astype(f32)
+            value = bias_ref[...]
+            for k in range(KC):
+                value = value + taps_ref[k : k + 1, :] * ext[16 - KC + 1 + k : 16 - KC + 1 + k + tile]
+            pre[p, span, :] = value
+            x = (value / (1.0 + jnp.exp(-value))).astype(bf16)
+            xb[p, span, :] = x
+            for b in range(blocks):
+                there = pl.ds(p + span.start * size, tile, stride=size)
+                x_s[b, there, :] = x[:, b * LANES : (b + 1) * LANES].astype(f32)
+
+        by_tiles(tt, tile, body)
+        value = jnp.dot(xb[p], x_w[...], preferred_element_type=f32)
+
+        @pl.when(i < half)
+        def _():
+            part[p] = value.astype(bf16)
+            pltpu.make_async_remote_copy(
+                src_ref=part.at[p], dst_ref=near.at[lax.div(p, 2)], send_sem=sems.at[0, lax.div(p, 2)],
+                recv_sem=sems.at[1, lax.div(p, 2)], device_id=(place, partner), device_id_type=MESH,
+            ).start()
+
+        @pl.when(i >= half)
+        def _():
+            total[lax.div(p, 2)] = value
+
+        return none
+
+    lax.fori_loop(0, size, conv, 0)
+    put(cext, cext_out)
+    put(pre, pre_out)
+    put(x_s, x_out)
+
+    def use(p):
+        block = out[p]
+        rank_ref[p] = block
+        proj_ref[pl.ds(p, tt, stride=size), :] = block.astype(f32)
+
+        def body(span):
+            step = jnp.dot(out[p, span, :], dt_w[...], preferred_element_type=f32) + dt_bias_ref[...]
+            delta = jnp.maximum(step, 0.0) + jnp.log1p(jnp.exp(-jnp.abs(step)))
+            for b in range(blocks):
+                there = pl.ds(p + span.start * size, 64, stride=size)
+                delta_s[b, there, :] = delta[:, b * LANES : (b + 1) * LANES]
+
+        by_tiles(tt, 64, body)
+
+    def between():
+        for k in range(cot_rows.steps):
+            cot_rows.step(k)
+
+    exchange_sums(size, near, total, mail, far, out, sems, use, between)
+    for j in range(half):
+        pltpu.make_async_remote_copy(
+            src_ref=part.at[j], dst_ref=near.at[j], send_sem=sems.at[0, j], recv_sem=sems.at[1, j],
+            device_id=(place, partner), device_id_type=MESH,
+        ).wait_send()
+    put(delta_s, delta_out)
+    put(wc, w_out.at[:, :, pl.ds(0, el)])
+
+    cot_rows.own()
+    cot_rows.paired()
+    put(cot_s, cot_out)
+    swapped(wg, wg_recv)
+    put(wg, w_out.at[:, :, pl.ds(el, el)])
+
+    def gates(p, none):
+        weight = wg[...].reshape(size * share, el)
+        gate_s[p] = jnp.dot(normed[p], weight, preferred_element_type=f32)
+        gg_s[p] = lax.dot_general(
+            cot_s[p], out_w[...], (((1,), (1,)), ((), ())), preferred_element_type=f32
+        )
+
+        def body(span):
+            gate = gate_s[p, span, :]
+            gy = gg_s[p, span, :] * gate / (1.0 + jnp.exp(-gate))
+            for b in range(blocks):
+                there = pl.ds(p + span.start * size, tile, stride=size)
+                gy_s[b, there, :] = gy[:, b * LANES : (b + 1) * LANES]
+
+        by_tiles(tt, tile, body)
+        return none
+
+    lax.fori_loop(0, size, gates, 0)
+    put(gy_s, gy_out)
+    put(gate_s, gate_out)
+    put(gg_s, gg_out)
+
+    for i in range(size):
+
+        @pl.when(place < seq - 1)
+        def _(i=i):
+            halo(i, i).wait_send()
+
+    token_rows.drain()
+    cot_rows.drain()
+    for copy in sent:
+        copy.wait_send()
+    for copy in stores:
+        copy.wait()
+
+
+def front(tokens, cot, notes, w_local, out_w, x_w, dt_w, taps, bias, dt_bias, size, seq, direct):
+    tt, width = tokens.shape
+    el = out_w.shape[0]
+    share = width // size
+    blocks = el // LANES
+    away = pl.BlockSpec(memory_space=pl.ANY)
+    here = pl.BlockSpec(memory_space=pltpu.VMEM)
+    f32, bf16 = jnp.float32, jnp.bfloat16
+    rows, scan = (size, tt, width), (blocks, tt * size, LANES)
+    channels, ext = (size, tt, el), (size, tt + 16, el)
+    shapes = [
+        (rows, bf16), (rows, bf16), ((size, share, 2 * el), bf16), (scan, f32), (scan, f32), (scan, f32),
+        (channels, f32), (channels, f32), (channels, f32), (ext, bf16),
+        ((tt * size, LANES), f32), ((size, tt, LANES), bf16), ((size,) + notes.shape, bf16),
+    ]
+    weights = (size, share, el)
+    scratch = [
+        (rows, bf16), (rows, bf16), (rows, bf16), (weights, bf16), (weights, bf16), (ext, bf16),
+        (channels, f32), (channels, bf16), (scan, f32), (scan, f32), (scan, f32),
+        (channels, f32), (channels, f32), ((1, width), f32),
+    ]
+    one = pltpu.SemaphoreType.DMA((size,))
+    return pl.pallas_call(
+        functools.partial(front_kernel, size, seq, direct),
+        in_specs=[away] * 4 + [here] * 6,
+        out_specs=[away] * 10 + [here] * 3,
+        out_shape=[jax.ShapeDtypeStruct(*v) for v in shapes],
+        scratch_shapes=[pltpu.VMEM(*v) for v in scratch]
+        + RowGather.sems(size) * 2
+        + sum_scratch(size, tt)
+        + [one] * 8
+        + [pltpu.SemaphoreType.DMA((size + 10,))],
+        compiler_params=pltpu.CompilerParams(
+            vmem_limit_bytes=62 * MIB, collective_id=0, has_side_effects=True
+        ),
+        name="front",
+    )(tokens, cot, notes, w_local, out_w, x_w, dt_w, taps, bias, dt_bias)
 
 
 class RowScatter:
@@ -999,57 +1192,58 @@
     count = nr * tt
     assert rd == 1 and ITEM % tt == 0 and nr % 8 == 0
 
-    w_in = lax.all_to_all(
-        in_proj.reshape(D // size, 2, size, el), "rows", split_axis=2, concat_axis=0, tiled=True
-    ).reshape(D, 2 * el)
+    elp = pad_lanes(el)
     share = D // size
-    notes = jnp.zeros((16, -(-share // 256) * 256), jnp.bfloat16)
-    notes = notes.at[0, :share].set(norm_gain).at[1, 0].set(1.0 - resets[0, 0].astype(jnp.bfloat16))
-    all_tokens, all_cot, all_notes = gather_rows([tokens[0], cotangent[0], notes], size)
-    all_tokens, all_cot = all_tokens.reshape(count, D), all_cot.reshape(count, D)
-    gain = all_notes[:, 0, :share].reshape(D).astype(jnp.float32)
-    alive = all_notes[:, 1, :1].astype(jnp.float32)
-
-    flat = all_tokens.astype(jnp.float32)
-    inv_all = lax.rsqrt(jnp.mean(flat * flat, axis=1, keepdims=True) + epsilon)
-    normed = (flat * inv_all * gain).astype(jnp.bfloat16)
-    mixed = jnp.dot(normed, w_in, preferred_element_type=jnp.float32)
-    conv_in = mixed[:, :el].astype(jnp.bfloat16).reshape(nr, tt, el)
-    gate_pre = mixed[:, el:]
-    left_rim = from_behind(conv_in[:, tt - (KC - 1) :], "seq", 1)
-    extended = jnp.concatenate([left_rim, conv_in], axis=1)
-    taps = conv_weight.astype(jnp.float32)
-    conv_pre = conv_bias.astype(jnp.float32) + sum(
-        taps[k] * extended[:, k : k + tt].astype(jnp.float32) for k in range(KC)
+    direct = elp == el
+    f32, bf16 = jnp.float32, jnp.bfloat16
+
+    def widen(value, axis):
+        pad = [(0, 0)] * value.ndim
+        pad[axis] = (0, elp - el)
+        return jnp.pad(value, pad)
+
+    if direct:
+        w_local = in_proj
+    else:
+        w_local = jnp.moveaxis(in_proj.reshape(share, 2, size, el), 2, 0)
+        w_local = widen(w_local, 3).reshape(size, share, 2 * elp)
+    out_proj, x_proj = widen(out_proj, 0), widen(x_proj, 0)
+    dt_pad = widen(jnp.pad(dt_proj, ((0, LANES - R), (0, 0))), 1)
+    taps = widen(conv_weight.astype(f32), 1)
+    bias = widen(conv_bias.astype(f32), 0)[None]
+    rate = widen(-jnp.exp(a_log.astype(f32)), 1)
+    notes = jnp.zeros((16, -(-share // 256) * 256), bf16)
+    notes = notes.at[0, :share].set(norm_gain).at[1, 0].set(1.0 - resets[0, 0].astype(bf16))
+    (
+        normed, all_cot, w_in, x_t, delta_t, gy_t, conv_pre, gate_pre, grad_gated, conv_ext, proj_t, rank_all,
+        all_notes,
+    ) = front(
+        tokens[0], cotangent[0], notes, w_local, out_proj, x_proj, dt_pad, taps, bias,
+        widen(dt_bias.astype(f32), 0)[None], size, seq, direct,
     )
-    conv_out = jax.nn.silu(conv_pre).astype(jnp.bfloat16).reshape(count, el)
-    dt_pad = jnp.pad(dt_proj, ((0, LANES - R), (0, 0)))
-    proj_t, step_size, rank_all = project(
-        conv_out.reshape(nr, tt, el), x_proj, dt_pad, dt_bias.astype(jnp.float32)[None]
-    )
-    step_size = step_size.reshape(count, el)
+    normed, all_cot = normed.reshape(count, D), all_cot.reshape(count, D)
+    w_in = w_in.reshape(D, 2 * elp)
+    gate_pre, grad_gated = gate_pre.reshape(count, elp), grad_gated.reshape(count, elp)
+    gain = all_notes[:, 0, :share].reshape(D).astype(f32)
+    alive = all_notes[:, 1, :1].astype(f32)
     rank_part = rank_all.reshape(count, LANES)[:, :R]
-    decay_rate = -jnp.exp(a_log.astype(jnp.float32))
-    rate2 = decay_rate * LOG2E
-    conv_float = conv_out.astype(jnp.float32)
-
-    grad_gated = contract_cols(all_cot, out_proj)
-    gate_sig = jax.nn.sigmoid(gate_pre)
-    gate_act = gate_pre * gate_sig
-    grad_y = grad_gated * gate_act
-
-    wide = -(-el // LANES) * LANES
-    extra = [(0, 0), (0, wide - el)]
-    scanned = [jnp.pad(v, extra) for v in (step_size, conv_float, grad_y)]
-    rate2 = jnp.pad(rate2, extra)
-    ends = scan_ends(*scanned, proj_t, rate2, nr, tt)
-    carry = exchange_carry(ends, alive, seq)
+    extended = conv_ext[:, 16 - KC + 1 :]
+
+    def by_row(value):
+        value = value.reshape(elp // LANES, tt, nr, LANES)
+        return jnp.transpose(value, (2, 1, 0, 3)).reshape(count, elp)
+
+    rate2 = rate * LOG2E
+    scanned = (delta_t, x_t, gy_t)
+    carry = scan_ends(*scanned, proj_t, rate2, alive, nr, tt, seq)
     scan_y, grad_delta, grad_input, grad_bc, grate = scan_main(
         *scanned, proj_t, rate2, carry, nr, tt
     )
-    scan_y, grad_delta, grad_input = scan_y[:, :el], grad_delta[:, :el], grad_input[:, :el]
-    grate = grate[:, :, :el]
-    grad_a_log = jnp.sum(grate, axis=1) * decay_rate
+    scan_y, grad_delta, grad_input, step_size = (by_row(v) for v in (scan_y, grad_delta, grad_input, delta_t))
+    conv_out = jax.nn.silu(conv_pre).astype(bf16).reshape(count, elp)
+    gate_sig = jax.nn.sigmoid(gate_pre)
+    gate_act = gate_pre * gate_sig
+    grad_a_log = jnp.sum(grate, axis=1) * rate
 
     gated = (scan_y * gate_act).astype(jnp.bfloat16)
     branch = jnp.dot(gated, out_proj, preferred_element_type=jnp.float32).astype(jnp.bfloat16)
@@ -1060,12 +1254,12 @@
     grad_dt_bias = jnp.sum(grad_step_pre, axis=0)
     low_step = grad_step_pre.astype(jnp.bfloat16)
     grad_dt_proj = contract_rows(rank_part, low_step)
-    grad_projected = back_project(low_step.reshape(nr, tt, el), dt_pad, grad_bc).reshape(count, LANES)
+    grad_projected = back_project(low_step.reshape(nr, tt, elp), dt_pad, grad_bc).reshape(count, LANES)
     grad_x_proj = contract_rows(conv_out, grad_projected)
     grad_conv_out = contract_cols(grad_projected, x_proj) + grad_input
-    conv_sig = jax.nn.sigmoid(conv_pre).reshape(count, el)
-    conv_flat = conv_pre.reshape(count, el)
-    grad_conv_pre = (grad_conv_out * conv_sig * (1.0 + conv_flat * (1.0 - conv_sig))).reshape(nr, tt, el)
+    conv_sig = jax.nn.sigmoid(conv_pre).reshape(count, elp)
+    conv_flat = conv_pre.reshape(count, elp)
+    grad_conv_pre = (grad_conv_out * conv_sig * (1.0 + conv_flat * (1.0 - conv_sig))).reshape(nr, tt, elp)
     grad_conv_bias = jnp.sum(grad_conv_pre, axis=(0, 1))
     grad_taps = jnp.stack(
         [
@@ -1080,7 +1274,7 @@
     grad_conv_in = grad_ext[:, KC - 1 :] + jnp.pad(
         right_rim.astype(jnp.float32), ((0, 0), (tt - (KC - 1), 0), (0, 0))
     )
-    grad_mixed = jnp.concatenate([grad_conv_in.reshape(count, el), grad_gate_pre], axis=1).astype(
+    grad_mixed = jnp.concatenate([grad_conv_in.reshape(count, elp), grad_gate_pre], axis=1).astype(
         jnp.bfloat16
     )
     grad_in_proj = contract_rows(normed, grad_mixed).astype(jnp.bfloat16)
@@ -1089,7 +1283,7 @@
         [grad_x_proj.T, grad_dt_proj, grad_taps, grad_conv_bias[None], grad_dt_bias[None], grad_a_log],
         axis=0,
     )
-    piece = (share // 2, 2 * el)
+    piece = (share // 2, 2 * elp)
     folded = shortened(small)
     folded = jnp.pad(folded, ((0, -folded.shape[0] % 2), (0, 0)))
     high = folded.shape[0] // 2
@@ -1097,15 +1291,15 @@
     folded = jnp.pad(folded, ((0, -high % piece[0]), (0, 0)))
     branch_own, grad_normed, summed = reduce_all(
         branch.reshape(nr, tt, D), grad_normed_part.reshape(nr, tt, D),
-        grad_in_proj.reshape(size, share, 2 * el), shortened(grad_out_proj), folded, size, seq,
+        grad_in_proj.reshape(size, share, 2 * elp), shortened(grad_out_proj)[:el], folded, size, seq,
     )
     summed = summed.astype(jnp.float32)
     out_rows, out_cols = el // piece[0], D // piece[1]
     at = out_rows * out_cols
     sum_out = jnp.swapaxes(summed[:at].reshape(out_rows, out_cols, *piece), 1, 2).reshape(el, D)
     folded = summed[at : at + folded.shape[0] // piece[0]].reshape(folded.shape)
-    small = jnp.concatenate([folded[:high, :el], folded[:high, el:]], axis=0)
-    blocks = summed[-2 * size :].reshape(size, share, 2, el)
+    small = jnp.concatenate([folded[:high, :elp], folded[:high, elp:]], axis=0)[:, :el]
+    blocks = summed[-2 * size :].reshape(size, share, 2, elp)[..., :el]
     me = lax.axis_index("rows")
     places = [chunk_order(size).index(m) for m in range(size)]
     order = jnp.array(places)[jnp.array(range(size)) ^ me]

time: 544 us -> 539 us (level)
  local copies, waits for them, and re-layouts: 52.8 us -> 86.2 us
  matrix products: 43.5 us -> 31.7 us
  starting transfers between devices: 10.9 us -> 1.28 us
  Pallas kernels: 385 us -> 379 us
    pallas_call x1, Pallas kernels: 90.8 us -> 69.5 us  [scan_main(): pl.pallas_call(functools.partial(main_kernel, nr, tt, ct, min(8, ct)), in...]
    pallas_call x4 -> x2, Pallas kernels: 150 us -> 164 us  [the longest x1 120 us: front(): pl.pallas_call(functools.partial(front_kernel, size, seq, direct), in_spe...]
    reshape x2 -> x5, local copies, waits for them, and re-layouts: 9.95 us -> 22 us  [the longest x2 7.84 us: by_row(): return jnp.transpose(value, (2, 1, 0, 3)).reshape(count, elp)]
    dot_general x1 -> x0, matrix products: 8.22 us -> none  [local(): mixed = jnp.dot(normed, w_in, preferred_element_type=jnp.float32)]
    mul x1 -> x2, other arithmetic: 0.62 us -> 7.05 us  [the longest x1 5.72 us: local(): grad_step_pre = grad_delta * -jnp.expm1(-step_size)]
    convert_element_type x8 -> x4, other arithmetic: 12.8 us -> 7.23 us  [the longest x1 3.85 us: local(): gated = (scan_y * gate_act).astype(jnp.bfloat16)]
    dot_general x3 -> x2, matrix products: 16 us -> 10.8 us  [contract_cols(): lax.dot_general(left, right, (((1,), (1,)), ((), ())), preferred_element_...]
    unnamed x94 -> x73, local copies, waits for them, and re-layouts: 17 us -> 18 us
  transfers between devices with their start and end apart: 3 -> 1, of which waited for: 1 -> 0; matrix products, arithmetic and copies ran while one was open for 4% -> 9% of each run, Pallas kernels for 16% -> 0%
where the time goes in v2:
time: 539 us; the launch traced here: 533 us
  Pallas kernels  379 us (70%)
  local copies, waits for them, and re-layouts  86.2 us (16%)
  other arithmetic  32.9 us (6%)
  matrix products  31.7 us (6%)
    pallas_call x1, Pallas kernels, reduce_all(): pl.pallas_call(functools.partial(tail_kernel, size, seq), in_specs=[away]...  132 us
    pallas_call x1, Pallas kernels, front(): pl.pallas_call(functools.partial(front_kernel, size, seq, direct), in_spe...  120 us
    pallas_call x1, Pallas kernels, scan_main(): pl.pallas_call(functools.partial(main_kernel, nr, tt, ct, min(8, ct)), in...  69.5 us
    pallas_call x1, Pallas kernels, scan_ends(): pl.pallas_call(functools.partial(ends_kernel, seq, nr, tt, ct, min(8, ct)...  43.5 us
    unnamed x73, local copies, waits for them, and re-layouts  18 us
    dot_general x4, matrix products, contract_rows(): lax.dot_general(left, right, (((0,), (0,)), ((), ())), preferred_element_...  15.6 us
    pallas_call x1, Pallas kernels, back_project(): pl.pallas_call(functools.partial(back_project_kernel, size), in_specs=[he...  13.9 us
    dot_general x2, matrix products, contract_cols(): lax.dot_general(left, right, (((1,), (1,)), ((), ())), preferred_element_...  10.8 us
  transfers between devices with their start and end apart: 1, of which 0 were waited for; matrix products, arithmetic and copies ran while one was open for 9% of the time, Pallas kernels for 0%

profile of v2, /device:TPU:0, one launch (start us, length us, event | category | flops | bytes accessed | tf_op | source)
XLA Modules:
  0.0 533.0 jit_solution(7032740165464840450)
XLA Ops:
  0.6 1.2 slice.160
  2.5 0.7 reshape.260
  3.1 1.2 reshape.286.refs_8_
  4.4 1.2 reshape.287.refs_9_
  5.6 0.7 convert_element_type.113.refs_7_
  6.3 1.3 fusion.28.a_ref
  7.7 1.5 pad.40.refs_6_.dt_ref
  9.8 120.5 %front.1 = (bf16[8,256,1536]{2,1,0:T(8,128)(2,1)}, bf16[8,256,1536]{2,1,0:T(8,128)(2,1)}, bf16[8,192,768]{2,1,0:T(8,128)(2,1)}, f32[3,2048,128]{2,1,0:T(8,128)},...) custom-call(bf16[256,1536]{1,0:T(8,128)(2,1)} %bitcast.156, ...), custom_call_target="tpu_custom_call" | custom-call | tf_op jit(solution)/shard_map/front/pallas_call | solution.py:887
  130.3 1.3 slice_convert_fusion.1
  131.6 43.5 %scan_ends.1.carry_ref = f32[2,16,8,384]{3,2,1,0:T(8,128)} custom-call(f32[3,2048,128]{2,1,0:T(8,128)} %get-tuple-element.56.delta_in, f32[3,2048,128]{2,1,0:T(8,128)} %get-tuple-element.57.x_in, f32[3,2048,128]{2,1,0:T(8,128)} %get-tuple-element.58.gy_in, f32[2048,128]{1,0:T(8,128)} %get-tuple-element.59.proj_ref, f32[16,384]{1,0:T(8,128)} %fusion.28.a_ref, ...), custom_call_target="tpu_custom_call" | custom-call | tf_op jit(solution)/shard_map/scan_ends/pallas_call | solution.py:109
  175.2 69.5 %scan_main.1 = (f32[3,2048,128]{2,1,0:T(8,128)}, f32[3,2048,128]{2,1,0:T(8,128)}, f32[3,2048,128]{2,1,0:T(8,128)}, f32[2048,128]{1,0:T(8,128)}, f32[16,8,384]{2,1,0:T(8,128)}) custom-call(f32[3,2048,128]{2,1,0:T(8,128)} %get-tuple-element.56.delta_in, f32[3,2048,128]{2,1,0:T(8,128)} %get-tuple-element.57.x_in, f32[3,2048,128]{2,1,0:T(8,128)} %get-tuple-element.58.gy_in, ...), custom_call_target="tpu_custom_call" | custom-call | tf_op jit(solution)/shard_map/scan_main/pallas_call | solution.py:284
  244.6 5.7 %multiply_bitcast_fusion = f32[3,256,8,128]{3,2,1,0:T(8,128)} fusion(f32[3,2048,128]{2,1,0:T(8,128)} %get-tuple-element.63, f32[3,2048,128]{2,1,0:T(8,128)} %get-tuple-element.56.delta_in), kind=kLoop, calls=%fused_computation.32 | loop fusion | flops 2359296 | bytes 9437184 | tf_op jit(solution)/shard_map/mul | solution.py:1253
  250.4 2.4 copy.39
  252.8 1.5 bitcast_convert_fusion
  254.3 0.7 copy-done.2
  254.9 1.9 copy.40.low_ref
  256.8 3.7 copy.41
  260.5 5.1 copy.56
  265.5 3.6 copy.42
  269.2 2.9 add_divide_fusion
  272.1 13.9 %back_project.1 = bf16[8,256,128]{2,1,0:T(8,128)(2,1)S(1)} custom-call(bf16[8,256,384]{2,1,0:T(8,128)(2,1)S(1)} %copy.40.low_ref, bf16[128,384]{1,0:T(8,128)(2,1)S(1)} %copy-done.1, f32[2048,128]{1,0:T(8,128)S(1)} %copy-done), custom_call_target="tpu_custom_call" | custom-call | tf_op jit(solution)/shard_map/back_project/pallas_call | solution.py:432
  286.1 3.7 multiply_reduce_fusion.1
  289.8 1.4 broadcast_multiply_fusion.3
  291.5 1.0 pad_add_fusion
  292.5 0.6 slice.198
  293.1 1.3 collective-permute-start
  294.4 1.4 convert_reduce_fusion
  296.0 1.1 fusion.22
  297.4 2.0 copy.47
  299.4 0.6 gather_fusion
  300.6 2.2 reduce_sum.94
  302.8 1.0 reduce_sum.96
  303.8 3.1 copy.58
  307.0 3.6 copy.36
  310.6 3.5 copy.44
  314.1 3.8 fusion.11
  318.0 0.9 copy.45
  318.9 1.7 copy.57
  322.8 1.2 convolution_convert_fusion.4
  324.0 1.9 concatenate.19
  326.0 4.2 copy.53
  330.2 2.7 fusion.3
  332.9 5.3 convolution_convert_fusion.1
  338.2 3.6 convolution_convert_fusion.3.refs_3_
  341.8 0.7 fusion.26.refs_4_
  342.6 1.2 fusion.4
  344.1 9.6 %convolution_convert_fusion.2 = bf16[1536,768]{1,0:T(8,128)(2,1)} fusion(bf16[2048,1536]{1,0:T(8,128)(2,1)} %bitcast.179, bf16[2048,384]{1,0:T(8,128)(2,1)S(1)} %copy-done.18, bf16[2048,384]{1,0:T(8,128)(2,1)S(1)} %bitcast.172), kind=kOutput, calls=%fused_computation.5 | convolution fusion | flops 4839309312 | bytes 11796480 | tf_op jit(solution)/shard_map/dot_general | solution.py:1176
  353.7 7.1 %convolution_convert_fusion = bf16[2048,1536]{1,0:T(8,128)(2,1)} fusion(bf16[1536,768]{1,0:T(8,128)(2,1)S(1)} %bitcast.183, bf16[2048,384]{1,0:T(8,128)(2,1)S(1)} %copy-done.18, bf16[2048,384]{1,0:T(8,128)(2,1)S(1)} %bitcast.173), kind=kOutput, calls=%fused_computation.2 | convolution fusion | flops 4841275392 | bytes 11796480 | tf_op jit(solution)/shard_map/dot_general | solution.py:1180
  360.8 131.6 %reduce_all.1 = (bf16[256,1536]{1,0:T(8,128)(2,1)}, bf16[256,1536]{1,0:T(8,128)(2,1)}, bf16[26,96,768]{2,1,0:T(8,128)(2,1)}) custom-call(bf16[8,256,1536]{2,1,0:T(8,128)(2,1)} %bitcast.160, bf16[8,256,1536]{2,1,0:T(8,128)(2,1)} %bitcast.161, bf16[8,192,768]{2,1,0:T(8,128)(2,1)} %bitcast.165, bf16[384,1536]{1,0:T(8,128)(2,1)} %convolution_convert_fusion.3.refs_3_, ...), custom_call_target="tpu_custom_call" | custom-call | tf_op jit(solution)/shard_map/reduce_all/pallas_call | solution.py:1149
  492.4 1.0 slice.171
  493.4 0.6 slice_reduce_fusion
  494.6 0.6 slice.178
  495.2 0.7 slice.174
  495.9 1.5 slice.179
  497.4 2.7 slice.170
  500.1 0.8 copy.50
  500.9 1.8 copy.49
  502.7 1.6 copy.61
  504.3 6.9 %reshape.281 = f32[8,192,2,384]{3,2,1,0:T(2,128)} reshape(f32[16,96,768]{2,1,0:T(8,128)} %slice.170) | data formatting | bytes 9437184 | tf_op jit(solution)/shard_map/reshape | solution.py:1302
  511.2 9.4 %gather_fusion.1 = f32[8,192,2,384]{3,2,1,0:T(2,128)} fusion(f32[8,192,2,384]{3,2,1,0:T(2,128)} %reshape.281, s32[1024]{0:T(1024)S(1)} %pad_clamp_fusion), kind=kCustom, calls=%fused_computation.1 | custom fusion | bytes 9437216 | tf_op jit(solution)/shard_map/gather | solution.py:1306
  520.6 5.1 copy.48
  525.7 1.8 copy.60
  528.1 1.8 copy-done.4
  531.1 1.7 fusion.18
  (91 shorter events, 7.1 us)
Async XLA Ops:
  6.3 2.9 copy-start.23
  9.2 0.6 copy-start.25
  252.8 2.2 copy-start.2
  269.2 2.9 copy-start
  269.2 2.9 copy-start.1
  269.2 16.9 %copy-start.14 = (f32[2048,384]{1,0:T(8,128)S(1)}, f32[2048,384]{1,0:T(8,128)}, u32[]{:S(2)}) copy-start(f32[2048,384]{1,0:T(8,128)} %copy.42) | copy-start | bytes 9437188
  269.2 16.9 %copy-start.30 = (bf16[8,272,384]{2,1,0:T(8,128)(2,1)S(1)}, bf16[8,272,384]{2,1,0:T(8,128)(2,1)}, u32[]{:S(2)}) copy-start(bf16[8,272,384]{2,1,0:T(8,128)(2,1)} %get-tuple-element.72) | copy-start | bytes 5013508
  272.1 14.0 %copy-start.13 = (f32[8,256,384]{2,1,0:T(8,128)S(1)}, f32[8,256,384]{2,1,0:T(8,128)}, u32[]{:S(2)}) copy-start(f32[8,256,384]{2,1,0:T(8,128)} %get-tuple-element.66) | copy-start | bytes 9437188
  272.1 14.0 %copy-start.22 = (bf16[384,128]{1,0:T(8,128)(2,1)S(1)}, bf16[384,128]{1,0:T(8,128)(2,1)}, u32[]{:S(2)}) copy-start(bf16[384,128]{1,0:T(8,128)(2,1)} %refs_5_.1) | copy-start | bytes 294916
  289.8 1.7 copy-start.7
  291.5 4.2 copy-start.3
  293.1 49.6 %collective-permute-start = (bf16[8,3,384]{2,1,0:T(4,128)(2,1)}, bf16[8,3,384]{2,1,0:T(4,128)(2,1)}, u32[]{:S(2)}, u32[]{:S(2)}) collective-permute-start(bf16[8,3,384]{2,1,0:T(4,128)(2,1)} %slice.198), channel_id=1, source_target_pairs={{8,0},{16,8},{24,16},{9,1},{17,9},{25,17},{10,2},{18,10},{26,18},{... | collective-permute-start | bytes 55304 | tf_op jit(solution)/shard_map/ppermute | solution.py:1168
  296.0 1.4 copy-start.6
  297.4 6.4 %copy-start.24 = (bf16[16,384]{1,0:T(8,128)(2,1)S(1)}, bf16[16,384]{1,0:T(8,128)(2,1)}, u32[]{:S(2)}) copy-start(bf16[16,384]{1,0:T(8,128)(2,1)} %param.27) | copy-start | bytes 36868
  317.9 4.8 copy-start.11
  318.0 4.8 copy-start.21
  325.9 4.2 copy-start.8
  325.9 4.2 copy-start.16
  330.2 2.7 copy-start.19
  330.2 8.0 %slice-start = ((s8[6291456]{0:T(1024)(128)(4,1)}), s8[4194304]{0:T(1024)(128)(4,1)S(1)}, s32[]{:S(2)}) async-start(s8[6291456]{0:T(1024)(128)(4,1)} %bitcast.180), calls=%async_computation | async-start | bytes 8388608
  332.9 5.3 copy-start.17
  332.9 5.3 slice-start.1
  338.2 4.4 copy-start.28
  338.2 4.4 copy-start.26
  342.6 1.4 copy-start.18
  344.1 9.6 %copy-start.29 = (bf16[8,192,768]{2,1,0:T(8,128)(2,1)S(1)}, bf16[8,192,768]{2,1,0:T(8,128)(2,1)}, u32[]{:S(2)}) copy-start(bf16[8,192,768]{2,1,0:T(8,128)(2,1)} %get-tuple-element.68) | copy-start | bytes 7077892
  493.4 4.0 copy-start.5
  525.7 1.8 copy-start.9
  527.5 2.4 copy-start.4
  527.5 2.4 copy-start.27
  527.5 2.9 copy-start.10
  527.5 2.9 copy-start.12
  527.5 3.4 copy-start.15
  527.6 3.5 copy-start.20

commit v3 on v2

--- a/solution.py
+++ b/solution.py
@@ -128,35 +128,29 @@
     )(delta, x, gy, proj, rate, alive)
 
 
-def main_kernel(
-    nr, tt, ct, uu,
-    delta_in, x_in, gy_in, proj_ref, a_ref, carry_ref,
-    y_out, gdelta_out, gx_out, gbc_ref, grate_ref,
-    sel, bc, hist, prod, state_ref, fold, delta_ref, x_ref, gy_ref, y_ref, gdelta_ref, gx_ref, sems, out_sems,
+def forward_kernel(
+    nr, tt, ct, uu, delta_in, x_in, proj_ref, a_ref, carry_ref,
+    y_out, hist_out, last_ref, sel, bc, hist, delta_ref, x_ref, y_ref, sems, out_sem, hist_sems,
 ):
     el = a_ref.shape[1]
     blocks = el // LANES
-    copies = copy_all((delta_in, x_in, gy_in), (delta_ref, x_ref, gy_ref), sems)
+    copies = copy_all((delta_in, x_in), (delta_ref, x_ref), sems)
     sel[...] = selector(LANES)
-    fold_row = lax.broadcasted_iota(jnp.int32, fold.shape, 0) // LANES
-    fold_col = lax.broadcasted_iota(jnp.int32, fold.shape, 1)
-    fold[...] = (fold_row + R == fold_col).astype(jnp.bfloat16)
-    state_ref[...] = carry_ref[0]
-
-    def enter(p):
-        return pl.ds(2 * p * nr, 2 * nr)
-
-    def keep(b, t, state):
-        for p in range(NS // 2):
-            both = jnp.concatenate([state[2 * p], state[2 * p + 1]], axis=0)
-            hist[b, t, enter(p), :] = both.astype(jnp.bfloat16)
-
-    for b in range(blocks):
-        keep(b, 0, [carry_ref[0, n, :, b * LANES : (b + 1) * LANES] for n in range(NS)])
+    last_ref[...] = carry_ref[0]
     for copy in copies:
         copy.wait()
 
+    def store(c):
+        slot = lax.rem(c, 2)
+        return pltpu.make_async_copy(hist.at[slot], hist_out.at[pl.ds(c * ct, ct)], hist_sems.at[slot])
+
     def forward(c, none):
+        slot = lax.rem(c, 2)
+
+        @pl.when(c >= 2)
+        def _():
+            store(c - 2).wait()
+
         rows = pl.multiple_of(c * (ct * nr), ct * nr)
         bc[...] = spread(proj_ref[pl.ds(rows, ct * nr), :], sel)
         for b in range(blocks):
@@ -167,147 +161,70 @@
                 state = list(carried)
                 for u in range(uu):
                     at = s * uu + u
-                    t = c * ct + at
-                    here = pl.ds(pl.multiple_of(t * nr, nr), nr)
+                    here = pl.ds(pl.multiple_of((c * ct + at) * nr, nr), nr)
                     delta = delta_ref[b, here, :]
                     du = delta * x_ref[b, here, :]
                     near = pl.ds(pl.multiple_of(at * nr, nr), nr)
                     y = None
                     for n in range(NS):
+                        if n % 2 == 0:
+                            both = jnp.concatenate([state[n], state[n + 1]], axis=0)
+                            hist[slot, at, b, pl.ds(n * nr, 2 * nr), :] = both.astype(jnp.bfloat16)
                         b_at, c_at = n * LANES, (NS + n) * LANES
                         decay = jnp.exp2(delta * rate[n])
                         state[n] = decay * state[n] + du * bc[near, b_at : b_at + LANES]
                         term = state[n] * bc[near, c_at : c_at + LANES]
                         y = term if y is None else y + term
-                    keep(b, t + 1, state)
                     y_ref[b, here, :] = y
                 return tuple(state)
 
-            start = tuple(state_ref[n, :, lanes] for n in range(NS))
+            start = tuple(last_ref[n, :, lanes] for n in range(NS))
             last = lax.fori_loop(0, ct // uu, steps, start)
             for n in range(NS):
-                state_ref[n, :, lanes] = last[n]
+                last_ref[n, :, lanes] = last[n]
+        store(c).start()
         return none
 
-    lax.fori_loop(0, tt // ct, forward, 0)
-    y_copies = copy_all((y_ref,), (y_out,), out_sems.at[pl.ds(0, 1)])
-
-    state_ref[...] = carry_ref[1]
-    grate_ref[...] = jnp.zeros_like(grate_ref)
-
-    def backward(k, none):
-        c = tt // ct - 1 - k
-        rows = pl.multiple_of(c * (ct * nr), ct * nr)
-        bc[...] = spread(proj_ref[pl.ds(rows, ct * nr), :], sel)
-        for b in range(blocks):
-            lanes = slice(b * LANES, (b + 1) * LANES)
-            for first in (True, False):
-                ns = range(0, NS // 2) if first else range(NS // 2, NS)
-                pairs = range(ns[0] // 2, ns[-1] // 2 + 1)
-                rate = [jnp.broadcast_to(a_ref[n : n + 1, lanes], (nr, LANES)) for n in ns]
-
-                def steps(s, carried):
-                    grad, total, after = (list(v) for v in carried)
-                    for u in reversed(range(uu)):
-                        at = (ct // uu - 1 - s) * uu + u
-                        t = c * ct + at
-                        here = pl.ds(pl.multiple_of(t * nr, nr), nr)
-                        delta = delta_ref[b, here, :]
-                        x = x_ref[b, here, :]
-                        gy = gy_ref[b, here, :]
-                        du = delta * x
-                        near = pl.ds(pl.multiple_of(at * nr, nr), nr)
-                        along_rate = along_b = None
-                        for p in pairs:
-                            pair = hist[b, t, enter(p), :].astype(jnp.float32)
-                            for n, before in ((2 * p, pair[:nr]), (2 * p + 1, pair[nr:])):
-                                i = n - ns[0]
-                                to_b_at = slice(n * LANES, (n + 1) * LANES)
-                                to_c_at = slice((NS + n) * LANES, (NS + n + 1) * LANES)
-                                decay = jnp.exp2(delta * rate[i])
-                                grad[i] = grad[i] + gy * bc[near, to_c_at]
-                                to_c = after[i] * gy
-                                to_b = grad[i] * du
-                                if b > 0:
-                                    to_c = to_c + prod[near, to_c_at]
-                                    to_b = to_b + prod[near, to_b_at]
-                                prod[near, to_c_at] = to_c
-                                prod[near, to_b_at] = to_b
-                                term_b = grad[i] * bc[near, to_b_at]
-                                along_b = term_b if along_b is None else along_b + term_b
-                                grad[i] = grad[i] * decay
-                                weighted = grad[i] * before
-                                total[i] = total[i] + weighted * delta
-                                term = weighted * rate[i]
-                                along_rate = term if along_rate is None else along_rate + term
-                                after[i] = before
-                        gdelta = along_rate * LN2 + along_b * x
-                        gx = along_b * delta
-                        if not first:
-                            gdelta = gdelta + gdelta_ref[b, here, :]
-                            gx = gx + gx_ref[b, here, :]
-                        gdelta_ref[b, here, :] = gdelta
-                        gx_ref[b, here, :] = gx
-                    return tuple(grad), tuple(total), tuple(after)
-
-                after = []
-                for p in pairs:
-                    pair = hist[b, (c + 1) * ct, enter(p), :].astype(jnp.float32)
-                    after += [pair[:nr], pair[nr:]]
-                start = (
-                    tuple(state_ref[n, :, lanes] for n in ns),
-                    tuple(grate_ref[n, :, lanes] for n in ns),
-                    tuple(after),
-                )
-                grad, total, unused = lax.fori_loop(0, ct // uu, steps, start)
-                for i, n in enumerate(ns):
-                    state_ref[n, :, lanes] = grad[i]
-                    grate_ref[n, :, lanes] = total[i]
-        gbc_ref[pl.ds(rows, ct * nr), :] = jnp.dot(
-            prod[...].astype(jnp.bfloat16), fold[...], preferred_element_type=jnp.float32
-        )
-        return none
-
-    lax.fori_loop(0, tt // ct, backward, 0)
-    late = copy_all((gdelta_ref, gx_ref), (gdelta_out, gx_out), out_sems.at[pl.ds(1, 2)])
-    for copy in y_copies + late:
+    count = tt // ct
+    lax.fori_loop(0, count, forward, 0)
+    copies = copy_all((y_ref,), (y_out,), out_sem)
+    for c in range(max(0, count - 2), count):
+        store(c).wait()
+    for copy in copies:
         copy.wait()
 
 
-def scan_main(delta, x, gy, proj, rate, carry, nr, tt):
+def scan_forward(delta, x, proj, rate, carry, nr, tt):
     el = rate.shape[1]
+    blocks = el // LANES
     ct = math.gcd(tt, 32)
     here = pl.BlockSpec(memory_space=pltpu.VMEM)
     away = pl.BlockSpec(memory_space=pl.ANY)
-    full = jax.ShapeDtypeStruct((el // LANES, tt * nr, LANES), jnp.float32)
-    blocks = pltpu.VMEM((el // LANES, nr * tt, LANES), jnp.float32)
+    f32, bf16 = jnp.float32, jnp.bfloat16
+    scan = (blocks, nr * tt, LANES)
     return pl.pallas_call(
-        functools.partial(main_kernel, nr, tt, ct, min(8, ct)),
-        in_specs=[away] * 3 + [here] * 3,
-        out_specs=[away] * 3 + [here] * 2,
+        functools.partial(forward_kernel, nr, tt, ct, min(8, ct)),
+        in_specs=[away] * 2 + [here] * 3,
+        out_specs=[away] * 2 + [here],
         out_shape=[
-            full,
-            full,
-            full,
-            jax.ShapeDtypeStruct((tt * nr, LANES), jnp.float32),
-            jax.ShapeDtypeStruct((NS, nr, el), jnp.float32),
+            jax.ShapeDtypeStruct(scan, f32),
+            jax.ShapeDtypeStruct((tt, blocks, NS * nr, LANES), bf16),
+            jax.ShapeDtypeStruct((NS, nr, el), f32),
         ],
         scratch_shapes=[
-            pltpu.VMEM((LANES, 2 * NS * LANES), jnp.bfloat16),
-            pltpu.VMEM((ct * nr, 2 * NS * LANES), jnp.float32),
-            pltpu.VMEM((el // LANES, tt + 1, NS * nr, LANES), jnp.bfloat16),
-            pltpu.VMEM((ct * nr, 2 * NS * LANES), jnp.float32),
-            pltpu.VMEM((NS, nr, el), jnp.float32),
-            pltpu.VMEM((2 * NS * LANES, LANES), jnp.bfloat16),
-        ]
-        + [blocks] * 6
-        + [
-            pltpu.SemaphoreType.DMA((3,)),
-            pltpu.SemaphoreType.DMA((3,)),
+            pltpu.VMEM((LANES, 2 * NS * LANES), bf16),
+            pltpu.VMEM((ct * nr, 2 * NS * LANES), f32),
+            pltpu.VMEM((2, ct, blocks, NS * nr, LANES), bf16),
+            pltpu.VMEM(scan, f32),
+            pltpu.VMEM(scan, f32),
+            pltpu.VMEM(scan, f32),
+            pltpu.SemaphoreType.DMA((2,)),
+            pltpu.SemaphoreType.DMA((1,)),
+            pltpu.SemaphoreType.DMA((2,)),
         ],
-        compiler_params=pltpu.CompilerParams(vmem_limit_bytes=63 * MIB),
-        name="scan_main",
-    )(delta, x, gy, proj, rate, carry)
+        compiler_params=pltpu.CompilerParams(vmem_limit_bytes=56 * MIB),
+        name="scan_forward",
+    )(delta, x, proj, rate, carry)
 
 
 MESH = pl.DeviceIdType.MESH
@@ -333,25 +250,6 @@
     half = size // 2
     mine = me // 2
     return me, me % 2, me + 1 - 2 * (me % 2), [lax.rem(mine + k, half) for k in range(half)]
-
-
-def sum_rows(size, part_of, part, near, total, mail, far, out, sems, use):
-    me, parity, partner, others = row_peers(size)
-    place = lax.axis_index("seq")
-    half = size // 2
-    greet([(place, partner)] + [(place, 2 * j + parity) for j in others[1:]])
-    first = []
-    for j in range(half):
-        block = 2 * j + 1 - parity
-        part[block] = part_of(block).astype(jnp.bfloat16)
-        first.append(
-            remote(part.at[block], near.at[j], sems.at[0, j], sems.at[1, j], (place, partner))
-        )
-    for j in range(half):
-        total[j] = part_of(2 * j + parity)
-    exchange_sums(size, near, total, mail, far, out, sems, use)
-    for copy in first:
-        copy.wait_send()
 
 
 def exchange_sums(size, near, total, mail, far, out, sems, use, between=None):
@@ -409,39 +307,6 @@
     ]
 
 
-def back_project_kernel(
-    size, low_ref, dt_ref, gbc_ref, out_ref, part, near, total, mail, far, out, sems
-):
-    tt = low_ref.shape[1]
-
-    def part_of(p):
-        ranks = lax.dot_general(
-            low_ref[p], dt_ref[...], (((1,), (1,)), ((), ())), preferred_element_type=jnp.float32
-        )
-        return ranks + gbc_ref[pl.ds(p, tt, stride=size), :]
-
-    def use(p):
-        out_ref[p] = out[p]
-
-    sum_rows(size, part_of, part, near, total, mail, far, out, sems, use)
-
-
-def back_project(low_step, dt_pad, gbc):
-    size, tt, unused_el = low_step.shape
-    here = pl.BlockSpec(memory_space=pltpu.VMEM)
-    return pl.pallas_call(
-        functools.partial(back_project_kernel, size),
-        in_specs=[here] * 3,
-        out_specs=here,
-        out_shape=jax.ShapeDtypeStruct((size, tt, LANES), jnp.bfloat16),
-        scratch_shapes=sum_scratch(size, tt),
-        compiler_params=pltpu.CompilerParams(
-            vmem_limit_bytes=40 * MIB, collective_id=1, has_side_effects=True
-        ),
-        name="back_project",
-    )(low_step, dt_pad, gbc)
-
-
 class Carry:
     def __init__(self, seq, ends, alive, out, mail, land, sems):
         self.seq, self.ends, self.alive, self.out = seq, ends, alive, out
@@ -906,10 +771,9 @@
         self.size, self.part, self.keep, self.land, self.mail = size, part, keep, land, mail
         self.keep_sem, self.send, self.recv = keep_sem, send, recv
         self.me, self.place = lax.axis_index("rows"), lax.axis_index("seq")
-        self.tt, self.width = part.shape[1], part.shape[2] // 2
+        self.tt, self.width = keep.shape[1], keep.shape[2] // 2
         self.orders = bit_orders(size)
         self.steps = len(self.orders[0])
-        self.started, self.local = [], []
 
     @staticmethod
     def scratch(size, tt, width):
@@ -926,6 +790,8 @@
         return masks_of(self.orders[h][k + 1 :])
 
     def at(self, h, k, m):
+        if k == 0:
+            return m >> 1
         return sum(len(self.free(h, j)) for j in range(k)) + self.free(h, k).index(m)
 
     def cols(self, h):
@@ -941,20 +807,25 @@
             value = value + self.land[self.at(h, j, m), rows, self.cols(h)].astype(jnp.float32)
         return value
 
+    def staged(self, i, stage):
+        for h in range(2):
+            remote(
+                stage.at[i, :, self.cols(h)], self.land.at[i, :, self.cols(h)], self.send.at[h, i],
+                self.recv.at[h, i], (self.place, flip(self.me, 1)),
+            )
+
     def start(self):
         for h in range(2):
             self.scatter(h, 0)
         for m in self.free(0, 0):
-            copy = pltpu.make_async_copy(
+            pltpu.make_async_copy(
                 self.part.at[flip(self.me, m)], self.keep.at[m >> 1], self.keep_sem.at[m >> 1]
-            )
-            copy.start()
-            self.local.append(copy)
+            ).start()
 
     def step(self, k):
-        if k == 1:
-            for copy in self.local:
-                copy.wait()
+        if k == 1 and self.part is not None:
+            for j in range(self.size // 2):
+                wait_for(self.keep.at[j], self.keep_sem.at[j])
         for h in range(2):
             self.scatter(h, k)
 
@@ -975,12 +846,14 @@
 
                 by_tiles(self.tt, 32, fill)
                 source = self.mail.at[box, :, self.cols(h)]
-            self.started.append(
-                remote(
-                    source, self.land.at[slot, :, self.cols(h)], self.send.at[h, slot], self.recv.at[h, slot],
-                    (self.place, flip(self.me, bit)),
-                )
+            remote(
+                source, self.land.at[slot, :, self.cols(h)], self.send.at[h, slot], self.recv.at[h, slot],
+                (self.place, flip(self.me, bit)),
             )
+
+    def later(self, first):
+        for k in range(first, self.steps):
+            self.step(k)
 
     def finish(self, own):
         for h in range(2):
@@ -993,18 +866,19 @@
             by_tiles(self.tt, 32, fill)
 
     def drain(self):
-        for copy in self.started:
-            copy.wait_send()
+        for h in range(2):
+            for slot in range(self.size - 1):
+                wait_for(self.land.at[slot, :, self.cols(h)], self.send.at[h, slot])
 
 
 class SeqSum:
-    def __init__(self, seq, held, land, mail, fill_sem, send, recv):
-        self.seq, self.held, self.land, self.mail = seq, held, land, mail
+    def __init__(self, seq, lag, held, land, mail, fill_sem, send, recv):
+        self.seq, self.lag, self.held, self.land, self.mail = seq, lag, held, land, mail
         self.fill_sem, self.send, self.recv = fill_sem, send, recv
         self.me, self.place = lax.axis_index("rows"), lax.axis_index("seq")
         self.behind = (self.place, seq - 1 - self.place)
         self.chunks = held.shape[0]
-        self.last_step = self.chunks + seq - 1
+        self.last_step = self.chunks + lag * (seq - 1)
 
     @staticmethod
     def scratch(chunks, block):
@@ -1025,7 +899,7 @@
         )
 
     def hop(self, step, way):
-        n = step - self.behind[way]
+        n = step - self.lag * self.behind[way]
 
         @pl.when((n >= 0) & (n < self.chunks))
         def _():
@@ -1044,7 +918,7 @@
                     self.copy(n, way, self.mail.at[way, n]).start()
 
     def advance(self, step, total):
-        first = step - jnp.minimum(self.behind[0], self.behind[1])
+        first = step - self.lag * jnp.minimum(self.behind[0], self.behind[1])
 
         @pl.when((first >= 0) & (first < self.chunks))
         def _():
@@ -1052,7 +926,7 @@
 
         self.hop(step, 0)
         self.hop(step, 1)
-        n = step - jnp.maximum(self.behind[0], self.behind[1])
+        n = step - self.lag * jnp.maximum(self.behind[0], self.behind[1])
 
         @pl.when((n >= 0) & (n < self.chunks))
         def _():
@@ -1088,88 +962,445 @@
                 lax.fori_loop(0, self.chunks, sent, 0)
 
 
-def chunk_order(size):
-    return sorted(range(size), key=lambda m: (m > 1, (m >> 1).bit_count(), m))
-
-
-def tail_kernel(size, seq, *refs):
-    branch, normed, weight, out_w, small = refs[:5]
-    branch_own, normed_own, total = refs[5:8]
-    scatter_a = RowScatter(size, branch, *refs[8:14])
-    scatter_b = RowScatter(size, normed, *refs[14:20])
-    held, land, mail, fill_sem, zsend, zrecv, swap_send = refs[20:]
-    chain = SeqSum(seq, held, land, mail, fill_sem, zsend, zrecv)
+def fill_chunks(size, held, fill_sem, swap_send, sources, weight):
     me, place = lax.axis_index("rows"), lax.axis_index("seq")
     rows, cols = held.shape[1:]
-    greet_rows_and_seq(size, seq)
-    scatter_a.start()
     n = 0
-    for source in (out_w, small):
+    for source in sources:
         for i in range(source.shape[0] // rows):
             for j in range(source.shape[1] // cols):
                 piece = source.at[pl.ds(i * rows, rows), pl.ds(j * cols, cols)]
                 pltpu.make_async_copy(piece, held.at[n], fill_sem.at[n]).start()
                 n += 1
-    sent = []
-    for m in chunk_order(size):
+    for m in range(size):
+        q = flip(me, m)
         for i in range(weight.shape[1] // rows):
-            piece = weight.at[flip(me, m), pl.ds(i * rows, rows), :]
+            piece = weight.at[q, pl.ds(i * rows, rows), :]
             if m == 0:
                 pltpu.make_async_copy(piece, held.at[n], fill_sem.at[n]).start()
             else:
-                target = (place, flip(me, m))
-                sent.append(remote(piece, held.at[n], swap_send.at[n], fill_sem.at[n], target))
+                remote(piece, held.at[n], swap_send.at[n], fill_sem.at[n], (place, q))
             n += 1
-    scatter_b.start()
-    jobs = []
-    for k in range(1, scatter_a.steps):
-        jobs += [functools.partial(scatter_a.step, k), functools.partial(scatter_b.step, k)]
-    jobs += [functools.partial(scatter_a.finish, branch_own), functools.partial(scatter_b.finish, normed_own)]
-    done = 0
+
+
+def drain_swap(size, held, swap_send, weight):
+    parts = weight.shape[1] // held.shape[1]
+    first = held.shape[0] - (size - 1) * parts
+    for n in range(first, held.shape[0]):
+        wait_for(held.at[n], swap_send.at[n])
+
+
+def backward_kernel(size, seq, nr, tt, ct, uu, *refs):
+    delta_in, x_in, gy_in, hist_in, proj_ref, a_ref, carry_ref, last_ref, branch, out_w, gate_w = refs[:11]
+    gdelta_out, gx_out, gbc_ref, grate_ref, branch_own, total = refs[11:17]
+    sel, bc, hist, prod, state_ref, after_ref, fold, delta_ref, x_ref, gy_ref, gdelta_ref, gx_ref = refs[17:29]
+    sems, out_sems, hist_sems = refs[29:32]
+    scatter = RowScatter(size, branch, *refs[32:38])
+    held, land, mail, fill_sem, zsend, zrecv, swap_send = refs[38:]
+    chain = SeqSum(seq, 3, held, land, mail, fill_sem, zsend, zrecv)
+    el = a_ref.shape[1]
+    blocks = el // LANES
+    count = tt // ct
+
+    def fetch(c):
+        slot = lax.rem(c, 2)
+        return pltpu.make_async_copy(hist_in.at[pl.ds(c * ct, ct)], hist.at[slot], hist_sems.at[slot])
+
+    copies = copy_all((delta_in, x_in, gy_in), (delta_ref, x_ref, gy_ref), sems)
+    fetch(count - 1).start()
+    greet_rows_and_seq(size, seq)
+    scatter.start()
+    fill_chunks(size, held, fill_sem, swap_send, (out_w,), gate_w)
+    sel[...] = selector(LANES)
+    fold_row = lax.broadcasted_iota(jnp.int32, fold.shape, 0) // LANES
+    fold_col = lax.broadcasted_iota(jnp.int32, fold.shape, 1)
+    fold[...] = (fold_row + R == fold_col).astype(jnp.bfloat16)
+    state_ref[...] = carry_ref[1]
+    after_ref[...] = last_ref[...]
+    grate_ref[...] = jnp.zeros_like(grate_ref)
+    for copy in copies:
+        copy.wait()
+
+    def backward(k, none):
+        c = count - 1 - k
+        slot = lax.rem(c, 2)
+
+        @pl.when(c > 0)
+        def _():
+            fetch(c - 1).start()
+
+        for at_k, job in (
+            (1, functools.partial(scatter.step, 1)),
+            (count // 2, functools.partial(scatter.later, 2)),
+            (count - 2, functools.partial(scatter.finish, branch_own)),
+        ):
+            pl.when(k == at_k)(job)
+
+        rows = pl.multiple_of(c * (ct * nr), ct * nr)
+        bc[...] = spread(proj_ref[pl.ds(rows, ct * nr), :], sel)
+        fetch(c).wait()
+        for b in range(blocks):
+            lanes = slice(b * LANES, (b + 1) * LANES)
+            for first in (True, False):
+                ns = range(0, NS // 2) if first else range(NS // 2, NS)
+                pairs = range(ns[0] // 2, ns[-1] // 2 + 1)
+                rate = [jnp.broadcast_to(a_ref[n : n + 1, lanes], (nr, LANES)) for n in ns]
+
+                def steps(s, carried):
+                    grad, total_rate, after = (list(v) for v in carried)
+                    for u in reversed(range(uu)):
+                        at = (ct // uu - 1 - s) * uu + u
+                        here = pl.ds(pl.multiple_of((c * ct + at) * nr, nr), nr)
+                        delta = delta_ref[b, here, :]
+                        x = x_ref[b, here, :]
+                        gy = gy_ref[b, here, :]
+                        du = delta * x
+                        near = pl.ds(pl.multiple_of(at * nr, nr), nr)
+                        along_rate = along_b = None
+                        for p in pairs:
+                            pair = hist[slot, at, b, pl.ds(2 * p * nr, 2 * nr), :].astype(jnp.float32)
+                            for n, before in ((2 * p, pair[:nr]), (2 * p + 1, pair[nr:])):
+                                i = n - ns[0]
+                                to_b_at = slice(n * LANES, (n + 1) * LANES)
+                                to_c_at = slice((NS + n) * LANES, (NS + n + 1) * LANES)
+                                decay = jnp.exp2(delta * rate[i])
+                                grad[i] = grad[i] + gy * bc[near, to_c_at]
+                                to_c = after[i] * gy
+                                to_b = grad[i] * du
+                                if b > 0:
+                                    to_c = to_c + prod[near, to_c_at]
+                                    to_b = to_b + prod[near, to_b_at]
+                                prod[near, to_c_at] = to_c
+                                prod[near, to_b_at] = to_b
+                                term_b = grad[i] * bc[near, to_b_at]
+                                along_b = term_b if along_b is None else along_b + term_b
+                                grad[i] = grad[i] * decay
+                                weighted = grad[i] * before
+                                total_rate[i] = total_rate[i] + weighted * delta
+                                term = weighted * rate[i]
+                                along_rate = term if along_rate is None else along_rate + term
+                                after[i] = before
+                        gdelta = along_rate * LN2 + along_b * x
+                        gx = along_b * delta
+                        if not first:
+                            gdelta = gdelta + gdelta_ref[b, here, :]
+                            gx = gx + gx_ref[b, here, :]
+                        gdelta_ref[b, here, :] = gdelta
+                        gx_ref[b, here, :] = gx
+                    return tuple(grad), tuple(total_rate), tuple(after)
+
+                start = tuple(tuple(ref[n, :, lanes] for n in ns) for ref in (state_ref, grate_ref, after_ref))
+                ends = lax.fori_loop(0, ct // uu, steps, start)
+                for i, n in enumerate(ns):
+                    for ref, end in zip((state_ref, grate_ref, after_ref), ends):
+                        ref[n, :, lanes] = end[i]
+            if b < 2:
+                chain.advance(2 * k + b, total)
+        gbc_ref[pl.ds(rows, ct * nr), :] = jnp.dot(
+            prod[...].astype(jnp.bfloat16), fold[...], preferred_element_type=jnp.float32
+        )
+        return none
+
+    lax.fori_loop(0, count, backward, 0)
+    late = copy_all((gdelta_ref, gx_ref), (gdelta_out, gx_out), out_sems)
+    done = min(2, blocks) * count if blocks > 1 else count
+    chain.run(2 * count, max(2 * count, chain.last_step), total)
+    scatter.drain()
+    chain.drain()
+    drain_swap(size, held, swap_send, gate_w)
+    for copy in late:
+        copy.wait()
+
+
+def scan_backward(delta, x, gy, hist, proj, rate, carry, last, branch, out_w, gate_w, size, seq):
+    nr, tt, width = branch.shape
+    el = rate.shape[1]
+    blocks = el // LANES
+    ct = math.gcd(tt, 16)
+    here = pl.BlockSpec(memory_space=pltpu.VMEM)
+    away = pl.BlockSpec(memory_space=pl.ANY)
+    f32, bf16 = jnp.float32, jnp.bfloat16
+    scan = (blocks, nr * tt, LANES)
+    piece = gate_w.shape[1:]
+    chunks = (out_w.size + gate_w.size) // math.prod(piece)
+    return pl.pallas_call(
+        functools.partial(backward_kernel, size, seq, nr, tt, ct, min(8, ct)),
+        in_specs=[away] * 4 + [here] * 4 + [away] * 3,
+        out_specs=[away] * 2 + [here] * 4,
+        out_shape=[
+            jax.ShapeDtypeStruct(scan, f32),
+            jax.ShapeDtypeStruct(scan, f32),
+            jax.ShapeDtypeStruct((tt * nr, LANES), f32),
+            jax.ShapeDtypeStruct((NS, nr, el), f32),
+            jax.ShapeDtypeStruct((tt, width), bf16),
+            jax.ShapeDtypeStruct((chunks,) + piece, bf16),
+        ],
+        scratch_shapes=[
+            pltpu.VMEM((LANES, 2 * NS * LANES), bf16),
+            pltpu.VMEM((ct * nr, 2 * NS * LANES), f32),
+            pltpu.VMEM((2, ct, blocks, NS * nr, LANES), bf16),
+            pltpu.VMEM((ct * nr, 2 * NS * LANES), f32),
+            pltpu.VMEM((NS, nr, el), f32),
+            pltpu.VMEM((NS, nr, el), f32),
+            pltpu.VMEM((2 * NS * LANES, LANES), bf16),
+        ]
+        + [pltpu.VMEM(scan, f32)] * 5
+        + [
+            pltpu.SemaphoreType.DMA((3,)),
+            pltpu.SemaphoreType.DMA((2,)),
+            pltpu.SemaphoreType.DMA((2,)),
+        ]
+        + RowScatter.scratch(size, tt, width)
+        + SeqSum.scratch(chunks, piece)
+        + [pltpu.SemaphoreType.DMA((chunks,))],
+        compiler_params=pltpu.CompilerParams(
+            vmem_limit_bytes=62 * MIB, collective_id=3, has_side_effects=True
+        ),
+        name="scan_backward",
+    )(delta, x, gy, hist, proj, rate, carry, last, branch, out_w, gate_w)
+
+
+def small_rows(piece_rows):
+    rows = 2 * LANES + 32
+    return rows + -rows % piece_rows
+
+
+def back_kernel(size, seq, *refs):
+    gdelta_in, gx_in, delta_in, normed_in, w_in, pre_in, cext_in, ggp_in, gbc_in = refs[:9]
+    rank_ref, dt_w, x_w, taps_ref, rate_ref, grate_ref = refs[9:15]
+    own, sums = refs[15:17]
+    (
+        gdelta, gx, delta, normed, wv, pre, cext, gmix, gbc, low, gcp, turned, w_stage, acc_x, acc_dt, acc,
+        small, hmail, hland, stage,
+    ) = refs[17:37]
+    part, near, total, mail, far, out, sems = refs[37:44]
+    scatter = RowScatter(size, None, *refs[44:50])
+    held, zland, zmail, fill_sem, zsend, zrecv = refs[50:56]
+    swap_send, in_sems, halo_send, halo_recv = refs[56:]
+    chain = SeqSum(seq, 2, held, zland, zmail, fill_sem, zsend, zrecv)
+    me, parity, partner, others = row_peers(size)
+    place = lax.axis_index("seq")
+    share, el = w_stage.shape[1:]
+    tt = low.shape[0]
+    width = normed.shape[1]
+    blocks = el // LANES
+    half = size // 2
+    f32, bf16 = jnp.float32, jnp.bfloat16
+    nt = (((1,), (1,)), ((), ()))
+    tn = (((0,), (0,)), ((), ()))
+    copies = copy_all(
+        (gdelta_in, delta_in, gbc_in, pre_in, cext_in, gx_in, ggp_in, w_in, normed_in),
+        (gdelta, delta, gbc, pre, cext, gx, gmix.at[:, :, pl.ds(el, el)], wv, normed),
+        in_sems,
+    )
+    greet_rows_and_seq(size, seq)
+    for ref in (acc_x, acc_dt, acc, small):
+        ref[...] = jnp.zeros_like(ref)
+    for copy in copies[:3]:
+        copy.wait()
+
+    def fold8(value):
+        return jnp.sum(value.reshape(value.shape[0] // 8, 8, value.shape[1]), axis=0)
+
+    def block_at(i):
+        return 2 * lax.rem(me // 2 + lax.rem(i, half), half) + lax.rem(parity + 1 + lax.div(i, half), 2)
+
+    def steps_back(i, none):
+        p = block_at(i)
+
+        def body(span):
+            for b in range(blocks):
+                lanes = slice(b * LANES, (b + 1) * LANES)
+                there = pl.ds(p + span.start * size, 32, stride=size)
+                dl = delta[b, there, :]
+                near_zero = dl * (1.0 - dl * (0.5 - dl * (1.0 / 6.0)))
+                value = gdelta[b, there, :] * jnp.where(dl < 0.01, near_zero, 1.0 - jnp.exp(-dl))
+                low[span, lanes] = value.astype(bf16)
+                acc[KC + 1, :, lanes] = acc[KC + 1, :, lanes] + fold8(value)
+
+        by_tiles(tt, 32, body)
+        value = lax.dot_general(low[...], dt_w[...], nt, preferred_element_type=f32)
+        value = value + gbc[pl.ds(p, tt, stride=size), :]
+        acc_dt[...] += lax.dot_general(rank_ref[p], low[...], tn, preferred_element_type=f32)
+
+        @pl.when(i < half)
+        def _():
+            part[p] = value.astype(bf16)
+            remote(
+                part.at[p], near.at[lax.div(p, 2)], sems.at[0, lax.div(p, 2)], sems.at[1, lax.div(p, 2)],
+                (place, partner),
+            )
+
+        @pl.when(i >= half)
+        def _():
+            total[lax.div(p, 2)] = value
+
+        return none
+
+    lax.fori_loop(0, size, steps_back, 0)
+    for copy in copies[3:]:
+        copy.wait()
+    exchange_sums(size, near, total, mail, far, out, sems, lambda p: None)
+    for j in range(half):
+        wait_for(near.at[j], sems.at[0, j])
+
+    def halo(p):
+        return pltpu.make_async_remote_copy(
+            src_ref=hmail.at[p], dst_ref=hland.at[p], send_sem=halo_send.at[p], recv_sem=halo_recv.at[p],
+            device_id=(jnp.maximum(place - 1, 0), me), device_id_type=MESH,
+        )
+
+    def conv_back(p, none):
+        def body(span):
+            value = lax.dot_general(out[p, span, :], x_w[...], nt, preferred_element_type=f32)
+            there = pl.ds(p + span.start * size, 32, stride=size)
+            value = value + jnp.concatenate([gx[b, there, :] for b in range(blocks)], axis=1)
+            here = pre[p, span, :]
+            sig = 1.0 / (1.0 + jnp.exp(-here))
+            low[span, :] = (here * sig).astype(bf16)
+            value = value * sig * (1.0 + here * (1.0 - sig))
+            gcp[p, span, :] = value
+            ext = cext[p, pl.ds(span.start, 48), :].astype(f32)
+            acc[KC] = acc[KC] + fold8(value)
+            for k in range(KC):
+                acc[k] = acc[k] + fold8(value * ext[16 - KC + 1 + k : 16 - KC + 1 + k + 32])
+
+        by_tiles(tt, 32, body)
+        acc_x[...] += lax.dot_general(out[p], low[...], tn, preferred_element_type=f32)
+        hmail[p] = gcp[p, 0:16, :].astype(bf16)
+
+        @pl.when(place > 0)
+        def _():
+            halo(p).start()
+
+        return none
+
+    lax.fori_loop(0, size, conv_back, 0)
+
+    def turn(p, none):
+        @pl.when(place < seq - 1)
+        def _():
+            halo(p).wait_recv()
+            gcp[p, tt : tt + 8, :] = hland[p, 0:8, :].astype(f32)
+
+        @pl.when(place == seq - 1)
+        def _():
+            gcp[p, tt : tt + 8, :] = jnp.zeros((8, el), f32)
+
+        def body(span):
+            ext = gcp[p, pl.ds(span.start, 40), :]
+            value = taps_ref[KC - 1 : KC, :] * ext[0:32]
+            for k in range(KC - 1):
+                value = value + taps_ref[k : k + 1, :] * ext[KC - 1 - k : KC - 1 - k + 32]
+            gmix[p, span, 0:el] = value.astype(bf16)
+
+        by_tiles(tt, 32, body)
+        columns = pl.ds(pl.multiple_of(p * tt, tt), tt)
+        turned[:, columns] = jnp.transpose(gmix[p, :, 0:el].astype(f32)).astype(bf16)
+        return none
+
+    lax.fori_loop(0, size, turn, 0)
+
+    group = 384 // share
+
+    def weights(j, none):
+        columns = pl.ds(pl.multiple_of(j * 384, 384), 384)
+        value = jnp.dot(turned[...], normed[:, columns], preferred_element_type=f32)
+        value = jnp.transpose(value).astype(bf16)
+        for g in range(group):
+            w_stage[j * group + g] = value[g * share : (g + 1) * share, :]
+        return none
+
+    lax.fori_loop(0, width // 384, weights, 0)
+    rows = 2 * LANES
+    small[0:LANES, :] = acc_x[...].astype(bf16)
+    small[LANES:rows, :] = acc_dt[...].astype(bf16)
+    rate_sum = jnp.sum(grate_ref[...], axis=1) * rate_ref[...]
+    last = [rate_sum] + [jnp.sum(acc[k], axis=0, keepdims=True) for k in range(KC + 2)]
+    last.append(jnp.zeros((16 - KC - 2, el), f32))
+    small[rows : rows + 32, :] = jnp.concatenate(last, axis=0).astype(bf16)
+    fill_chunks(size, held, fill_sem, swap_send, (small,), w_stage)
+
+    def spread_back(i, none):
+        p = crossed(me, jnp.where(i < half, 2 * i + 1, 2 * (i - half)), size)
+        weight = wv[...].reshape(width, 2 * el)
+        value = lax.dot_general(gmix[p], weight, nt, preferred_element_type=f32).astype(bf16)
+
+        @pl.when(i < half)
+        def _():
+            stage[i] = value
+            scatter.staged(i, stage)
+
+        @pl.when(i >= half)
+        def _():
+            scatter.keep[i - half] = value
+
+        chain.advance(i, sums)
+        return none
+
+    lax.fori_loop(0, size, spread_back, 0)
+    jobs = [functools.partial(scatter.step, k) for k in range(1, scatter.steps)]
+    jobs.append(functools.partial(scatter.finish, own))
+    done = size
     for i, job in enumerate(jobs):
-        upto = chain.last_step * (i + 1) // (len(jobs) + 1)
-        chain.run(done, upto, total)
+        job()
+        upto = min(chain.last_step, done + chain.last_step // 4)
+        chain.run(done, upto, sums)
         done = upto
-        job()
-    chain.run(done, chain.last_step, total)
-    scatter_a.drain()
-    scatter_b.drain()
-    for copy in sent:
-        copy.wait_send()
+    chain.run(done, max(done, chain.last_step), sums)
+    scatter.drain()
     chain.drain()
-
-
-def reduce_all(branch, normed, weight, out_w, small, size, seq):
+    drain_swap(size, held, swap_send, w_stage)
+
+    def halo_sent(p, none):
+        halo(p).wait_send()
+        return none
+
+    @pl.when(place > 0)
+    def _():
+        lax.fori_loop(0, size, halo_sent, 0)
+
+
+def back(gdelta, gx, delta, normed, w_in, pre, cext, ggp, gbc, rank, dt_w, x_w, taps, rate, grate, size, seq):
     away = pl.BlockSpec(memory_space=pl.ANY)
     here = pl.BlockSpec(memory_space=pltpu.VMEM)
-    tt, width = branch.shape[1:]
-    share, cols = weight.shape[1:]
-    rows = share // 2
-    chunks = (weight.size + out_w.size + small.size) // (rows * cols)
+    f32, bf16 = jnp.float32, jnp.bfloat16
+    unused_size, tt, el = pre.shape
+    share = w_in.shape[1]
+    width = normed.shape[1]
+    piece = (share // 2, el)
+    low = small_rows(piece[0])
+    chunks = 2 * size + low // piece[0]
+    scratch = [
+        (gdelta.shape, f32), (gx.shape, f32), (delta.shape, f32), (normed.shape, bf16), (w_in.shape, bf16),
+        (pre.shape, f32), (cext.shape, bf16), ((size, tt, 2 * el), bf16), (gbc.shape, f32), ((tt, el), bf16),
+        ((size, tt + 8, el), f32), ((el, size * tt), bf16), ((size, share, el), bf16), ((LANES, el), f32),
+        ((LANES, el), f32), ((KC + 2, 8, el), f32), ((low, el), bf16), ((size, 16, el), bf16),
+        ((size, 16, el), bf16), ((size // 2, tt, width), bf16),
+    ]
     return pl.pallas_call(
-        functools.partial(tail_kernel, size, seq),
-        in_specs=[away] * 5,
-        out_specs=[here] * 3,
-        out_shape=[jax.ShapeDtypeStruct((tt, width), jnp.bfloat16)] * 2
-        + [jax.ShapeDtypeStruct((chunks, rows, cols), jnp.bfloat16)],
-        scratch_shapes=RowScatter.scratch(size, tt, width) * 2
-        + SeqSum.scratch(chunks, (rows, cols))
-        + [pltpu.SemaphoreType.DMA((chunks,))],
+        functools.partial(back_kernel, size, seq),
+        in_specs=[away] * 9 + [here] * 6,
+        out_specs=[here] * 2,
+        out_shape=[
+            jax.ShapeDtypeStruct((tt, width), bf16),
+            jax.ShapeDtypeStruct((chunks,) + piece, bf16),
+        ],
+        scratch_shapes=[pltpu.VMEM(*v) for v in scratch]
+        + sum_scratch(size, tt)
+        + RowScatter.scratch(size, tt, width)
+        + SeqSum.scratch(chunks, piece)
+        + [
+            pltpu.SemaphoreType.DMA((chunks,)),
+            pltpu.SemaphoreType.DMA((9,)),
+            pltpu.SemaphoreType.DMA((size,)),
+            pltpu.SemaphoreType.DMA((size,)),
+        ],
         compiler_params=pltpu.CompilerParams(
-            vmem_limit_bytes=60 * MIB, collective_id=4, has_side_effects=True
+            vmem_limit_bytes=63 * MIB, collective_id=4, has_side_effects=True
         ),
-        name="reduce_all",
-    )(branch, normed, weight, out_w, small)
-
-
-def from_behind(value, axis, steps):
-    count = lax.axis_size(axis)
-    first, last = (max(0, -steps), min(count, count - steps))
-    return lax.ppermute(value, axis, [(source, source + steps) for source in range(first, last)])
-
-
-def shortened(x):
-    return x.astype(jnp.bfloat16)
+        name="back",
+    )(gdelta, gx, delta, normed, w_in, pre, cext, ggp, gbc, rank, dt_w, x_w, taps, rate, grate)
 
 
 def contract_rows(left, right):
@@ -1222,13 +1453,9 @@
         widen(dt_bias.astype(f32), 0)[None], size, seq, direct,
     )
     normed, all_cot = normed.reshape(count, D), all_cot.reshape(count, D)
-    w_in = w_in.reshape(D, 2 * elp)
     gate_pre, grad_gated = gate_pre.reshape(count, elp), grad_gated.reshape(count, elp)
     gain = all_notes[:, 0, :share].reshape(D).astype(f32)
     alive = all_notes[:, 1, :1].astype(f32)
-    rank_part = rank_all.reshape(count, LANES)[:, :R]
-    extended = conv_ext[:, 16 - KC + 1 :]
-
     def by_row(value):
         value = value.reshape(elp // LANES, tt, nr, LANES)
         return jnp.transpose(value, (2, 1, 0, 3)).reshape(count, elp)
@@ -1236,74 +1463,31 @@
     rate2 = rate * LOG2E
     scanned = (delta_t, x_t, gy_t)
     carry = scan_ends(*scanned, proj_t, rate2, alive, nr, tt, seq)
-    scan_y, grad_delta, grad_input, grad_bc, grate = scan_main(
-        *scanned, proj_t, rate2, carry, nr, tt
+    scan_y, hist, last = scan_forward(delta_t, x_t, proj_t, rate2, carry, nr, tt)
+    scan_y = by_row(scan_y)
+    gate_sig = jax.nn.sigmoid(gate_pre)
+    gated = (scan_y * gate_pre * gate_sig).astype(bf16)
+    grad_gate_pre = grad_gated * scan_y * gate_sig * (1.0 + gate_pre * (1.0 - gate_sig))
+    grad_gate_pre = grad_gate_pre.astype(bf16)
+    branch = jnp.dot(gated, out_proj, preferred_element_type=f32).astype(bf16)
+    grad_out_proj = contract_rows(gated, all_cot).astype(bf16)[:el]
+    grad_in_gate = contract_rows(normed, grad_gate_pre).astype(bf16).reshape(size, share, elp)
+    grad_delta, grad_input, grad_bc, grate, branch_own, summed_gate = scan_backward(
+        *scanned, hist, proj_t, rate2, carry, last, branch.reshape(nr, tt, D),
+        grad_out_proj, grad_in_gate, size, seq,
     )
-    scan_y, grad_delta, grad_input, step_size = (by_row(v) for v in (scan_y, grad_delta, grad_input, delta_t))
-    conv_out = jax.nn.silu(conv_pre).astype(bf16).reshape(count, elp)
-    gate_sig = jax.nn.sigmoid(gate_pre)
-    gate_act = gate_pre * gate_sig
-    grad_a_log = jnp.sum(grate, axis=1) * rate
-
-    gated = (scan_y * gate_act).astype(jnp.bfloat16)
-    branch = jnp.dot(gated, out_proj, preferred_element_type=jnp.float32).astype(jnp.bfloat16)
-    grad_out_proj = contract_rows(gated, all_cot)
-    grad_gate_pre = grad_gated * scan_y * gate_sig * (1.0 + gate_pre * (1.0 - gate_sig))
-
-    grad_step_pre = grad_delta * -jnp.expm1(-step_size)
-    grad_dt_bias = jnp.sum(grad_step_pre, axis=0)
-    low_step = grad_step_pre.astype(jnp.bfloat16)
-    grad_dt_proj = contract_rows(rank_part, low_step)
-    grad_projected = back_project(low_step.reshape(nr, tt, elp), dt_pad, grad_bc).reshape(count, LANES)
-    grad_x_proj = contract_rows(conv_out, grad_projected)
-    grad_conv_out = contract_cols(grad_projected, x_proj) + grad_input
-    conv_sig = jax.nn.sigmoid(conv_pre).reshape(count, elp)
-    conv_flat = conv_pre.reshape(count, elp)
-    grad_conv_pre = (grad_conv_out * conv_sig * (1.0 + conv_flat * (1.0 - conv_sig))).reshape(nr, tt, elp)
-    grad_conv_bias = jnp.sum(grad_conv_pre, axis=(0, 1))
-    grad_taps = jnp.stack(
-        [
-            jnp.sum(grad_conv_pre * extended[:, k : k + tt].astype(jnp.float32), axis=(0, 1))
-            for k in range(KC)
-        ]
+    grad_normed, summed_conv = back(
+        grad_delta, grad_input, delta_t, normed, w_in, conv_pre, conv_ext,
+        grad_gate_pre.reshape(nr, tt, elp), grad_bc, rank_all, dt_pad, x_proj, taps, rate, grate, size, seq,
     )
-    grad_ext = sum(
-        jnp.pad(taps[k] * grad_conv_pre, ((0, 0), (k, KC - 1 - k), (0, 0))) for k in range(KC)
-    )
-    right_rim = from_behind(shortened(grad_ext[:, : KC - 1]), "seq", -1)
-    grad_conv_in = grad_ext[:, KC - 1 :] + jnp.pad(
-        right_rim.astype(jnp.float32), ((0, 0), (tt - (KC - 1), 0), (0, 0))
-    )
-    grad_mixed = jnp.concatenate([grad_conv_in.reshape(count, elp), grad_gate_pre], axis=1).astype(
-        jnp.bfloat16
-    )
-    grad_in_proj = contract_rows(normed, grad_mixed).astype(jnp.bfloat16)
-    grad_normed_part = contract_cols(grad_mixed, w_in).astype(jnp.bfloat16)
-    small = jnp.concatenate(
-        [grad_x_proj.T, grad_dt_proj, grad_taps, grad_conv_bias[None], grad_dt_bias[None], grad_a_log],
-        axis=0,
-    )
-    piece = (share // 2, 2 * elp)
-    folded = shortened(small)
-    folded = jnp.pad(folded, ((0, -folded.shape[0] % 2), (0, 0)))
-    high = folded.shape[0] // 2
-    folded = jnp.concatenate([folded[:high], folded[high:]], axis=1)
-    folded = jnp.pad(folded, ((0, -high % piece[0]), (0, 0)))
-    branch_own, grad_normed, summed = reduce_all(
-        branch.reshape(nr, tt, D), grad_normed_part.reshape(nr, tt, D),
-        grad_in_proj.reshape(size, share, 2 * elp), shortened(grad_out_proj)[:el], folded, size, seq,
-    )
-    summed = summed.astype(jnp.float32)
-    out_rows, out_cols = el // piece[0], D // piece[1]
-    at = out_rows * out_cols
-    sum_out = jnp.swapaxes(summed[:at].reshape(out_rows, out_cols, *piece), 1, 2).reshape(el, D)
-    folded = summed[at : at + folded.shape[0] // piece[0]].reshape(folded.shape)
-    small = jnp.concatenate([folded[:high, :elp], folded[:high, elp:]], axis=0)[:, :el]
-    blocks = summed[-2 * size :].reshape(size, share, 2, elp)[..., :el]
-    me = lax.axis_index("rows")
-    places = [chunk_order(size).index(m) for m in range(size)]
-    order = jnp.array(places)[jnp.array(range(size)) ^ me]
-    sum_in = jnp.moveaxis(blocks[order], 0, 2).reshape(share, 2 * E)
+    piece = (share, elp)
+    out_rows, out_cols = el // share, D // elp
+    sum_out = summed_gate[: out_rows * out_cols].reshape(out_rows, out_cols, *piece)
+    sum_out = jnp.swapaxes(sum_out, 1, 2).reshape(el, D).astype(f32)
+    small = summed_conv[: -2 * size].reshape(-1, elp)[:, :el].astype(f32)
+    order = jnp.array(range(size)) ^ lax.axis_index("rows")
+    sum_in = jnp.stack([summed_conv[-2 * size :].reshape((size,) + piece)[order], summed_gate[-size:][order]])
+    sum_in = jnp.transpose(sum_in[..., :el].astype(f32), (2, 0, 1, 3)).reshape(share, 2 * E)
     block_out = (tokens.astype(jnp.float32) + branch_own[None].astype(jnp.float32)).astype(jnp.bfloat16)
     grad_normed = grad_normed[None].astype(jnp.float32)
 
@@ -1316,23 +1500,18 @@
     )
     d_tokens = (cotangent.astype(jnp.float32) + grad_norm_in).astype(jnp.bfloat16)
 
-    cuts = [128, R, KC, 1, 1, NS]
-    parts = []
-    at = 0
-    for cut in cuts:
-        parts.append(small[at : at + cut])
-        at += cut
+    more = small[2 * LANES :]
     return (
         block_out,
         d_tokens,
         gain_own,
         sum_in,
-        parts[0].T,
-        parts[1],
-        parts[2],
-        parts[3][0],
-        parts[4][0],
-        parts[5],
+        small[:LANES].T,
+        small[LANES : LANES + R],
+        more[NS : NS + KC],
+        more[NS + KC],
+        more[NS + KC + 1],
+        more[:NS],
         sum_out,
     )
 

time: 539 us -> 464 us (0.86); the launches traced: 533 us -> 464 us
  local copies, waits for them, and re-layouts: 86.2 us -> 44.6 us
  other arithmetic: 32.9 us -> 16 us
  matrix products: 31.7 us -> 23.6 us
    mul x3 -> x0, other arithmetic: 8.47 us -> none  [the longest x1 5.72 us: local(): grad_step_pre = grad_delta * -jnp.expm1(-step_size)]
    unnamed x73 -> x27, local copies, waits for them, and re-layouts: 18 us -> 10 us
    gather x2, local copies, waits for them, and re-layouts: 10.1 us -> 2.88 us  [the longest x1 2.07 us: local(): summed_gate[-size:][order]]
    dot_general x3 -> x1, matrix products: 16.1 us -> 9.27 us  [local(): branch = jnp.dot(gated, out_proj, preferred_element_type=f32).astype(bf16)]
    another operation x4 -> x0, other arithmetic: 5.4 us -> none
    dot_general x4 -> x2, matrix products: 15.6 us -> 14.3 us  [contract_rows(): lax.dot_general(left, right, (((0,), (0,)), ((), ())), preferred_element_...]
  transfers between devices with their start and end apart: 1 -> 0, of which waited for: 0 -> 0; matrix products, arithmetic and copies ran while one was open for 9% -> 0% of each run, Pallas kernels for 0% -> 0%
where the time goes in v3:
time: 464 us
  Pallas kernels  378 us (81%)
  local copies, waits for them, and re-layouts  44.6 us (10%)
  matrix products  23.6 us (5%)
  other arithmetic  16 us (3%)
    pallas_call x1, Pallas kernels, front(): pl.pallas_call(functools.partial(front_kernel, size, seq, direct), in_spe...  120 us
    pallas_call x1, Pallas kernels, back(): pl.pallas_call(functools.partial(back_kernel, size, seq), in_specs=[away]...  97 us
    pallas_call x1, Pallas kernels, scan_backward(): pl.pallas_call(functools.partial(backward_kernel, size, seq, nr, tt, ct,...  90.2 us
    pallas_call x1, Pallas kernels, scan_ends(): pl.pallas_call(functools.partial(ends_kernel, seq, nr, tt, ct, min(8, ct)...  43.6 us
    pallas_call x1, Pallas kernels, scan_forward(): pl.pallas_call(functools.partial(forward_kernel, nr, tt, ct, min(8, ct)),...  26.8 us
    dot_general x2, matrix products, contract_rows(): lax.dot_general(left, right, (((0,), (0,)), ((), ())), preferred_element_...  14.3 us
    unnamed x27, local copies, waits for them, and re-layouts  10 us

profile of v3, /device:TPU:0, one launch (start us, length us, event | category | flops | bytes accessed | tf_op | source)
XLA Modules:
  0.0 463.5 jit_solution(5819687652144731419)
XLA Ops:
  0.6 1.5 pad.13.refs_6_.refs_10_
  2.2 1.3 convert_element_type.98.refs_7_.refs_12_
  3.5 0.7 reshape.191
  4.1 1.2 slice.97
  6.0 0.0 copy-start.8
  6.0 1.2 reshape.204.refs_8_
  7.3 1.2 reshape.205.refs_9_
  8.5 0.0 copy-done.8
  8.5 120.2 %front.1 = (bf16[8,256,1536]{2,1,0:T(8,128)(2,1)}, bf16[8,256,1536]{2,1,0:T(8,128)(2,1)}, bf16[8,192,768]{2,1,0:T(8,128)(2,1)}, f32[3,2048,128]{2,1,0:T(8,128)},...) custom-call(bf16[256,1536]{1,0:T(8,128)(2,1)} %bitcast.76, ...), custom_call_target="tpu_custom_call" | custom-call | tf_op jit(solution)/shard_map/front/pallas_call | solution.py:752
  128.8 1.3 slice_convert_fusion
  130.1 0.0 copy-done.9
  130.1 0.6 exponential_negate_fusion
  130.7 43.6 %scan_ends.1.carry_ref.refs_6_ = f32[2,16,8,384]{3,2,1,0:T(8,128)} custom-call(f32[3,2048,128]{2,1,0:T(8,128)} %get-tuple-element.59.delta_in.refs_0_.refs_2_, f32[3,2048,128]{2,1,0:T(8,128)} %get-tuple-element.60.x_in.refs_1_, f32[3,2048,128]{2,1,0:T(8,128)} %get-tuple-element.61.gy_in.refs_2_, f32[2048,128]{1,0:T(8,128)} %get-tuple-element.62.proj_ref.refs_4_, ...), custom_call_target="tpu_custom_call" | custom-call | tf_op jit(solution)/shard_map/scan_ends/pallas_call | solution.py:109
  174.3 26.8 %scan_forward.1 = (f32[3,2048,128]{2,1,0:T(8,128)}, bf16[256,3,128,128]{3,2,1,0:T(8,128)(2,1)}, f32[16,8,384]{2,1,0:T(8,128)}) custom-call(f32[3,2048,128]{2,1,0:T(8,128)} %get-tuple-element.59.delta_in.refs_0_.refs_2_, f32[3,2048,128]{2,1,0:T(8,128)} %get-tuple-element.60.x_in.refs_1_, f32[2048,128]{1,0:T(8,128)} %get-tuple-element.62.proj_ref.refs_4_, ...), custom_call_target="tpu_custom_call" | custom-call | tf_op jit(solution)/shard_map/scan_forward/pallas_call | solution.py:205
  201.1 3.6 copy.30
  204.6 3.7 copy.36
  208.4 0.0 copy-done
  208.4 4.0 multiply_convert_fusion.refs_7_
  212.4 0.0 copy-start.4
  212.4 7.9 %fusion.2 = bf16[1536,384]{1,0:T(8,128)(2,1)} fusion(bf16[8,256,1536]{2,1,0:T(8,128)(2,1)} %get-tuple-element.69, bf16[8,256,384]{2,1,0:T(8,128)(2,1)S(1)} %multiply_convert_fusion.refs_7_), kind=kOutput, calls=%fused_computation.11 | convolution fusion | flops 2416508928 | bytes 9043968 | tf_op jit(solution)/shard_map/dot_general | solution.py:1407
  220.3 0.0 copy-done.4
  220.3 2.4 copy.34
  222.7 4.0 fusion.1
  226.7 0.9 copy.35
  227.6 0.5 copy.44
  228.1 6.4 %convolution_convert_fusion.1.refs_9_ = bf16[384,1536]{1,0:T(8,128)(2,1)} fusion(bf16[2048,384]{0,1:T(8,128)(2,1)S(1)} %bitcast.87, bf16[2048,1536]{1,0:T(8,128)(2,1)} %bitcast.90), kind=kOutput, calls=%fused_computation.12 | convolution fusion | flops 2416508928 | bytes 9043968 | tf_op jit(solution)/shard_map/dot_general | solution.py:1407
  234.5 3.6 copy.31
  238.0 4.9 %copy.43 = f32[48,8,8,256]{3,1,2,0:T(8,128)} copy(f32[48,8,8,256]{3,2,1,0:T(8,128)} %bitcast.73) | data formatting | bytes 6291456
  243.0 2.4 copy.32
  245.3 9.3 %convolution_convert_fusion = bf16[2048,1536]{1,0:T(8,128)(2,1)} fusion(bf16[384,1536]{1,0:T(8,128)(2,1)} %refs_4_.1, f32[2048,384]{0,1:T(8,128)} %copy.32, f32[2048,384]{0,1:T(8,128)} %bitcast.84), kind=kOutput, calls=%fused_computation.2 | convolution fusion | flops 2423783424 | bytes 13762560 | tf_op jit(solution)/shard_map/dot_general | solution.py:1472
  254.6 90.2 %scan_backward.1 = (f32[3,2048,128]{2,1,0:T(8,128)}, f32[3,2048,128]{2,1,0:T(8,128)}, f32[2048,128]{1,0:T(8,128)}, f32[16,8,384]{2,1,0:T(8,128)}, bf16[256,1536]...) custom-call(f32[3,2048,128]{2,1,0:T(8,128)} %get-tuple-element.59.delta_in.refs_0_.refs_2_, ...), custom_call_target="tpu_custom_call" | custom-call | tf_op jit(solution)/shard_map/scan_backward/pallas_call | solution.py:1126
  344.8 97.0 %back.1 = (bf16[256,1536]{1,0:T(8,128)(2,1)}, bf16[19,96,384]{2,1,0:T(8,128)(2,1)}) custom-call(f32[3,2048,128]{2,1,0:T(8,128)} %get-tuple-element.72.refs_0_, f32[3,2048,128]{2,1,0:T(8,128)} %get-tuple-element.73.refs_1_, f32[3,2048,128]{2,1,0:T(8,128)} %get-tuple-element.59.delta_in.refs_0_.refs_2_, bf16[2048,1536]{1,0:T(8,128)(2,1)} %bitcast.78, ...), custom_call_target="tpu_custom_call" | custom-call | tf_op jit(solution)/shard_map/back/pallas_call | solution.py:1381
  441.8 1.4 slice.83
  443.3 0.8 gather_fusion
  444.1 2.9 fusion.14
  447.0 2.1 gather_fusion.1
  449.0 0.3 convert_bitcast_fusion
  449.3 0.0 copy-start.2
  449.4 0.5 copy.45
  449.9 0.0 copy-start.1
  449.9 1.4 copy-done.2
  451.4 0.6 multiply_reduce_fusion
  451.9 0.2 copy-done.1
  452.1 0.0 copy-done.10
  452.1 0.6 convert_divide_fusion
  452.7 0.2 convert_bitcast_fusion.1
  452.8 1.5 copy.39
  454.4 0.0 copy-start.3
  454.4 0.0 copy-start.5
  454.4 0.0 copy-start.6
  454.4 1.6 copy.46
  456.0 1.0 convert_reduce_fusion
  456.9 0.1 reshape.208
  457.0 0.4 fusion.4
  457.5 0.0 copy-done.6
  457.5 0.0 copy-done.7
  457.5 1.7 fusion.9
  459.2 1.0 slice.85
  460.1 0.1 bitcast_convert_fusion
  460.2 0.8 copy.40
  461.0 0.7 slice.99
  461.7 0.6 slice.103
  462.3 0.6 slice.100
  462.9 0.6 slice_reduce_fusion
  (12 shorter events, 0.1 us)
Async XLA Ops:
  6.0 2.5 copy-start.8
  8.5 121.6 %copy-start.9 = (bf16[16,384]{1,0:T(8,128)(2,1)S(1)}, bf16[16,384]{1,0:T(8,128)(2,1)}, u32[]{:S(2)}) copy-start(bf16[16,384]{1,0:T(8,128)(2,1)} %param.26) | copy-start | bytes 36868
  204.6 3.7 copy-start
  212.4 7.9 %copy-start.4 = (bf16[8,256,384]{2,1,0:T(8,128)(2,1)}, bf16[8,256,384]{2,1,0:T(8,128)(2,1)S(1)}, u32[]{:S(2)}) copy-start(bf16[8,256,384]{2,1,0:T(8,128)(2,1)S(1)} %multiply_convert_fusion.refs_7_) | copy-start | bytes 4718596
  449.3 2.0 copy-start.2
  449.9 2.2 copy-start.1
  451.3 0.8 copy-start.10
  454.4 2.7 copy-start.3
  454.4 2.6 copy-start.5
  454.4 3.1 copy-start.6
  454.4 3.1 copy-start.7

commit v4 on v3

--- a/solution.py
+++ b/solution.py
@@ -44,187 +44,6 @@
         copies.append(pltpu.make_async_copy(source, target, sems.at[i]))
         copies[-1].start()
     return copies
-
-
-def ends_kernel(
-    seq, nr, tt, ct, uu, delta_in, x_in, gy_in, proj_ref, a_ref, alive_ref, carry_ref,
-    out_ref, mail, land, carry_sems, sel, bc, delta_ref, x_ref, gy_ref, sems,
-):
-    el = a_ref.shape[1]
-    carry = Carry(seq, out_ref, alive_ref, carry_ref, mail, land, carry_sems)
-    greet_seq(seq)
-    half = NS // 2
-    copies = copy_all((delta_in, x_in, gy_in), (delta_ref, x_ref, gy_ref), sems)
-    sel[...] = selector(LANES)
-    out_ref[0] = jnp.zeros((NS, nr, el), jnp.float32)
-    out_ref[1] = jnp.ones((NS, nr, el), jnp.float32)
-    out_ref[2] = jnp.zeros((NS, nr, el), jnp.float32)
-    for copy in copies:
-        copy.wait()
-
-    def chunk(c, none):
-        rows = pl.multiple_of(c * (ct * nr), ct * nr)
-        bc[...] = spread(proj_ref[pl.ds(rows, ct * nr), :], sel)
-        for b in range(el // LANES):
-            lanes = slice(b * LANES, (b + 1) * LANES)
-            for n0 in range(0, NS, half):
-                ns = range(n0, n0 + half)
-                rate = [jnp.broadcast_to(a_ref[n : n + 1, lanes], (nr, LANES)) for n in ns]
-
-                def steps(s, carried):
-                    state, through, back = (list(v) for v in carried)
-                    for u in range(uu):
-                        at = s * uu + u
-                        here = pl.ds(pl.multiple_of((c * ct + at) * nr, nr), nr)
-                        delta = delta_ref[b, here, :]
-                        gy = gy_ref[b, here, :]
-                        du = delta * x_ref[b, here, :]
-                        near = pl.ds(pl.multiple_of(at * nr, nr), nr)
-                        for i, n in enumerate(ns):
-                            b_at, c_at = n * LANES, (NS + n) * LANES
-                            decay = jnp.exp2(delta * rate[i])
-                            state[i] = decay * state[i] + du * bc[near, b_at : b_at + LANES]
-                            through[i] = through[i] * decay
-                            back[i] = back[i] + through[i] * (gy * bc[near, c_at : c_at + LANES])
-                    return tuple(state), tuple(through), tuple(back)
-
-                start = tuple(tuple(out_ref[k, n, :, lanes] for n in ns) for k in range(3))
-                last = lax.fori_loop(0, ct // uu, steps, start)
-                for k in range(3):
-                    for i, n in enumerate(ns):
-                        out_ref[k, n, :, lanes] = last[k][i]
-        return none
-
-    lax.fori_loop(0, tt // ct, chunk, 0)
-    carry.both()
-    carry.drain()
-
-
-def scan_ends(delta, x, gy, proj, rate, alive, nr, tt, seq):
-    el = rate.shape[1]
-    ct = math.gcd(tt, 32)
-    here = pl.BlockSpec(memory_space=pltpu.VMEM)
-    away = pl.BlockSpec(memory_space=pl.ANY)
-    blocks = pltpu.VMEM((el // LANES, nr * tt, LANES), jnp.float32)
-    return pl.pallas_call(
-        functools.partial(ends_kernel, seq, nr, tt, ct, min(8, ct)),
-        in_specs=[away] * 3 + [here] * 3,
-        out_specs=here,
-        out_shape=jax.ShapeDtypeStruct((2, NS, nr, el), jnp.float32),
-        scratch_shapes=[pltpu.VMEM((3, NS, nr, el), jnp.float32)]
-        + Carry.scratch((NS, nr, el))
-        + [
-            pltpu.VMEM((LANES, 2 * NS * LANES), jnp.bfloat16),
-            pltpu.VMEM((ct * nr, 2 * NS * LANES), jnp.float32),
-            blocks,
-            blocks,
-            blocks,
-            pltpu.SemaphoreType.DMA((3,)),
-        ],
-        compiler_params=pltpu.CompilerParams(
-            vmem_limit_bytes=56 * MIB, collective_id=2, has_side_effects=True
-        ),
-        name="scan_ends",
-    )(delta, x, gy, proj, rate, alive)
-
-
-def forward_kernel(
-    nr, tt, ct, uu, delta_in, x_in, proj_ref, a_ref, carry_ref,
-    y_out, hist_out, last_ref, sel, bc, hist, delta_ref, x_ref, y_ref, sems, out_sem, hist_sems,
-):
-    el = a_ref.shape[1]
-    blocks = el // LANES
-    copies = copy_all((delta_in, x_in), (delta_ref, x_ref), sems)
-    sel[...] = selector(LANES)
-    last_ref[...] = carry_ref[0]
-    for copy in copies:
-        copy.wait()
-
-    def store(c):
-        slot = lax.rem(c, 2)
-        return pltpu.make_async_copy(hist.at[slot], hist_out.at[pl.ds(c * ct, ct)], hist_sems.at[slot])
-
-    def forward(c, none):
-        slot = lax.rem(c, 2)
-
-        @pl.when(c >= 2)
-        def _():
-            store(c - 2).wait()
-
-        rows = pl.multiple_of(c * (ct * nr), ct * nr)
-        bc[...] = spread(proj_ref[pl.ds(rows, ct * nr), :], sel)
-        for b in range(blocks):
-            lanes = slice(b * LANES, (b + 1) * LANES)
-            rate = [jnp.broadcast_to(a_ref[n : n + 1, lanes], (nr, LANES)) for n in range(NS)]
-
-            def steps(s, carried):
-                state = list(carried)
-                for u in range(uu):
-                    at = s * uu + u
-                    here = pl.ds(pl.multiple_of((c * ct + at) * nr, nr), nr)
-                    delta = delta_ref[b, here, :]
-                    du = delta * x_ref[b, here, :]
-                    near = pl.ds(pl.multiple_of(at * nr, nr), nr)
-                    y = None
-                    for n in range(NS):
-                        if n % 2 == 0:
-                            both = jnp.concatenate([state[n], state[n + 1]], axis=0)
-                            hist[slot, at, b, pl.ds(n * nr, 2 * nr), :] = both.astype(jnp.bfloat16)
-                        b_at, c_at = n * LANES, (NS + n) * LANES
-                        decay = jnp.exp2(delta * rate[n])
-                        state[n] = decay * state[n] + du * bc[near, b_at : b_at + LANES]
-                        term = state[n] * bc[near, c_at : c_at + LANES]
-                        y = term if y is None else y + term
-                    y_ref[b, here, :] = y
-                return tuple(state)
-
-            start = tuple(last_ref[n, :, lanes] for n in range(NS))
-            last = lax.fori_loop(0, ct // uu, steps, start)
-            for n in range(NS):
-                last_ref[n, :, lanes] = last[n]
-        store(c).start()
-        return none
-
-    count = tt // ct
-    lax.fori_loop(0, count, forward, 0)
-    copies = copy_all((y_ref,), (y_out,), out_sem)
-    for c in range(max(0, count - 2), count):
-        store(c).wait()
-    for copy in copies:
-        copy.wait()
-
-
-def scan_forward(delta, x, proj, rate, carry, nr, tt):
-    el = rate.shape[1]
-    blocks = el // LANES
-    ct = math.gcd(tt, 32)
-    here = pl.BlockSpec(memory_space=pltpu.VMEM)
-    away = pl.BlockSpec(memory_space=pl.ANY)
-    f32, bf16 = jnp.float32, jnp.bfloat16
-    scan = (blocks, nr * tt, LANES)
-    return pl.pallas_call(
-        functools.partial(forward_kernel, nr, tt, ct, min(8, ct)),
-        in_specs=[away] * 2 + [here] * 3,
-        out_specs=[away] * 2 + [here],
-        out_shape=[
-            jax.ShapeDtypeStruct(scan, f32),
-            jax.ShapeDtypeStruct((tt, blocks, NS * nr, LANES), bf16),
-            jax.ShapeDtypeStruct((NS, nr, el), f32),
-        ],
-        scratch_shapes=[
-            pltpu.VMEM((LANES, 2 * NS * LANES), bf16),
-            pltpu.VMEM((ct * nr, 2 * NS * LANES), f32),
-            pltpu.VMEM((2, ct, blocks, NS * nr, LANES), bf16),
-            pltpu.VMEM(scan, f32),
-            pltpu.VMEM(scan, f32),
-            pltpu.VMEM(scan, f32),
-            pltpu.SemaphoreType.DMA((2,)),
-            pltpu.SemaphoreType.DMA((1,)),
-            pltpu.SemaphoreType.DMA((2,)),
-        ],
-        compiler_params=pltpu.CompilerParams(vmem_limit_bytes=56 * MIB),
-        name="scan_forward",
-    )(delta, x, proj, rate, carry)
 
 
 MESH = pl.DeviceIdType.MESH
@@ -330,7 +149,7 @@
 
     def hop(self, way):
         first, last = ((0, self.seq - 1), (self.seq - 1, 0))[way]
-        alive = self.alive[...][None]
+        alive = self.alive[:, 0:1][None]
 
         @pl.when(self.place == first)
         def _():
@@ -351,16 +170,9 @@
             self.mail[way] = leaving.astype(jnp.bfloat16)
             self.copy(way).start()
 
-    def both(self):
-        @pl.when(self.place < self.seq // 2)
-        def _():
-            self.hop(0)
-            self.hop(1)
-
-        @pl.when(self.place >= self.seq // 2)
-        def _():
-            self.hop(1)
-            self.hop(0)
+    def turn(self, way, t):
+        behind = (self.place, self.seq - 1 - self.place)[way]
+        pl.when(behind == t)(functools.partial(self.hop, way))
 
     def drain(self):
         for way, last in ((0, self.seq - 1), (1, 0)):
@@ -506,22 +318,28 @@
             copy.wait_send()
 
 
-def front_kernel(size, seq, direct, *refs):
-    (tokens, cot, notes, w_local, out_w, x_w, dt_w, taps_ref, bias_ref, dt_bias_ref) = refs[:10]
+def front_kernel(size, seq, direct, ct, uu, *refs):
+    (tokens, cot, notes, w_local, out_w, x_w, dt_w, taps_ref, bias_ref, dt_bias_ref, a_ref) = refs[:11]
     (
-        normed_out, cot_out, w_out, x_out, delta_out, gy_out, pre_out, gate_out, gg_out, cext_out,
-        proj_ref, rank_ref, all_notes,
-    ) = refs[10:23]
+        normed_out, w_out, x_out, delta_out, gy_out, cext_out, hist_out, branch_out, dout_out, dwg_out, ggp_out,
+        proj_ref, rank_ref, all_notes, last_ref, leaving_ref,
+    ) = refs[11:27]
     (
-        tok, normed, cot_s, wc, wg, cext, pre, xb, x_s, delta_s, gy_s, gate_s, gg_s, gain_ref,
-    ) = refs[23:37]
-    token_sems, cot_sems = refs[37:40], refs[40:43]
-    part, near, total, mail, far, out, sems = refs[43:50]
-    note_send, note_recv, wc_send, wc_recv, wg_send, wg_recv, halo_send, halo_recv, out_sems = refs[50:]
+        tok, cot_s, wc, wg, cext, xb, x_s, delta_s, gy_s, gate_s, gg_s, gain_ref, alive_ref, sel, bc, ends, entered,
+        delta_sum, hist, y_s, gated, ggp, branch_s, turned, d_stage, w_stage,
+    ) = refs[27:53]
+    token_sems, cot_sems = refs[53:56], refs[56:59]
+    part, near, total, mail, far, out, sems = refs[59:66]
+    carry = Carry(seq, ends, alive_ref, entered, *refs[66:69])
+    (
+        note_send, note_recv, wc_send, wc_recv, wg_send, wg_recv, halo_send, halo_recv, out_sems, hist_sems, branch_sems,
+    ) = refs[69:]
+    normed = tok
     me, parity, partner, others = row_peers(size)
     place = lax.axis_index("seq")
     tt, width = tokens.shape
     share, el = wc.shape[1:]
+    nr = size
     blocks = el // LANES
     half = size // 2
     f32, bf16 = jnp.float32, jnp.bfloat16
@@ -565,7 +383,9 @@
     for m in range(size):
         wait_for(all_notes.at[flip(me, m)], note_recv.at[m])
     for p in range(size):
-        gain_ref[:, p * share : (p + 1) * share] = all_notes[p, 0:1, :share].astype(f32)
+        note = all_notes[p].astype(f32)
+        gain_ref[:, p * share : (p + 1) * share] = note[0:1, :share]
+        alive_ref[p : p + 1, :] = note[1:2, :LANES]
 
     def norm(p, base, rows):
         def body(span):
@@ -581,11 +401,15 @@
 
     token_rows.own()
     norm(me, 0, tt)
+    sel[...] = selector(LANES)
     for k in range(token_rows.steps):
-        token_rows.step(k, norm_half)
+        token_rows.step(k)
     cot_rows.start()
     sent += swap(1, wg, wg_send, wg_recv)
     token_rows.paired(norm_half)
+    token_rows.drain()
+    for m in masks_of(token_rows.orders[0])[1:]:
+        norm(flip(me, m), 0, tt)
     swapped(wc, wc_recv)
 
     @pl.when(place == 0)
@@ -629,15 +453,14 @@
             value = bias_ref[...]
             for k in range(KC):
                 value = value + taps_ref[k : k + 1, :] * ext[16 - KC + 1 + k : 16 - KC + 1 + k + tile]
-            pre[p, span, :] = value
             x = (value / (1.0 + jnp.exp(-value))).astype(bf16)
-            xb[p, span, :] = x
+            xb[span, :] = x
             for b in range(blocks):
                 there = pl.ds(p + span.start * size, tile, stride=size)
                 x_s[b, there, :] = x[:, b * LANES : (b + 1) * LANES].astype(f32)
 
         by_tiles(tt, tile, body)
-        value = jnp.dot(xb[p], x_w[...], preferred_element_type=f32)
+        value = jnp.dot(xb[...], x_w[...], preferred_element_type=f32)
 
         @pl.when(i < half)
         def _():
@@ -655,7 +478,6 @@
 
     lax.fori_loop(0, size, conv, 0)
     put(cext, cext_out)
-    put(pre, pre_out)
     put(x_s, x_out)
 
     def use(p):
@@ -685,22 +507,72 @@
     put(delta_s, delta_out)
     put(wc, w_out.at[:, :, pl.ds(0, el)])
 
+    count = tt // ct
+    ends[0] = jnp.zeros((NS, nr, el), f32)
+    ends[2] = jnp.zeros((NS, nr, el), f32)
+    ends[3] = jnp.ones((NS, nr, el), f32)
+    delta_sum[...] = jnp.zeros_like(delta_sum)
+
+    def spread_chunk(c):
+        rows = pl.multiple_of(c * (ct * nr), ct * nr)
+        bc[...] = spread(proj_ref[pl.ds(rows, ct * nr), :], sel)
+
+    def token(c, at):
+        return pl.ds(pl.multiple_of((c * ct + at) * nr, nr), nr), pl.ds(pl.multiple_of(at * nr, nr), nr)
+
+    def rates(ns, lanes):
+        return [jnp.broadcast_to(a_ref[n : n + 1, lanes], (nr, LANES)) for n in ns]
+
+    def ends_forward(c, none):
+        spread_chunk(c)
+        for b in range(blocks):
+            lanes = slice(b * LANES, (b + 1) * LANES)
+            rate = rates(range(NS), lanes)
+
+            def steps(s, carried):
+                state, so_far = list(carried[:-1]), carried[-1]
+                for u in range(uu):
+                    here, close = token(c, s * uu + u)
+                    delta = delta_s[b, here, :]
+                    du = delta * x_s[b, here, :]
+                    so_far = so_far + delta
+                    for n in range(NS):
+                        b_at = n * LANES
+                        state[n] = jnp.exp2(delta * rate[n]) * state[n] + du * bc[close, b_at : b_at + LANES]
+                return tuple(state) + (so_far,)
+
+            start = tuple(ends[0, n, :, lanes] for n in range(NS)) + (delta_sum[b],)
+            last = lax.fori_loop(0, ct // uu, steps, start)
+            for n in range(NS):
+                ends[0, n, :, lanes] = last[n]
+            delta_sum[b] = last[NS]
+        return none
+
+    lax.fori_loop(0, count, ends_forward, 0)
+    for b in range(blocks):
+        lanes = slice(b * LANES, (b + 1) * LANES)
+        for n in range(NS):
+            ends[1, n, :, lanes] = jnp.exp2(delta_sum[b] * a_ref[n : n + 1, lanes])
+    carry.turn(0, 0)
+
     cot_rows.own()
     cot_rows.paired()
-    put(cot_s, cot_out)
     swapped(wg, wg_recv)
     put(wg, w_out.at[:, :, pl.ds(el, el)])
 
-    def gates(p, none):
+    def gates(p):
         weight = wg[...].reshape(size * share, el)
-        gate_s[p] = jnp.dot(normed[p], weight, preferred_element_type=f32)
-        gg_s[p] = lax.dot_general(
+        gate_s[...] = jnp.dot(normed[p], weight, preferred_element_type=f32)
+        gg_s[...] = lax.dot_general(
             cot_s[p], out_w[...], (((1,), (1,)), ((), ())), preferred_element_type=f32
         )
 
+    def grad_y(p, none):
+        gates(p)
+
         def body(span):
-            gate = gate_s[p, span, :]
-            gy = gg_s[p, span, :] * gate / (1.0 + jnp.exp(-gate))
+            gate = gate_s[span, :]
+            gy = gg_s[span, :] * gate / (1.0 + jnp.exp(-gate))
             for b in range(blocks):
                 there = pl.ds(p + span.start * size, tile, stride=size)
                 gy_s[b, there, :] = gy[:, b * LANES : (b + 1) * LANES]
@@ -708,10 +580,163 @@
         by_tiles(tt, tile, body)
         return none
 
-    lax.fori_loop(0, size, gates, 0)
+    lax.fori_loop(0, size, grad_y, 0)
     put(gy_s, gy_out)
-    put(gate_s, gate_out)
-    put(gg_s, gg_out)
+    carry.turn(0, 1)
+
+    def hops(way, c, first):
+        @pl.when(lax.rem(c, 2) == 1)
+        def _():
+            carry.turn(way, lax.div(c, 2) + first)
+
+    def ends_back(c, none):
+        spread_chunk(c)
+        for b in range(blocks):
+            lanes = slice(b * LANES, (b + 1) * LANES)
+            for n0 in (0, NS // 2):
+                ns = range(n0, n0 + NS // 2)
+                rate = rates(ns, lanes)
+
+                def steps(s, carried):
+                    through, back = (list(v) for v in carried)
+                    for u in range(uu):
+                        here, close = token(c, s * uu + u)
+                        delta = delta_s[b, here, :]
+                        gy = gy_s[b, here, :]
+                        for i, n in enumerate(ns):
+                            c_at = (NS + n) * LANES
+                            through[i] = through[i] * jnp.exp2(delta * rate[i])
+                            back[i] = back[i] + through[i] * (gy * bc[close, c_at : c_at + LANES])
+                    return tuple(through), tuple(back)
+
+                start = tuple(tuple(ends[k, n, :, lanes] for n in ns) for k in (3, 2))
+                last = lax.fori_loop(0, ct // uu, steps, start)
+                for i, n in enumerate(ns):
+                    ends[3, n, :, lanes] = last[0][i]
+                    ends[2, n, :, lanes] = last[1][i]
+        hops(0, c, 2)
+        return none
+
+    lax.fori_loop(0, count, ends_back, 0)
+    for t in range(count // 2 + 2, seq):
+        carry.turn(0, t)
+    carry.turn(1, 0)
+    last_ref[...] = entered[0]
+
+    def store_hist(c):
+        slot = lax.rem(c, 2)
+        return pltpu.make_async_copy(hist.at[slot], hist_out.at[pl.ds(c * ct, ct)], hist_sems.at[slot])
+
+    def forward(c, none):
+        slot = lax.rem(c, 2)
+
+        @pl.when(c >= 2)
+        def _():
+            store_hist(c - 2).wait()
+
+        spread_chunk(c)
+        for b in range(blocks):
+            lanes = slice(b * LANES, (b + 1) * LANES)
+            rate = rates(range(NS), lanes)
+
+            def steps(s, carried):
+                state = list(carried)
+                for u in range(uu):
+                    at = s * uu + u
+                    here, close = token(c, at)
+                    delta = delta_s[b, here, :]
+                    du = delta * x_s[b, here, :]
+                    y = None
+                    for n in range(NS):
+                        if n % 2 == 0:
+                            both = jnp.concatenate([state[n], state[n + 1]], axis=0)
+                            hist[slot, at, b, pl.ds(n * nr, 2 * nr), :] = both.astype(bf16)
+                        b_at, c_at = n * LANES, (NS + n) * LANES
+                        decay = jnp.exp2(delta * rate[n])
+                        state[n] = decay * state[n] + du * bc[close, b_at : b_at + LANES]
+                        term = state[n] * bc[close, c_at : c_at + LANES]
+                        y = term if y is None else y + term
+                    y_s[b, here, :] = y
+                return tuple(state)
+
+            last = lax.fori_loop(0, ct // uu, steps, tuple(last_ref[n, :, lanes] for n in range(NS)))
+            for n in range(NS):
+                last_ref[n, :, lanes] = last[n]
+        store_hist(c).start()
+        hops(1, c, 1)
+        return none
+
+    lax.fori_loop(0, count, forward, 0)
+    for t in range(count // 2 + 1, seq):
+        carry.turn(1, t)
+    leaving_ref[...] = entered[1]
+
+    def store_branch(i):
+        slot = lax.rem(i, 2)
+        return pltpu.make_async_copy(branch_s.at[slot], branch_out.at[i], branch_sems.at[slot])
+
+    def turn(value, p):
+        columns = pl.ds(pl.multiple_of(p * tt, tt), tt)
+        turned[:, columns] = jnp.transpose(value.astype(f32)).astype(bf16)
+
+    def products(p, none):
+        gates(p)
+
+        def body(span):
+            there = pl.ds(p + span.start * size, tile, stride=size)
+            y = jnp.concatenate([y_s[b, there, :] for b in range(blocks)], axis=1)
+            gate = gate_s[span, :]
+            sig = 1.0 / (1.0 + jnp.exp(-gate))
+            gated[span, :] = (y * gate * sig).astype(bf16)
+            ggp[p, span, :] = (gg_s[span, :] * y * sig * (1.0 + gate * (1.0 - sig))).astype(bf16)
+
+        by_tiles(tt, tile, body)
+
+        @pl.when(p >= 2)
+        def _():
+            store_branch(p - 2).wait()
+
+        branch = jnp.dot(gated[...], out_w[...], preferred_element_type=f32)
+        branch_s[lax.rem(p, 2)] = branch.astype(bf16)
+        store_branch(p).start()
+        turn(gated[...], p)
+        return none
+
+    lax.fori_loop(0, size, products, 0)
+    put(ggp, ggp_out)
+    wide = 384
+    group = wide // share
+
+    def out_weights(j, none):
+        columns = pl.ds(pl.multiple_of(j * wide, wide), wide)
+        right = cot_s[:, :, columns].reshape(size * tt, wide)
+        d_stage[:, columns] = jnp.dot(turned[...], right, preferred_element_type=f32).astype(bf16)
+        return none
+
+    lax.fori_loop(0, width // wide, out_weights, 0)
+    put(d_stage, dout_out)
+
+    def turn_gate(p, none):
+        turn(ggp[p], p)
+        return none
+
+    lax.fori_loop(0, size, turn_gate, 0)
+
+    def gate_weights(j, none):
+        columns = pl.ds(pl.multiple_of(j * wide, wide), wide)
+        right = normed[:, :, columns].reshape(size * tt, wide)
+        value = jnp.transpose(jnp.dot(turned[...], right, preferred_element_type=f32)).astype(bf16)
+        for g in range(group):
+            w_stage[j * group + g] = value[g * share : (g + 1) * share, :]
+        return none
+
+    lax.fori_loop(0, width // wide, gate_weights, 0)
+    put(w_stage, dwg_out)
+    for c in range(max(0, count - 2), count):
+        store_hist(c).wait()
+    for p in range(size - 2, size):
+        store_branch(p).wait()
+    carry.drain()
 
     for i in range(size):
 
@@ -719,7 +744,6 @@
         def _(i=i):
             halo(i, i).wait_send()
 
-    token_rows.drain()
     cot_rows.drain()
     for copy in sent:
         copy.wait_send()
@@ -727,43 +751,52 @@
         copy.wait()
 
 
-def front(tokens, cot, notes, w_local, out_w, x_w, dt_w, taps, bias, dt_bias, size, seq, direct):
+def front(tokens, cot, notes, w_local, out_w, x_w, dt_w, taps, bias, dt_bias, rate, size, seq, direct):
     tt, width = tokens.shape
     el = out_w.shape[0]
     share = width // size
     blocks = el // LANES
+    ct = math.gcd(tt, 32)
     away = pl.BlockSpec(memory_space=pl.ANY)
     here = pl.BlockSpec(memory_space=pltpu.VMEM)
     f32, bf16 = jnp.float32, jnp.bfloat16
-    rows, scan = (size, tt, width), (blocks, tt * size, LANES)
+    rows, scan, states = (size, tt, width), (blocks, tt * size, LANES), (NS, size, el)
     channels, ext = (size, tt, el), (size, tt + 16, el)
+    weights = (size, share, el)
     shapes = [
-        (rows, bf16), (rows, bf16), ((size, share, 2 * el), bf16), (scan, f32), (scan, f32), (scan, f32),
-        (channels, f32), (channels, f32), (channels, f32), (ext, bf16),
-        ((tt * size, LANES), f32), ((size, tt, LANES), bf16), ((size,) + notes.shape, bf16),
+        (rows, bf16), ((size, share, 2 * el), bf16), (scan, f32), (scan, f32), (scan, f32), (ext, bf16),
+        ((tt, blocks, NS * size, LANES), bf16), (rows, bf16), ((el, width), bf16), (weights, bf16), (channels, bf16),
+        ((tt * size, LANES), f32), ((size, tt, LANES), bf16), ((size,) + notes.shape, bf16), (states, f32),
+        (states, f32),
     ]
-    weights = (size, share, el)
     scratch = [
-        (rows, bf16), (rows, bf16), (rows, bf16), (weights, bf16), (weights, bf16), (ext, bf16),
-        (channels, f32), (channels, bf16), (scan, f32), (scan, f32), (scan, f32),
-        (channels, f32), (channels, f32), ((1, width), f32),
+        (rows, bf16), (rows, bf16), (weights, bf16), (weights, bf16), (ext, bf16), ((tt, el), bf16), (scan, f32),
+        (scan, f32), (scan, f32), ((tt, el), f32), ((tt, el), f32), ((1, width), f32), ((size, LANES), f32),
+        ((LANES, 2 * NS * LANES), bf16), ((ct * size, 2 * NS * LANES), f32), ((4,) + states, f32), ((2,) + states, f32),
+        ((blocks, size, LANES), f32), ((2, ct, blocks, NS * size, LANES), bf16), (scan, f32), ((tt, el), bf16), (channels, bf16),
+        ((2, tt, width), bf16), ((el, size * tt), bf16), ((el, width), bf16), (weights, bf16),
     ]
     one = pltpu.SemaphoreType.DMA((size,))
     return pl.pallas_call(
-        functools.partial(front_kernel, size, seq, direct),
-        in_specs=[away] * 4 + [here] * 6,
-        out_specs=[away] * 10 + [here] * 3,
+        functools.partial(front_kernel, size, seq, direct, ct, min(8, ct)),
+        in_specs=[away] * 4 + [here] * 7,
+        out_specs=[away] * 11 + [here] * 5,
         out_shape=[jax.ShapeDtypeStruct(*v) for v in shapes],
         scratch_shapes=[pltpu.VMEM(*v) for v in scratch]
         + RowGather.sems(size) * 2
         + sum_scratch(size, tt)
+        + Carry.scratch(states)
         + [one] * 8
-        + [pltpu.SemaphoreType.DMA((size + 10,))],
+        + [
+            pltpu.SemaphoreType.DMA((size + 9,)),
+            pltpu.SemaphoreType.DMA((2,)),
+            pltpu.SemaphoreType.DMA((2,)),
+        ],
         compiler_params=pltpu.CompilerParams(
-            vmem_limit_bytes=62 * MIB, collective_id=0, has_side_effects=True
+            vmem_limit_bytes=63 * MIB, collective_id=0, has_side_effects=True
         ),
         name="front",
-    )(tokens, cot, notes, w_local, out_w, x_w, dt_w, taps, bias, dt_bias)
+    )(tokens, cot, notes, w_local, out_w, x_w, dt_w, taps, bias, dt_bias, rate)
 
 
 class RowScatter:
@@ -1015,7 +1048,7 @@
     fold_row = lax.broadcasted_iota(jnp.int32, fold.shape, 0) // LANES
     fold_col = lax.broadcasted_iota(jnp.int32, fold.shape, 1)
     fold[...] = (fold_row + R == fold_col).astype(jnp.bfloat16)
-    state_ref[...] = carry_ref[1]
+    state_ref[...] = carry_ref[...]
     after_ref[...] = last_ref[...]
     grate_ref[...] = jnp.zeros_like(grate_ref)
     for copy in copies:
@@ -1166,17 +1199,17 @@
 
 
 def back_kernel(size, seq, *refs):
-    gdelta_in, gx_in, delta_in, normed_in, w_in, pre_in, cext_in, ggp_in, gbc_in = refs[:9]
-    rank_ref, dt_w, x_w, taps_ref, rate_ref, grate_ref = refs[9:15]
+    gdelta_in, gx_in, delta_in, normed_in, w_in, cext_in, ggp_in, gbc_in = refs[:8]
+    rank_ref, dt_w, x_w, taps_ref, bias_ref, rate_ref, grate_ref = refs[8:15]
     own, sums = refs[15:17]
     (
-        gdelta, gx, delta, normed, wv, pre, cext, gmix, gbc, low, gcp, turned, w_stage, acc_x, acc_dt, acc,
+        gdelta, gx, delta, normed, wv, cext, gmix, gbc, low, gcp, turned, w_stage, acc_x, acc_dt, acc,
         small, hmail, hland, stage,
-    ) = refs[17:37]
-    part, near, total, mail, far, out, sems = refs[37:44]
-    scatter = RowScatter(size, None, *refs[44:50])
-    held, zland, zmail, fill_sem, zsend, zrecv = refs[50:56]
-    swap_send, in_sems, halo_send, halo_recv = refs[56:]
+    ) = refs[17:36]
+    part, near, total, mail, far, out, sems = refs[36:43]
+    scatter = RowScatter(size, None, *refs[43:49])
+    held, zland, zmail, fill_sem, zsend, zrecv = refs[49:55]
+    swap_send, in_sems, halo_send, halo_recv = refs[55:]
     chain = SeqSum(seq, 2, held, zland, zmail, fill_sem, zsend, zrecv)
     me, parity, partner, others = row_peers(size)
     place = lax.axis_index("seq")
@@ -1189,8 +1222,8 @@
     nt = (((1,), (1,)), ((), ()))
     tn = (((0,), (0,)), ((), ()))
     copies = copy_all(
-        (gdelta_in, delta_in, gbc_in, pre_in, cext_in, gx_in, ggp_in, w_in, normed_in),
-        (gdelta, delta, gbc, pre, cext, gx, gmix.at[:, :, pl.ds(el, el)], wv, normed),
+        (gdelta_in, delta_in, gbc_in, cext_in, gx_in, ggp_in, w_in, normed_in),
+        (gdelta, delta, gbc, cext, gx, gmix.at[:, :, pl.ds(el, el)], wv, normed),
         in_sems,
     )
     greet_rows_and_seq(size, seq)
@@ -1255,12 +1288,14 @@
             value = lax.dot_general(out[p, span, :], x_w[...], nt, preferred_element_type=f32)
             there = pl.ds(p + span.start * size, 32, stride=size)
             value = value + jnp.concatenate([gx[b, there, :] for b in range(blocks)], axis=1)
-            here = pre[p, span, :]
+            ext = cext[p, pl.ds(span.start, 48), :].astype(f32)
+            here = bias_ref[...]
+            for k in range(KC):
+                here = here + taps_ref[k : k + 1, :] * ext[16 - KC + 1 + k : 16 - KC + 1 + k + 32]
             sig = 1.0 / (1.0 + jnp.exp(-here))
             low[span, :] = (here * sig).astype(bf16)
             value = value * sig * (1.0 + here * (1.0 - sig))
             gcp[p, span, :] = value
-            ext = cext[p, pl.ds(span.start, 48), :].astype(f32)
             acc[KC] = acc[KC] + fold8(value)
             for k in range(KC):
                 acc[k] = acc[k] + fold8(value * ext[16 - KC + 1 + k : 16 - KC + 1 + k + 32])
@@ -1361,11 +1396,11 @@
         lax.fori_loop(0, size, halo_sent, 0)
 
 
-def back(gdelta, gx, delta, normed, w_in, pre, cext, ggp, gbc, rank, dt_w, x_w, taps, rate, grate, size, seq):
+def back(gdelta, gx, delta, normed, w_in, cext, ggp, gbc, rank, dt_w, x_w, taps, bias, rate, grate, size, seq):
     away = pl.BlockSpec(memory_space=pl.ANY)
     here = pl.BlockSpec(memory_space=pltpu.VMEM)
     f32, bf16 = jnp.float32, jnp.bfloat16
-    unused_size, tt, el = pre.shape
+    unused_size, tt, el = ggp.shape
     share = w_in.shape[1]
     width = normed.shape[1]
     piece = (share // 2, el)
@@ -1373,14 +1408,14 @@
     chunks = 2 * size + low // piece[0]
     scratch = [
         (gdelta.shape, f32), (gx.shape, f32), (delta.shape, f32), (normed.shape, bf16), (w_in.shape, bf16),
-        (pre.shape, f32), (cext.shape, bf16), ((size, tt, 2 * el), bf16), (gbc.shape, f32), ((tt, el), bf16),
+        (cext.shape, bf16), ((size, tt, 2 * el), bf16), (gbc.shape, f32), ((tt, el), bf16),
         ((size, tt + 8, el), f32), ((el, size * tt), bf16), ((size, share, el), bf16), ((LANES, el), f32),
         ((LANES, el), f32), ((KC + 2, 8, el), f32), ((low, el), bf16), ((size, 16, el), bf16),
         ((size, 16, el), bf16), ((size // 2, tt, width), bf16),
     ]
     return pl.pallas_call(
         functools.partial(back_kernel, size, seq),
-        in_specs=[away] * 9 + [here] * 6,
+        in_specs=[away] * 8 + [here] * 7,
         out_specs=[here] * 2,
         out_shape=[
             jax.ShapeDtypeStruct((tt, width), bf16),
@@ -1392,7 +1427,7 @@
         + SeqSum.scratch(chunks, piece)
         + [
             pltpu.SemaphoreType.DMA((chunks,)),
-            pltpu.SemaphoreType.DMA((9,)),
+            pltpu.SemaphoreType.DMA((8,)),
             pltpu.SemaphoreType.DMA((size,)),
             pltpu.SemaphoreType.DMA((size,)),
         ],
@@ -1400,15 +1435,7 @@
             vmem_limit_bytes=63 * MIB, collective_id=4, has_side_effects=True
         ),
         name="back",
-    )(gdelta, gx, delta, normed, w_in, pre, cext, ggp, gbc, rank, dt_w, x_w, taps, rate, grate)
-
-
-def contract_rows(left, right):
-    return lax.dot_general(left, right, (((0,), (0,)), ((), ())), preferred_element_type=jnp.float32)
-
-
-def contract_cols(left, right):
-    return lax.dot_general(left, right, (((1,), (1,)), ((), ())), preferred_element_type=jnp.float32)
+    )(gdelta, gx, delta, normed, w_in, cext, ggp, gbc, rank, dt_w, x_w, taps, bias, rate, grate)
 
 
 def local(
@@ -1444,41 +1471,22 @@
     bias = widen(conv_bias.astype(f32), 0)[None]
     rate = widen(-jnp.exp(a_log.astype(f32)), 1)
     notes = jnp.zeros((16, -(-share // 256) * 256), bf16)
-    notes = notes.at[0, :share].set(norm_gain).at[1, 0].set(1.0 - resets[0, 0].astype(bf16))
+    notes = notes.at[0, :share].set(norm_gain).at[1].set(1.0 - resets[0, 0].astype(bf16))
     (
-        normed, all_cot, w_in, x_t, delta_t, gy_t, conv_pre, gate_pre, grad_gated, conv_ext, proj_t, rank_all,
-        all_notes,
+        normed, w_in, x_t, delta_t, gy_t, conv_ext, hist, branch, grad_out_proj, grad_in_gate, grad_gate_pre, proj_t,
+        rank_all, all_notes, last, carry_back,
     ) = front(
         tokens[0], cotangent[0], notes, w_local, out_proj, x_proj, dt_pad, taps, bias,
-        widen(dt_bias.astype(f32), 0)[None], size, seq, direct,
+        widen(dt_bias.astype(f32), 0)[None], rate * LOG2E, size, seq, direct,
     )
-    normed, all_cot = normed.reshape(count, D), all_cot.reshape(count, D)
-    gate_pre, grad_gated = gate_pre.reshape(count, elp), grad_gated.reshape(count, elp)
     gain = all_notes[:, 0, :share].reshape(D).astype(f32)
-    alive = all_notes[:, 1, :1].astype(f32)
-    def by_row(value):
-        value = value.reshape(elp // LANES, tt, nr, LANES)
-        return jnp.transpose(value, (2, 1, 0, 3)).reshape(count, elp)
-
-    rate2 = rate * LOG2E
-    scanned = (delta_t, x_t, gy_t)
-    carry = scan_ends(*scanned, proj_t, rate2, alive, nr, tt, seq)
-    scan_y, hist, last = scan_forward(delta_t, x_t, proj_t, rate2, carry, nr, tt)
-    scan_y = by_row(scan_y)
-    gate_sig = jax.nn.sigmoid(gate_pre)
-    gated = (scan_y * gate_pre * gate_sig).astype(bf16)
-    grad_gate_pre = grad_gated * scan_y * gate_sig * (1.0 + gate_pre * (1.0 - gate_sig))
-    grad_gate_pre = grad_gate_pre.astype(bf16)
-    branch = jnp.dot(gated, out_proj, preferred_element_type=f32).astype(bf16)
-    grad_out_proj = contract_rows(gated, all_cot).astype(bf16)[:el]
-    grad_in_gate = contract_rows(normed, grad_gate_pre).astype(bf16).reshape(size, share, elp)
     grad_delta, grad_input, grad_bc, grate, branch_own, summed_gate = scan_backward(
-        *scanned, hist, proj_t, rate2, carry, last, branch.reshape(nr, tt, D),
-        grad_out_proj, grad_in_gate, size, seq,
+        delta_t, x_t, gy_t, hist, proj_t, rate * LOG2E, carry_back, last, branch,
+        grad_out_proj[:el], grad_in_gate, size, seq,
     )
     grad_normed, summed_conv = back(
-        grad_delta, grad_input, delta_t, normed, w_in, conv_pre, conv_ext,
-        grad_gate_pre.reshape(nr, tt, elp), grad_bc, rank_all, dt_pad, x_proj, taps, rate, grate, size, seq,
+        grad_delta, grad_input, delta_t, normed.reshape(count, D), w_in, conv_ext, grad_gate_pre, grad_bc, rank_all,
+        dt_pad, x_proj, taps, bias, rate, grate, size, seq,
     )
     piece = (share, elp)
     out_rows, out_cols = el // share, D // elp

time: 464 us -> 409 us (0.88)
  matrix products: 23.6 us -> 0 us
  local copies, waits for them, and re-layouts: 44.6 us -> 22.6 us
  other arithmetic: 16 us -> 7.3 us
    dot_general x3 -> x0, matrix products: 23.6 us -> none  [the longest x2 14.3 us: contract_rows(): lax.dot_general(left, right, (((0,), (0,)), ((), ())), preferred_element_...]
    reshape x3 -> x0, local copies, waits for them, and re-layouts: 9.65 us -> none  [the longest x1 3.72 us: by_row(): return jnp.transpose(value, (2, 1, 0, 3)).reshape(count, elp)]
    convert_element_type x3 -> x0, other arithmetic: 9.31 us -> none  [the longest x1 4.04 us: local(): grad_gate_pre = grad_gate_pre.astype(bf16)]
    unnamed x27 -> x19, local copies, waits for them, and re-layouts: 10 us -> 4.56 us
    pallas_call x3 -> x1, Pallas kernels: 191 us -> 193 us  [front(): pl.pallas_call(functools.partial(front_kernel, size, seq, direct, ct, min...]
where the time goes in v4:
time: 409 us; the launch traced here: 408 us
  Pallas kernels  377 us (92%)
  local copies, waits for them, and re-layouts  22.6 us (6%)
  other arithmetic  7.3 us (2%)
    pallas_call x1, Pallas kernels, front(): pl.pallas_call(functools.partial(front_kernel, size, seq, direct, ct, min...  193 us
    pallas_call x1, Pallas kernels, back(): pl.pallas_call(functools.partial(back_kernel, size, seq), in_specs=[away]...  95.1 us
    pallas_call x1, Pallas kernels, scan_backward(): pl.pallas_call(functools.partial(backward_kernel, size, seq, nr, tt, ct,...  87.9 us

profile of v4, /device:TPU:0, one launch (start us, length us, event | category | flops | bytes accessed | tf_op | source)
XLA Modules:
  0.0 408.0 jit_solution(17418644381702742062)
XLA Ops:
  0.6 1.3 exponential_negate_fusion
  2.0 1.5 pad.11.refs_6_.refs_9_
  3.5 1.3 convert_element_type.71.refs_7_.refs_11_
  4.8 1.2 reshape.143.refs_8_.refs_12_
  6.0 0.7 reshape.138
  6.7 1.2 slice.89
  8.6 0.0 copy-start.6
  8.6 1.2 reshape.144.refs_9_
  9.8 0.0 copy-done.6
  9.8 193.5 %front.1 = (bf16[8,256,1536]{2,1,0:T(8,128)(2,1)}, bf16[8,192,768]{2,1,0:T(8,128)(2,1)}, f32[3,2048,128]{2,1,0:T(8,128)}, f32[3,2048,128]{2,1,0:T(8,128)}, f32[3...) custom-call(bf16[256,1536]{1,0:T(8,128)(2,1)} %bitcast.35, ...), custom_call_target="tpu_custom_call" | custom-call | tf_op jit(solution)/shard_map/front/pallas_call | solution.py:780
  203.3 87.9 %scan_backward.1 = (f32[3,2048,128]{2,1,0:T(8,128)}, f32[3,2048,128]{2,1,0:T(8,128)}, f32[2048,128]{1,0:T(8,128)}, f32[16,8,384]{2,1,0:T(8,128)}, bf16[256,1536]...) custom-call(f32[3,2048,128]{2,1,0:T(8,128)} %get-tuple-element.59.refs_0_.refs_2_, f32[3,2048,128]{2,1,0:T(8,128)} %get-tuple-element.60.refs_1_, ...), custom_call_target="tpu_custom_call" | custom-call | tf_op jit(solution)/shard_map/scan_backward/pallas_call | solution.py:1159
  291.3 95.1 %back.1 = (bf16[256,1536]{1,0:T(8,128)(2,1)}, bf16[19,96,384]{2,1,0:T(8,128)(2,1)}) custom-call(f32[3,2048,128]{2,1,0:T(8,128)} %get-tuple-element.70.refs_0_, f32[3,2048,128]{2,1,0:T(8,128)} %get-tuple-element.71.refs_1_, f32[3,2048,128]{2,1,0:T(8,128)} %get-tuple-element.59.refs_0_.refs_2_, bf16[2048,1536]{1,0:T(8,128)(2,1)} %bitcast.36, ...), custom_call_target="tpu_custom_call" | custom-call | tf_op jit(solution)/shard_map/back/pallas_call | solution.py:1416
  386.4 1.4 slice.75
  387.8 0.8 gather_fusion
  388.6 2.9 fusion.9
  391.5 2.1 gather_fusion.1
  393.6 0.3 convert_bitcast_fusion
  393.9 0.0 copy-start.1
  393.9 0.5 copy.29
  394.5 0.0 copy-start
  394.5 1.4 copy-done.1
  395.9 0.0 copy-start.7
  395.9 0.6 multiply_reduce_fusion
  396.5 0.2 copy-done
  396.7 0.0 copy-done.7
  396.7 0.6 convert_divide_fusion
  397.2 0.2 convert_bitcast_fusion.1
  397.4 1.5 copy.27
  398.9 0.0 copy-start.2
  398.9 0.0 copy-start.3
  399.0 1.6 copy.30
  400.5 0.0 copy-start.4
  400.5 0.0 copy-start.5
  400.5 0.9 convert_reduce_fusion
  401.4 0.1 reshape.146
  401.5 0.0 copy-done.2
  401.5 0.0 copy-done.3
  401.5 0.4 fusion.1
  401.9 0.0 copy-done.4
  402.0 0.0 copy-done.5
  402.0 1.7 fusion.6
  403.7 1.0 slice.77
  404.6 0.1 bitcast_convert_fusion
  404.7 0.8 copy.28
  405.5 0.7 slice.91
  406.2 0.6 slice.95
  406.8 0.6 slice.92
  407.4 0.6 slice_reduce_fusion
  (7 shorter events, 0.1 us)
Async XLA Ops:
  8.6 1.3 copy-start.6
  393.9 2.0 copy-start.1
  394.5 2.2 copy-start
  395.9 0.8 copy-start.7
  398.9 2.6 copy-start.2
  398.9 2.6 copy-start.3
  400.5 1.4 copy-start.4
  400.5 1.4 copy-start.5

commit v5 on v4

--- a/solution.py
+++ b/solution.py
@@ -357,17 +357,32 @@
             return w_local.at[:, pl.ds(at, el)]
         return w_local.at[q, :, pl.ds(gate * el, el)]
 
+    cut = share // 2
+    beside = (flip(place, 1), me)
+
     def swap(gate, target, send, recv):
-        copies = []
+        there = pl.ds(pl.multiple_of(lax.rem(place, 2) * cut, cut), cut)
         for m in range(1, size):
             q = flip(me, m)
-            copies.append(remote(piece(q, gate), target.at[me], send.at[m], recv.at[m], (place, q)))
-        pltpu.make_async_copy(piece(me, gate), target.at[me], recv.at[0]).start()
-        return copies
-
-    def swapped(target, recv):
-        for m in range(size):
-            wait_for(target.at[flip(me, m)], recv.at[m])
+            remote(piece(q, gate).at[there, :], target.at[me, there, :], send.at[0, m], recv.at[0, m], (place, q))
+        pltpu.make_async_copy(piece(me, gate), target.at[me], recv.at[0, 0]).start()
+
+    def swap_on(target, send, recv):
+        there = pl.ds(pl.multiple_of(lax.rem(place, 2) * cut, cut), cut)
+        for m in range(1, size):
+            block = target.at[flip(me, m), there, :]
+            wait_for(block, recv.at[0, m])
+            remote(block, block, send.at[1, m], recv.at[1, m], beside)
+
+    def swapped(target, send, recv):
+        wait_for(target.at[me], recv.at[0, 0])
+        for m in range(1, size):
+            wait_for(target.at[flip(me, m), pl.ds(0, cut), :], recv.at[1, m])
+
+    def swap_drain(target, send):
+        for k in range(2):
+            for m in range(1, size):
+                wait_for(target.at[0, pl.ds(0, cut), :], send.at[k, m])
 
     greet_rows_and_seq(size, seq)
 
@@ -377,8 +392,8 @@
     pltpu.make_async_copy(notes, all_notes.at[me], note_recv.at[0]).start()
     token_rows = RowGather(size, tokens, tok, *token_sems)
     cot_rows = RowGather(size, cot, cot_s, *cot_sems)
+    swap(0, wc, wc_send, wc_recv)
     token_rows.start()
-    sent += swap(0, wc, wc_send, wc_recv)
 
     for m in range(size):
         wait_for(all_notes.at[flip(me, m)], note_recv.at[m])
@@ -394,23 +409,23 @@
             inv = lax.rsqrt(jnp.mean(x * x, axis=1, keepdims=True) + epsilon)
             normed[p, there, :] = (x * inv * gain_ref[...]).astype(bf16)
 
-        by_tiles(rows, 16, body)
+        by_tiles(rows, 64, body)
 
     def norm_half(h, m):
         norm(flip(me, m), h * (tt // 2), tt // 2)
 
     token_rows.own()
     norm(me, 0, tt)
+    swap_on(wc, wc_send, wc_recv)
     sel[...] = selector(LANES)
     for k in range(token_rows.steps):
         token_rows.step(k)
     cot_rows.start()
-    sent += swap(1, wg, wg_send, wg_recv)
     token_rows.paired(norm_half)
     token_rows.drain()
     for m in masks_of(token_rows.orders[0])[1:]:
         norm(flip(me, m), 0, tt)
-    swapped(wc, wc_recv)
+    swapped(wc, wc_send, wc_recv)
 
     @pl.when(place == 0)
     def _():
@@ -485,8 +500,10 @@
         rank_ref[p] = block
         proj_ref[pl.ds(p, tt, stride=size), :] = block.astype(f32)
 
+        gate_s[...] = jnp.dot(block, dt_w[...], preferred_element_type=f32)
+
         def body(span):
-            step = jnp.dot(out[p, span, :], dt_w[...], preferred_element_type=f32) + dt_bias_ref[...]
+            step = gate_s[span, :] + dt_bias_ref[...]
             delta = jnp.maximum(step, 0.0) + jnp.log1p(jnp.exp(-jnp.abs(step)))
             for b in range(blocks):
                 there = pl.ds(p + span.start * size, 64, stride=size)
@@ -495,6 +512,7 @@
         by_tiles(tt, 64, body)
 
     def between():
+        swap(1, wg, wg_send, wg_recv)
         for k in range(cot_rows.steps):
             cot_rows.step(k)
 
@@ -513,9 +531,10 @@
     ends[3] = jnp.ones((NS, nr, el), f32)
     delta_sum[...] = jnp.zeros_like(delta_sum)
 
-    def spread_chunk(c):
+    def spread_chunk(c, first, last):
         rows = pl.multiple_of(c * (ct * nr), ct * nr)
-        bc[...] = spread(proj_ref[pl.ds(rows, ct * nr), :], sel)
+        lanes = slice(first * LANES, last * LANES)
+        bc[:, lanes] = spread(proj_ref[pl.ds(rows, ct * nr), :], sel.at[:, lanes])
 
     def token(c, at):
         return pl.ds(pl.multiple_of((c * ct + at) * nr, nr), nr), pl.ds(pl.multiple_of(at * nr, nr), nr)
@@ -524,7 +543,11 @@
         return [jnp.broadcast_to(a_ref[n : n + 1, lanes], (nr, LANES)) for n in ns]
 
     def ends_forward(c, none):
-        spread_chunk(c)
+        @pl.when(c == count // 2)
+        def _():
+            swap_on(wg, wg_send, wg_recv)
+
+        spread_chunk(c, 0, NS)
         for b in range(blocks):
             lanes = slice(b * LANES, (b + 1) * LANES)
             rate = rates(range(NS), lanes)
@@ -557,7 +580,7 @@
 
     cot_rows.own()
     cot_rows.paired()
-    swapped(wg, wg_recv)
+    swapped(wg, wg_send, wg_recv)
     put(wg, w_out.at[:, :, pl.ds(el, el)])
 
     def gates(p):
@@ -590,7 +613,7 @@
             carry.turn(way, lax.div(c, 2) + first)
 
     def ends_back(c, none):
-        spread_chunk(c)
+        spread_chunk(c, NS, 2 * NS)
         for b in range(blocks):
             lanes = slice(b * LANES, (b + 1) * LANES)
             for n0 in (0, NS // 2):
@@ -634,7 +657,7 @@
         def _():
             store_hist(c - 2).wait()
 
-        spread_chunk(c)
+        spread_chunk(c, 0, 2 * NS)
         for b in range(blocks):
             lanes = slice(b * LANES, (b + 1) * LANES)
             rate = rates(range(NS), lanes)
@@ -745,6 +768,8 @@
             halo(i, i).wait_send()
 
     cot_rows.drain()
+    swap_drain(wc, wc_send)
+    swap_drain(wg, wg_send)
     for copy in sent:
         copy.wait_send()
     for copy in stores:
@@ -778,7 +803,7 @@
     ]
     one = pltpu.SemaphoreType.DMA((size,))
     return pl.pallas_call(
-        functools.partial(front_kernel, size, seq, direct, ct, min(8, ct)),
+        functools.partial(front_kernel, size, seq, direct, ct, ct),
         in_specs=[away] * 4 + [here] * 7,
         out_specs=[away] * 11 + [here] * 5,
         out_shape=[jax.ShapeDtypeStruct(*v) for v in shapes],
@@ -786,7 +811,9 @@
         + RowGather.sems(size) * 2
         + sum_scratch(size, tt)
         + Carry.scratch(states)
-        + [one] * 8
+        + [one] * 2
+        + [pltpu.SemaphoreType.DMA((2, size))] * 4
+        + [one] * 2
         + [
             pltpu.SemaphoreType.DMA((size + 9,)),
             pltpu.SemaphoreType.DMA((2,)),
@@ -905,8 +932,8 @@
 
 
 class SeqSum:
-    def __init__(self, seq, lag, held, land, mail, fill_sem, send, recv):
-        self.seq, self.lag, self.held, self.land, self.mail = seq, lag, held, land, mail
+    def __init__(self, seq, lag, held, land, fill_sem, send, recv):
+        self.seq, self.lag, self.held, self.land = seq, lag, held, land
         self.fill_sem, self.send, self.recv = fill_sem, send, recv
         self.me, self.place = lax.axis_index("rows"), lax.axis_index("seq")
         self.behind = (self.place, seq - 1 - self.place)
@@ -917,7 +944,6 @@
     def scratch(chunks, block):
         return [
             pltpu.VMEM((chunks,) + block, jnp.bfloat16),
-            pltpu.VMEM((2, chunks) + block, jnp.bfloat16),
             pltpu.VMEM((2, chunks) + block, jnp.bfloat16),
             pltpu.SemaphoreType.DMA((chunks,)),
             pltpu.SemaphoreType.DMA((2, chunks)),
@@ -947,8 +973,8 @@
                 @pl.when(self.behind[way] < self.seq - 1)
                 def _():
                     value = self.held[n].astype(jnp.float32) + self.land[way, n].astype(jnp.float32)
-                    self.mail[way, n] = value.astype(jnp.bfloat16)
-                    self.copy(n, way, self.mail.at[way, n]).start()
+                    self.land[way, n] = value.astype(jnp.bfloat16)
+                    self.copy(n, way, self.land.at[way, n]).start()
 
     def advance(self, step, total):
         first = step - self.lag * jnp.minimum(self.behind[0], self.behind[1])
@@ -972,6 +998,8 @@
                 @pl.when(there)
                 def _(ways=ways):
                     value = self.held[n].astype(jnp.float32)
+                    if len(ways) == 2:
+                        value = -value
                     for way in ways:
                         value = value + self.land[way, n].astype(jnp.float32)
                     total[n] = value.astype(jnp.bfloat16)
@@ -995,42 +1023,58 @@
                 lax.fori_loop(0, self.chunks, sent, 0)
 
 
-def fill_chunks(size, held, fill_sem, swap_send, sources, weight):
-    me, place = lax.axis_index("rows"), lax.axis_index("seq")
+def fill_chunks(held, fill_sem, source, first=0):
     rows, cols = held.shape[1:]
-    n = 0
-    for source in sources:
-        for i in range(source.shape[0] // rows):
-            for j in range(source.shape[1] // cols):
-                piece = source.at[pl.ds(i * rows, rows), pl.ds(j * cols, cols)]
+    n = first
+    if len(source.shape) == 3:
+        for j in range(source.shape[0]):
+            for i in range(source.shape[1] // rows):
+                piece = source.at[j, pl.ds(i * rows, rows), :]
                 pltpu.make_async_copy(piece, held.at[n], fill_sem.at[n]).start()
                 n += 1
+        return n
+    for i in range(source.shape[0] // rows):
+        for j in range(source.shape[1] // cols):
+            piece = source.at[pl.ds(i * rows, rows), pl.ds(j * cols, cols)]
+            pltpu.make_async_copy(piece, held.at[n], fill_sem.at[n]).start()
+            n += 1
+    return n
+
+
+def early_blocks(size):
+    return size // 4
+
+
+def swap_blocks(size, weight, slots):
+    me, place = lax.axis_index("rows"), lax.axis_index("seq")
     for m in range(size):
         q = flip(me, m)
-        for i in range(weight.shape[1] // rows):
+        parts = weight.shape[1] // slots(m, 0)[0].shape[0]
+        for i in range(parts):
+            target, recv, send = slots(m, i)
+            rows = target.shape[0]
             piece = weight.at[q, pl.ds(i * rows, rows), :]
             if m == 0:
-                pltpu.make_async_copy(piece, held.at[n], fill_sem.at[n]).start()
+                pltpu.make_async_copy(piece, target, recv).start()
             else:
-                remote(piece, held.at[n], swap_send.at[n], fill_sem.at[n], (place, q))
-            n += 1
-
-
-def drain_swap(size, held, swap_send, weight):
-    parts = weight.shape[1] // held.shape[1]
-    first = held.shape[0] - (size - 1) * parts
-    for n in range(first, held.shape[0]):
-        wait_for(held.at[n], swap_send.at[n])
+                remote(piece, target, send, recv, (place, q))
+
+
+def drain_swap(size, weight, slots):
+    for m in range(1, size):
+        for i in range(weight.shape[1] // slots(m, 0)[0].shape[0]):
+            target, unused_recv, send = slots(m, i)
+            wait_for(target, send)
 
 
 def backward_kernel(size, seq, nr, tt, ct, uu, *refs):
     delta_in, x_in, gy_in, hist_in, proj_ref, a_ref, carry_ref, last_ref, branch, out_w, gate_w = refs[:11]
-    gdelta_out, gx_out, gbc_ref, grate_ref, branch_own, total = refs[11:17]
-    sel, bc, hist, prod, state_ref, after_ref, fold, delta_ref, x_ref, gy_ref, gdelta_ref, gx_ref = refs[17:29]
-    sems, out_sems, hist_sems = refs[29:32]
-    scatter = RowScatter(size, branch, *refs[32:38])
-    held, land, mail, fill_sem, zsend, zrecv, swap_send = refs[38:]
-    chain = SeqSum(seq, 3, held, land, mail, fill_sem, zsend, zrecv)
+    gdelta_out, gx_out, gate_out, gbc_ref, grate_ref, branch_own, total = refs[11:18]
+    sel, bc, hist, prod, state_ref, after_ref, fold, delta_ref, x_ref, gy_ref, gdelta_ref, gx_ref, gate_s = refs[18:31]
+    sems, out_sems, hist_sems = refs[31:34]
+    scatter = RowScatter(size, branch, *refs[34:40])
+    chain = SeqSum(seq, 3, *refs[40:45])
+    gate_send, gate_recv, gate_sem = refs[45:]
     el = a_ref.shape[1]
     blocks = el // LANES
     count = tt // ct
@@ -1043,7 +1087,18 @@
     fetch(count - 1).start()
     greet_rows_and_seq(size, seq)
     scatter.start()
-    fill_chunks(size, held, fill_sem, swap_send, (out_w,), gate_w)
+    fill_chunks(chain.held, chain.fill_sem, out_w)
+    early = early_blocks(size)
+    halves = gate_w.shape[1] // chain.held.shape[1]
+    first = chain.chunks - early * halves
+
+    def slots(m, i):
+        if m < early:
+            n = first + m * halves + i
+            return chain.held.at[n], chain.fill_sem.at[n], gate_send.at[m, i]
+        return gate_s.at[m - early], gate_recv.at[m], gate_send.at[m, 0]
+
+    swap_blocks(size, gate_w, slots)
     sel[...] = selector(LANES)
     fold_row = lax.broadcasted_iota(jnp.int32, fold.shape, 0) // LANES
     fold_col = lax.broadcasted_iota(jnp.int32, fold.shape, 1)
@@ -1063,9 +1118,9 @@
             fetch(c - 1).start()
 
         for at_k, job in (
-            (1, functools.partial(scatter.step, 1)),
-            (count // 2, functools.partial(scatter.later, 2)),
-            (count - 2, functools.partial(scatter.finish, branch_own)),
+            (count // 8, functools.partial(scatter.step, 1)),
+            (count * 5 // 8, functools.partial(scatter.later, 2)),
+            (count - 1, functools.partial(scatter.finish, branch_own)),
         ):
             pl.when(k == at_k)(job)
 
@@ -1127,8 +1182,7 @@
                 for i, n in enumerate(ns):
                     for ref, end in zip((state_ref, grate_ref, after_ref), ends):
                         ref[n, :, lanes] = end[i]
-            if b < 2:
-                chain.advance(2 * k + b, total)
+            chain.advance(blocks * k + b, total)
         gbc_ref[pl.ds(rows, ct * nr), :] = jnp.dot(
             prod[...].astype(jnp.bfloat16), fold[...], preferred_element_type=jnp.float32
         )
@@ -1136,11 +1190,13 @@
 
     lax.fori_loop(0, count, backward, 0)
     late = copy_all((gdelta_ref, gx_ref), (gdelta_out, gx_out), out_sems)
-    done = min(2, blocks) * count if blocks > 1 else count
-    chain.run(2 * count, max(2 * count, chain.last_step), total)
+    for m in range(early, size):
+        wait_for(gate_s.at[m - early], gate_recv.at[m])
+    late += copy_all((gate_s,), (gate_out,), gate_sem)
+    chain.run(blocks * count, max(blocks * count, chain.last_step), total)
     scatter.drain()
     chain.drain()
-    drain_swap(size, held, swap_send, gate_w)
+    drain_swap(size, gate_w, slots)
     for copy in late:
         copy.wait()
 
@@ -1149,20 +1205,22 @@
     nr, tt, width = branch.shape
     el = rate.shape[1]
     blocks = el // LANES
-    ct = math.gcd(tt, 16)
+    ct = math.gcd(tt, 32)
     here = pl.BlockSpec(memory_space=pltpu.VMEM)
     away = pl.BlockSpec(memory_space=pl.ANY)
     f32, bf16 = jnp.float32, jnp.bfloat16
     scan = (blocks, nr * tt, LANES)
-    piece = gate_w.shape[1:]
-    chunks = (out_w.size + gate_w.size) // math.prod(piece)
+    piece = (gate_w.shape[1] // 2, gate_w.shape[2])
+    early = early_blocks(size)
+    chunks = out_w.size // math.prod(piece) + 2 * early
     return pl.pallas_call(
-        functools.partial(backward_kernel, size, seq, nr, tt, ct, min(8, ct)),
+        functools.partial(backward_kernel, size, seq, nr, tt, ct, ct),
         in_specs=[away] * 4 + [here] * 4 + [away] * 3,
-        out_specs=[away] * 2 + [here] * 4,
+        out_specs=[away] * 3 + [here] * 4,
         out_shape=[
             jax.ShapeDtypeStruct(scan, f32),
             jax.ShapeDtypeStruct(scan, f32),
+            jax.ShapeDtypeStruct((size - early,) + gate_w.shape[1:], bf16),
             jax.ShapeDtypeStruct((tt * nr, LANES), f32),
             jax.ShapeDtypeStruct((NS, nr, el), f32),
             jax.ShapeDtypeStruct((tt, width), bf16),
@@ -1179,13 +1237,14 @@
         ]
         + [pltpu.VMEM(scan, f32)] * 5
         + [
+            pltpu.VMEM((size - early,) + gate_w.shape[1:], bf16),
             pltpu.SemaphoreType.DMA((3,)),
             pltpu.SemaphoreType.DMA((2,)),
             pltpu.SemaphoreType.DMA((2,)),
         ]
         + RowScatter.scratch(size, tt, width)
         + SeqSum.scratch(chunks, piece)
-        + [pltpu.SemaphoreType.DMA((chunks,))],
+        + [pltpu.SemaphoreType.DMA((size, 2)), pltpu.SemaphoreType.DMA((size,)), pltpu.SemaphoreType.DMA((1,))],
         compiler_params=pltpu.CompilerParams(
             vmem_limit_bytes=62 * MIB, collective_id=3, has_side_effects=True
         ),
@@ -1199,18 +1258,18 @@
 
 
 def back_kernel(size, seq, *refs):
-    gdelta_in, gx_in, delta_in, normed_in, w_in, cext_in, ggp_in, gbc_in = refs[:8]
-    rank_ref, dt_w, x_w, taps_ref, bias_ref, rate_ref, grate_ref = refs[8:15]
-    own, sums = refs[15:17]
+    gdelta_in, gx_in, delta_in, normed_in, w_in, cext_in, ggp_in, gbc_in, gate_w = refs[:9]
+    rank_ref, dt_w, x_w, taps_ref, bias_ref, rate_ref, grate_ref = refs[9:16]
+    own, sums = refs[16:18]
     (
         gdelta, gx, delta, normed, wv, cext, gmix, gbc, low, gcp, turned, w_stage, acc_x, acc_dt, acc,
-        small, hmail, hland, stage,
-    ) = refs[17:36]
-    part, near, total, mail, far, out, sems = refs[36:43]
-    scatter = RowScatter(size, None, *refs[43:49])
-    held, zland, zmail, fill_sem, zsend, zrecv = refs[49:55]
-    swap_send, in_sems, halo_send, halo_recv = refs[55:]
-    chain = SeqSum(seq, 2, held, zland, zmail, fill_sem, zsend, zrecv)
+        small, hmail, hland, stage, gco,
+    ) = refs[18:38]
+    part, near, total, mail, far, out, sems = refs[38:45]
+    scatter = RowScatter(size, None, *refs[45:51])
+    chain = SeqSum(seq, 4, *refs[51:56])
+    held, fill_sem = chain.held, chain.fill_sem
+    swap_send, in_sems, halo_send, halo_recv = refs[56:]
     me, parity, partner, others = row_peers(size)
     place = lax.axis_index("seq")
     share, el = w_stage.shape[1:]
@@ -1226,6 +1285,7 @@
         (gdelta, delta, gbc, cext, gx, gmix.at[:, :, pl.ds(el, el)], wv, normed),
         in_sems,
     )
+    early = fill_chunks(held, fill_sem, gate_w)
     greet_rows_and_seq(size, seq)
     for ref in (acc_x, acc_dt, acc, small):
         ref[...] = jnp.zeros_like(ref)
@@ -1284,8 +1344,10 @@
         )
 
     def conv_back(p, none):
+        gco[...] = lax.dot_general(out[p], x_w[...], nt, preferred_element_type=f32)
+
         def body(span):
-            value = lax.dot_general(out[p, span, :], x_w[...], nt, preferred_element_type=f32)
+            value = gco[span, :]
             there = pl.ds(p + span.start * size, 32, stride=size)
             value = value + jnp.concatenate([gx[b, there, :] for b in range(blocks)], axis=1)
             ext = cext[p, pl.ds(span.start, 48), :].astype(f32)
@@ -1308,6 +1370,10 @@
         def _():
             halo(p).start()
 
+        @pl.when(p < early)
+        def _():
+            chain.advance(p, sums)
+
         return none
 
     lax.fori_loop(0, size, conv_back, 0)
@@ -1332,9 +1398,15 @@
         by_tiles(tt, 32, body)
         columns = pl.ds(pl.multiple_of(p * tt, tt), tt)
         turned[:, columns] = jnp.transpose(gmix[p, :, 0:el].astype(f32)).astype(bf16)
+
+        @pl.when(size + p < early)
+        def _():
+            chain.advance(size + p, sums)
+
         return none
 
     lax.fori_loop(0, size, turn, 0)
+    chain.run(2 * size, max(2 * size, early), sums)
 
     group = 384 // share
 
@@ -1354,7 +1426,14 @@
     last = [rate_sum] + [jnp.sum(acc[k], axis=0, keepdims=True) for k in range(KC + 2)]
     last.append(jnp.zeros((16 - KC - 2, el), f32))
     small[rows : rows + 32, :] = jnp.concatenate(last, axis=0).astype(bf16)
-    fill_chunks(size, held, fill_sem, swap_send, (small,), w_stage)
+    late = fill_chunks(held, fill_sem, small, early)
+    halves = share // held.shape[1]
+
+    def slots(m, i):
+        n = late + m * halves + i
+        return held.at[n], fill_sem.at[n], swap_send.at[n]
+
+    swap_blocks(size, w_stage, slots)
 
     def spread_back(i, none):
         p = crossed(me, jnp.where(i < half, 2 * i + 1, 2 * (i - half)), size)
@@ -1370,22 +1449,22 @@
         def _():
             scatter.keep[i - half] = value
 
-        chain.advance(i, sums)
+        chain.advance(early + i, sums)
         return none
 
     lax.fori_loop(0, size, spread_back, 0)
+    done = early + size
     jobs = [functools.partial(scatter.step, k) for k in range(1, scatter.steps)]
     jobs.append(functools.partial(scatter.finish, own))
-    done = size
-    for i, job in enumerate(jobs):
+    for k, job in enumerate(jobs):
         job()
-        upto = min(chain.last_step, done + chain.last_step // 4)
+        upto = min(chain.last_step, done + (chain.last_step - done) * (2 if k else 3) // 4)
         chain.run(done, upto, sums)
         done = upto
-    chain.run(done, max(done, chain.last_step), sums)
+    chain.run(done, chain.last_step, sums)
     scatter.drain()
     chain.drain()
-    drain_swap(size, held, swap_send, w_stage)
+    drain_swap(size, w_stage, slots)
 
     def halo_sent(p, none):
         halo(p).wait_send()
@@ -1396,7 +1475,9 @@
         lax.fori_loop(0, size, halo_sent, 0)
 
 
-def back(gdelta, gx, delta, normed, w_in, cext, ggp, gbc, rank, dt_w, x_w, taps, bias, rate, grate, size, seq):
+def back(
+    gdelta, gx, delta, normed, w_in, cext, ggp, gbc, rank, dt_w, x_w, taps, bias, rate, grate, gate_w, size, seq
+):
     away = pl.BlockSpec(memory_space=pl.ANY)
     here = pl.BlockSpec(memory_space=pltpu.VMEM)
     f32, bf16 = jnp.float32, jnp.bfloat16
@@ -1405,17 +1486,17 @@
     width = normed.shape[1]
     piece = (share // 2, el)
     low = small_rows(piece[0])
-    chunks = 2 * size + low // piece[0]
+    chunks = 4 * size - 2 * early_blocks(size) + low // piece[0]
     scratch = [
         (gdelta.shape, f32), (gx.shape, f32), (delta.shape, f32), (normed.shape, bf16), (w_in.shape, bf16),
         (cext.shape, bf16), ((size, tt, 2 * el), bf16), (gbc.shape, f32), ((tt, el), bf16),
         ((size, tt + 8, el), f32), ((el, size * tt), bf16), ((size, share, el), bf16), ((LANES, el), f32),
         ((LANES, el), f32), ((KC + 2, 8, el), f32), ((low, el), bf16), ((size, 16, el), bf16),
-        ((size, 16, el), bf16), ((size // 2, tt, width), bf16),
+        ((size, 16, el), bf16), ((size // 2, tt, width), bf16), ((tt, el), f32),
     ]
     return pl.pallas_call(
         functools.partial(back_kernel, size, seq),
-        in_specs=[away] * 8 + [here] * 7,
+        in_specs=[away] * 9 + [here] * 7,
         out_specs=[here] * 2,
         out_shape=[
             jax.ShapeDtypeStruct((tt, width), bf16),
@@ -1435,7 +1516,7 @@
             vmem_limit_bytes=63 * MIB, collective_id=4, has_side_effects=True
         ),
         name="back",
-    )(gdelta, gx, delta, normed, w_in, cext, ggp, gbc, rank, dt_w, x_w, taps, bias, rate, grate)
+    )(gdelta, gx, delta, normed, w_in, cext, ggp, gbc, gate_w, rank, dt_w, x_w, taps, bias, rate, grate)
 
 
 def local(
@@ -1480,22 +1561,25 @@
         widen(dt_bias.astype(f32), 0)[None], rate * LOG2E, size, seq, direct,
     )
     gain = all_notes[:, 0, :share].reshape(D).astype(f32)
-    grad_delta, grad_input, grad_bc, grate, branch_own, summed_gate = scan_backward(
+    grad_delta, grad_input, gate_blocks, grad_bc, grate, branch_own, summed_out = scan_backward(
         delta_t, x_t, gy_t, hist, proj_t, rate * LOG2E, carry_back, last, branch,
         grad_out_proj[:el], grad_in_gate, size, seq,
     )
-    grad_normed, summed_conv = back(
+    grad_normed, summed = back(
         grad_delta, grad_input, delta_t, normed.reshape(count, D), w_in, conv_ext, grad_gate_pre, grad_bc, rank_all,
-        dt_pad, x_proj, taps, bias, rate, grate, size, seq,
+        dt_pad, x_proj, taps, bias, rate, grate, gate_blocks, size, seq,
     )
-    piece = (share, elp)
-    out_rows, out_cols = el // share, D // elp
-    sum_out = summed_gate[: out_rows * out_cols].reshape(out_rows, out_cols, *piece)
+    block = (share, elp)
+    early = 2 * early_blocks(size)
+    out_rows, out_cols = 2 * el // share, D // elp
+    sum_out = summed_out[:-early].reshape(out_rows, out_cols, share // 2, elp)
     sum_out = jnp.swapaxes(sum_out, 1, 2).reshape(el, D).astype(f32)
-    small = summed_conv[: -2 * size].reshape(-1, elp)[:, :el].astype(f32)
+    rest = 2 * size - early
+    small = summed[rest : -2 * size].reshape(-1, elp)[:, :el].astype(f32)
     order = jnp.array(range(size)) ^ lax.axis_index("rows")
-    sum_in = jnp.stack([summed_conv[-2 * size :].reshape((size,) + piece)[order], summed_gate[-size:][order]])
-    sum_in = jnp.transpose(sum_in[..., :el].astype(f32), (2, 0, 1, 3)).reshape(share, 2 * E)
+    sum_gate = jnp.concatenate([summed_out[-early:], summed[:rest]])
+    sum_in = [part.reshape((size,) + block)[order] for part in (summed[-2 * size :], sum_gate)]
+    sum_in = jnp.transpose(jnp.stack(sum_in)[..., :el].astype(f32), (2, 0, 1, 3)).reshape(share, 2 * E)
     block_out = (tokens.astype(jnp.float32) + branch_own[None].astype(jnp.float32)).astype(jnp.bfloat16)
     grad_normed = grad_normed[None].astype(jnp.float32)
 

time: 409 us -> 363 us (0.89)
  Pallas kernels: 377 us -> 331 us
    pallas_call x1, Pallas kernels: 87.9 us -> 61.5 us  [scan_backward(): pl.pallas_call(functools.partial(backward_kernel, size, seq, nr, tt, ct,...]
    pallas_call x1, Pallas kernels: 193 us -> 178 us  [front(): pl.pallas_call(functools.partial(front_kernel, size, seq, direct, ct, ct)...]
where the time goes in v5:
time: 363 us; the launch traced here: 361 us
  Pallas kernels  331 us (91%)
  local copies, waits for them, and re-layouts  21.3 us (6%)
  other arithmetic  7.52 us (2%)
    pallas_call x1, Pallas kernels, front(): pl.pallas_call(functools.partial(front_kernel, size, seq, direct, ct, ct)...  178 us
    pallas_call x1, Pallas kernels, back(): pl.pallas_call(functools.partial(back_kernel, size, seq), in_specs=[away]...  92.2 us
    pallas_call x1, Pallas kernels, scan_backward(): pl.pallas_call(functools.partial(backward_kernel, size, seq, nr, tt, ct,...  61.5 us

profile of v5, /device:TPU:0, one launch (start us, length us, event | category | flops | bytes accessed | tf_op | source)
XLA Modules:
  0.0 361.4 jit_solution(15677571758029048616)
XLA Ops:
  0.6 1.3 exponential_negate_fusion
  2.0 1.5 pad.11.refs_6_.refs_10_
  3.5 1.3 convert_element_type.71.refs_7_.refs_12_
  4.8 1.2 reshape.147.refs_8_.refs_13_
  6.0 0.7 reshape.141
  6.7 1.2 slice.93
  8.6 0.0 copy-start.7
  8.6 1.2 reshape.148.refs_9_
  9.8 0.0 copy-done.7
  9.8 177.5 %front.1 = (bf16[8,256,1536]{2,1,0:T(8,128)(2,1)}, bf16[8,192,768]{2,1,0:T(8,128)(2,1)}, f32[3,2048,128]{2,1,0:T(8,128)}, f32[3,2048,128]{2,1,0:T(8,128)}, f32[3...) custom-call(bf16[256,1536]{1,0:T(8,128)(2,1)} %bitcast.36, ...), custom_call_target="tpu_custom_call" | custom-call | tf_op jit(solution)/shard_map/front/pallas_call | solution.py:805
  187.4 61.5 %scan_backward.1 = (f32[3,2048,128]{2,1,0:T(8,128)}, f32[3,2048,128]{2,1,0:T(8,128)}, bf16[6,192,384]{2,1,0:T(8,128)(2,1)}, f32[2048,128]{1,0:T(8,128)}, f32[16,...) custom-call(f32[3,2048,128]{2,1,0:T(8,128)} %get-tuple-element.60.refs_0_.refs_2_, ...), custom_call_target="tpu_custom_call" | custom-call | tf_op jit(solution)/shard_map/scan_backward/pallas_call | solution.py:1216
  248.8 92.2 %back.1 = (bf16[256,1536]{1,0:T(8,128)(2,1)}, bf16[31,96,384]{2,1,0:T(8,128)(2,1)}) custom-call(f32[3,2048,128]{2,1,0:T(8,128)} %get-tuple-element.71.refs_0_, f32[3,2048,128]{2,1,0:T(8,128)} %get-tuple-element.72.refs_1_, f32[3,2048,128]{2,1,0:T(8,128)} %get-tuple-element.60.refs_0_.refs_2_, bf16[2048,1536]{1,0:T(8,128)(2,1)} %bitcast.37, ...), custom_call_target="tpu_custom_call" | custom-call | tf_op jit(solution)/shard_map/back/pallas_call | solution.py:1497
  341.0 1.3 slice.80
  342.3 1.0 slice.79
  343.3 0.1 pad_maximum_fusion
  343.4 0.8 gather_fusion.1
  344.2 1.4 slice.78
  345.6 0.8 gather_fusion
  346.5 0.3 convert_bitcast_fusion
  346.8 0.0 copy-start.1
  346.8 0.5 copy.27
  347.3 0.0 copy-start
  347.3 1.4 copy-done.1
  348.8 0.0 copy-start.8
  348.8 0.0 copy-start.5
  348.8 0.6 multiply_reduce_fusion
  349.3 0.2 copy-done
  349.5 0.0 copy-done.8
  349.5 0.6 convert_divide_fusion
  350.1 0.4 copy-done.5
  350.5 0.1 slice.88
  350.6 0.2 convert_bitcast_fusion.1
  350.9 1.5 copy.25
  352.4 0.0 copy-start.2
  352.4 0.0 copy-start.3
  352.4 1.6 copy.28
  354.0 0.0 copy-start.4
  354.0 0.0 copy-start.6
  354.0 0.9 convert_reduce_fusion
  354.9 0.1 reshape.150
  354.9 0.0 copy-done.2
  354.9 0.0 copy-done.3
  355.0 0.4 fusion.1
  355.4 0.0 copy-done.4
  355.4 0.0 copy-done.6
  355.4 1.7 fusion.6
  357.1 1.0 slice.81
  358.1 0.1 bitcast_convert_fusion
  358.2 0.8 copy.26
  359.0 0.7 slice.95
  359.6 0.6 slice.99
  360.2 0.6 slice.96
  360.8 0.6 slice_reduce_fusion
  (7 shorter events, 0.1 us)
Async XLA Ops:
  8.6 1.3 copy-start.7
  346.8 2.0 copy-start.1
  347.3 2.2 copy-start
  348.8 0.8 copy-start.8
  348.8 1.7 copy-start.5
  352.4 2.6 copy-start.2
  352.4 2.6 copy-start.3
  354.0 1.4 copy-start.4
  354.0 1.4 copy-start.6

commit v6 on v5

--- a/solution.py
+++ b/solution.py
@@ -32,6 +32,10 @@
     row = lax.broadcasted_iota(jnp.int32, (LANES, 2 * NS * wide), 0)
     col = lax.broadcasted_iota(jnp.int32, (LANES, 2 * NS * wide), 1) // wide
     return (row == col + R).astype(jnp.bfloat16)
+
+
+def decay_rates(params):
+    return -jnp.exp(params[8 : 8 + NS, :])
 
 
 def spread(proj, sel_ref):
@@ -137,38 +141,44 @@
         return [
             pltpu.VMEM((2,) + shape, jnp.bfloat16),
             pltpu.VMEM((2,) + shape, jnp.bfloat16),
-            pltpu.SemaphoreType.DMA((2, 2)),
+            pltpu.SemaphoreType.DMA((2, 2, shape[-1] // LANES)),
         ]
 
-    def copy(self, way):
+    def copy(self, way, b):
+        lanes = pl.ds(b * LANES, LANES)
         target = (jnp.clip(self.place + 1 - 2 * way, 0, self.seq - 1), self.me)
         return pltpu.make_async_remote_copy(
-            src_ref=self.mail.at[way], dst_ref=self.land.at[way], send_sem=self.sems.at[way, 0],
-            recv_sem=self.sems.at[way, 1], device_id=target, device_id_type=MESH,
+            src_ref=self.mail.at[way, :, :, lanes], dst_ref=self.land.at[way, :, :, lanes],
+            send_sem=self.sems.at[way, 0, b], recv_sem=self.sems.at[way, 1, b], device_id=target,
+            device_id_type=MESH,
         )
 
     def hop(self, way):
         first, last = ((0, self.seq - 1), (self.seq - 1, 0))[way]
         alive = self.alive[:, 0:1][None]
 
-        @pl.when(self.place == first)
-        def _():
-            self.out[way] = jnp.zeros_like(self.out[way])
-
-        @pl.when(self.place != first)
-        def _():
-            self.copy(way).wait_recv()
-            entering = self.land[way].astype(jnp.float32)
-            self.out[way] = entering * alive if way == 0 else entering
-
-        @pl.when(self.place != last)
-        def _():
-            if way == 0:
-                leaving = self.ends[0] + self.ends[1] * self.out[0]
-            else:
-                leaving = (self.ends[2] + self.ends[1] * self.out[1]) * alive
-            self.mail[way] = leaving.astype(jnp.bfloat16)
-            self.copy(way).start()
+        for b in range(self.mail.shape[-1] // LANES):
+            lanes = slice(b * LANES, (b + 1) * LANES)
+
+            @pl.when(self.place == first)
+            def _(lanes=lanes):
+                self.out[way, :, :, lanes] = jnp.zeros(self.out.shape[1:3] + (LANES,), jnp.float32)
+
+            @pl.when(self.place != first)
+            def _(b=b, lanes=lanes):
+                self.copy(way, b).wait_recv()
+                entering = self.land[way, :, :, lanes].astype(jnp.float32)
+                self.out[way, :, :, lanes] = entering * alive if way == 0 else entering
+
+            @pl.when(self.place != last)
+            def _(b=b, lanes=lanes):
+                passed = self.ends[1, :, :, lanes] * self.out[way, :, :, lanes]
+                if way == 0:
+                    leaving = self.ends[0, :, :, lanes] + passed
+                else:
+                    leaving = (self.ends[2, :, :, lanes] + passed) * alive
+                self.mail[way, :, :, lanes] = leaving.astype(jnp.bfloat16)
+                self.copy(way, b).start()
 
     def turn(self, way, t):
         behind = (self.place, self.seq - 1 - self.place)[way]
@@ -179,7 +189,8 @@
 
             @pl.when(self.place != last)
             def _(way=way):
-                self.copy(way).wait_send()
+                for b in range(self.mail.shape[-1] // LANES):
+                    self.copy(way, b).wait_send()
 
 
 def flip(place, mask):
@@ -257,7 +268,6 @@
         self.rows = source.shape[0] // 2
         self.orders = [order[1:] for order in bit_orders(size)]
         self.steps = len(self.orders[0])
-        self.started = []
 
     @staticmethod
     def sems(size):
@@ -270,11 +280,8 @@
     def push(self, h, m, bit):
         source = self.half(h, m, self.source if m == 0 else None)
         key = (h, m | bit)
-        self.started.append(
-            remote(
-                source, self.half(h, m), self.send.at[key], self.recv.at[key],
-                (self.place, flip(self.me, bit)),
-            )
+        remote(
+            source, self.half(h, m), self.send.at[key], self.recv.at[key], (self.place, flip(self.me, bit))
         )
 
     def arrived(self, h, m):
@@ -314,23 +321,25 @@
                     use(h, m | 1)
 
     def drain(self):
-        for copy in self.started:
-            copy.wait_send()
+        for h in range(2):
+            for m in range(1, self.size):
+                wait_for(self.half(h, 0), self.send.at[h, m])
 
 
 def front_kernel(size, seq, direct, ct, uu, *refs):
-    (tokens, cot, notes, w_local, out_w, x_w, dt_w, taps_ref, bias_ref, dt_bias_ref, a_ref) = refs[:11]
+    (tokens, cot, notes, w_local, out_w, x_w, dt_in, params) = refs[:8]
     (
         normed_out, w_out, x_out, delta_out, gy_out, cext_out, hist_out, branch_out, dout_out, dwg_out, ggp_out,
         proj_ref, rank_ref, all_notes, last_ref, leaving_ref,
-    ) = refs[11:27]
+    ) = refs[8:24]
     (
         tok, cot_s, wc, wg, cext, xb, x_s, delta_s, gy_s, gate_s, gg_s, gain_ref, alive_ref, sel, bc, ends, entered,
-        delta_sum, hist, y_s, gated, ggp, branch_s, turned, d_stage, w_stage,
-    ) = refs[27:53]
+        delta_sum, hist, y_s, gated, ggp, branch_s, turned, d_stage, w_stage, gate_b, dt_w, a_ref,
+    ) = refs[24:53]
     token_sems, cot_sems = refs[53:56], refs[56:59]
     part, near, total, mail, far, out, sems = refs[59:66]
     carry = Carry(seq, ends, alive_ref, entered, *refs[66:69])
+    taps_ref, bias_ref, dt_bias_ref = params.at[0:KC], params.at[KC : KC + 1], params.at[KC + 1 : KC + 2]
     (
         note_send, note_recv, wc_send, wc_recv, wg_send, wg_recv, halo_send, halo_recv, out_sems, hist_sems, branch_sems,
     ) = refs[69:]
@@ -418,9 +427,11 @@
     norm(me, 0, tt)
     swap_on(wc, wc_send, wc_recv)
     sel[...] = selector(LANES)
+    a_ref[...] = decay_rates(params) * LOG2E
+    dt_w[0:R, :] = dt_in[...]
+    dt_w[R:, :] = jnp.zeros((LANES - R, el), bf16)
     for k in range(token_rows.steps):
         token_rows.step(k)
-    cot_rows.start()
     token_rows.paired(norm_half)
     token_rows.drain()
     for m in masks_of(token_rows.orders[0])[1:]:
@@ -511,12 +522,11 @@
 
         by_tiles(tt, 64, body)
 
-    def between():
+    def second_wave():
+        cot_rows.start()
         swap(1, wg, wg_send, wg_recv)
-        for k in range(cot_rows.steps):
-            cot_rows.step(k)
-
-    exchange_sums(size, near, total, mail, far, out, sems, use, between)
+
+    exchange_sums(size, near, total, mail, far, out, sems, use, second_wave)
     for j in range(half):
         pltpu.make_async_remote_copy(
             src_ref=part.at[j], dst_ref=near.at[j], send_sem=sems.at[0, j], recv_sem=sems.at[1, j],
@@ -543,10 +553,7 @@
         return [jnp.broadcast_to(a_ref[n : n + 1, lanes], (nr, LANES)) for n in ns]
 
     def ends_forward(c, none):
-        @pl.when(c == count // 2)
-        def _():
-            swap_on(wg, wg_send, wg_recv)
-
+        pl.when(c == count // 2)(functools.partial(cot_rows.step, 0))
         spread_chunk(c, 0, NS)
         for b in range(blocks):
             lanes = slice(b * LANES, (b + 1) * LANES)
@@ -578,72 +585,9 @@
             ends[1, n, :, lanes] = jnp.exp2(delta_sum[b] * a_ref[n : n + 1, lanes])
     carry.turn(0, 0)
 
-    cot_rows.own()
-    cot_rows.paired()
-    swapped(wg, wg_send, wg_recv)
-    put(wg, w_out.at[:, :, pl.ds(el, el)])
-
-    def gates(p):
-        weight = wg[...].reshape(size * share, el)
-        gate_s[...] = jnp.dot(normed[p], weight, preferred_element_type=f32)
-        gg_s[...] = lax.dot_general(
-            cot_s[p], out_w[...], (((1,), (1,)), ((), ())), preferred_element_type=f32
-        )
-
-    def grad_y(p, none):
-        gates(p)
-
-        def body(span):
-            gate = gate_s[span, :]
-            gy = gg_s[span, :] * gate / (1.0 + jnp.exp(-gate))
-            for b in range(blocks):
-                there = pl.ds(p + span.start * size, tile, stride=size)
-                gy_s[b, there, :] = gy[:, b * LANES : (b + 1) * LANES]
-
-        by_tiles(tt, tile, body)
-        return none
-
-    lax.fori_loop(0, size, grad_y, 0)
-    put(gy_s, gy_out)
-    carry.turn(0, 1)
-
-    def hops(way, c, first):
-        @pl.when(lax.rem(c, 2) == 1)
-        def _():
-            carry.turn(way, lax.div(c, 2) + first)
-
-    def ends_back(c, none):
-        spread_chunk(c, NS, 2 * NS)
-        for b in range(blocks):
-            lanes = slice(b * LANES, (b + 1) * LANES)
-            for n0 in (0, NS // 2):
-                ns = range(n0, n0 + NS // 2)
-                rate = rates(ns, lanes)
-
-                def steps(s, carried):
-                    through, back = (list(v) for v in carried)
-                    for u in range(uu):
-                        here, close = token(c, s * uu + u)
-                        delta = delta_s[b, here, :]
-                        gy = gy_s[b, here, :]
-                        for i, n in enumerate(ns):
-                            c_at = (NS + n) * LANES
-                            through[i] = through[i] * jnp.exp2(delta * rate[i])
-                            back[i] = back[i] + through[i] * (gy * bc[close, c_at : c_at + LANES])
-                    return tuple(through), tuple(back)
-
-                start = tuple(tuple(ends[k, n, :, lanes] for n in ns) for k in (3, 2))
-                last = lax.fori_loop(0, ct // uu, steps, start)
-                for i, n in enumerate(ns):
-                    ends[3, n, :, lanes] = last[0][i]
-                    ends[2, n, :, lanes] = last[1][i]
-        hops(0, c, 2)
-        return none
-
-    lax.fori_loop(0, count, ends_back, 0)
-    for t in range(count // 2 + 2, seq):
+    for t in range(1, seq):
         carry.turn(0, t)
-    carry.turn(1, 0)
+    swap_on(wg, wg_send, wg_recv)
     last_ref[...] = entered[0]
 
     def store_hist(c):
@@ -657,6 +601,8 @@
         def _():
             store_hist(c - 2).wait()
 
+        for k in range(1, cot_rows.steps):
+            pl.when(c == min(count // 2 + k - 1, count - 1))(functools.partial(cot_rows.step, k))
         spread_chunk(c, 0, 2 * NS)
         for b in range(blocks):
             lanes = slice(b * LANES, (b + 1) * LANES)
@@ -686,13 +632,68 @@
             for n in range(NS):
                 last_ref[n, :, lanes] = last[n]
         store_hist(c).start()
-        hops(1, c, 1)
         return none
 
     lax.fori_loop(0, count, forward, 0)
-    for t in range(count // 2 + 1, seq):
-        carry.turn(1, t)
-    leaving_ref[...] = entered[1]
+    cot_rows.own()
+    cot_rows.paired()
+    swapped(wg, wg_send, wg_recv)
+    put(wg, w_out.at[:, :, pl.ds(el, el)])
+
+    def gates(p):
+        weight = wg[...].reshape(size * share, el)
+        gate_s[...] = jnp.dot(normed[p], weight, preferred_element_type=f32)
+        gg_s[...] = lax.dot_general(
+            cot_s[p], out_w[...], (((1,), (1,)), ((), ())), preferred_element_type=f32
+        )
+
+    def grad_y(p, none):
+        gates(p)
+
+        def body(span):
+            gate, gg = gate_s[span, :], gg_s[span, :]
+            gate_b[p, span, :] = gate.astype(bf16)
+            ggp[p, span, :] = gg.astype(bf16)
+            gy = gg * gate / (1.0 + jnp.exp(-gate))
+            for b in range(blocks):
+                there = pl.ds(p + span.start * size, tile, stride=size)
+                gy_s[b, there, :] = gy[:, b * LANES : (b + 1) * LANES]
+
+        by_tiles(tt, tile, body)
+        return none
+
+    lax.fori_loop(0, size, grad_y, 0)
+    put(gy_s, gy_out)
+
+    def ends_back(c, none):
+        spread_chunk(c, NS, 2 * NS)
+        for b in range(blocks):
+            lanes = slice(b * LANES, (b + 1) * LANES)
+            for n0 in (0, NS // 2):
+                ns = range(n0, n0 + NS // 2)
+                rate = rates(ns, lanes)
+
+                def steps(s, carried):
+                    through, back = (list(v) for v in carried)
+                    for u in range(uu):
+                        here, close = token(c, s * uu + u)
+                        delta = delta_s[b, here, :]
+                        gy = gy_s[b, here, :]
+                        for i, n in enumerate(ns):
+                            c_at = (NS + n) * LANES
+                            through[i] = through[i] * jnp.exp2(delta * rate[i])
+                            back[i] = back[i] + through[i] * (gy * bc[close, c_at : c_at + LANES])
+                    return tuple(through), tuple(back)
+
+                start = tuple(tuple(ends[k, n, :, lanes] for n in ns) for k in (3, 2))
+                last = lax.fori_loop(0, ct // uu, steps, start)
+                for i, n in enumerate(ns):
+                    ends[3, n, :, lanes] = last[0][i]
+                    ends[2, n, :, lanes] = last[1][i]
+        return none
+
+    lax.fori_loop(0, count, ends_back, 0)
+    carry.turn(1, 0)
 
     def store_branch(i):
         slot = lax.rem(i, 2)
@@ -703,15 +704,13 @@
         turned[:, columns] = jnp.transpose(value.astype(f32)).astype(bf16)
 
     def products(p, none):
-        gates(p)
-
         def body(span):
             there = pl.ds(p + span.start * size, tile, stride=size)
             y = jnp.concatenate([y_s[b, there, :] for b in range(blocks)], axis=1)
-            gate = gate_s[span, :]
+            gate = gate_b[p, span, :].astype(f32)
             sig = 1.0 / (1.0 + jnp.exp(-gate))
             gated[span, :] = (y * gate * sig).astype(bf16)
-            ggp[p, span, :] = (gg_s[span, :] * y * sig * (1.0 + gate * (1.0 - sig))).astype(bf16)
+            ggp[p, span, :] = (ggp[p, span, :].astype(f32) * y * sig * (1.0 + gate * (1.0 - sig))).astype(bf16)
 
         by_tiles(tt, tile, body)
 
@@ -723,9 +722,16 @@
         branch_s[lax.rem(p, 2)] = branch.astype(bf16)
         store_branch(p).start()
         turn(gated[...], p)
+
+        @pl.when(lax.rem(p, 2) == 1)
+        def _():
+            carry.turn(1, lax.div(p, 2) + 1)
+
         return none
 
     lax.fori_loop(0, size, products, 0)
+    for t in range(half + 1, seq):
+        carry.turn(1, t)
     put(ggp, ggp_out)
     wide = 384
     group = wide // share
@@ -759,6 +765,7 @@
         store_hist(c).wait()
     for p in range(size - 2, size):
         store_branch(p).wait()
+    leaving_ref[...] = entered[1]
     carry.drain()
 
     for i in range(size):
@@ -776,7 +783,7 @@
         copy.wait()
 
 
-def front(tokens, cot, notes, w_local, out_w, x_w, dt_w, taps, bias, dt_bias, rate, size, seq, direct):
+def front(tokens, cot, notes, w_local, out_w, x_w, dt_w, params, size, seq, direct):
     tt, width = tokens.shape
     el = out_w.shape[0]
     share = width // size
@@ -800,11 +807,12 @@
         ((LANES, 2 * NS * LANES), bf16), ((ct * size, 2 * NS * LANES), f32), ((4,) + states, f32), ((2,) + states, f32),
         ((blocks, size, LANES), f32), ((2, ct, blocks, NS * size, LANES), bf16), (scan, f32), ((tt, el), bf16), (channels, bf16),
         ((2, tt, width), bf16), ((el, size * tt), bf16), ((el, width), bf16), (weights, bf16),
+        (channels, bf16), ((LANES, el), bf16), ((NS, el), f32),
     ]
     one = pltpu.SemaphoreType.DMA((size,))
     return pl.pallas_call(
-        functools.partial(front_kernel, size, seq, direct, ct, ct),
-        in_specs=[away] * 4 + [here] * 7,
+        functools.partial(front_kernel, size, seq, direct, ct, max(1, ct * 8 // size)),
+        in_specs=[away] * 4 + [here] * 4,
         out_specs=[away] * 11 + [here] * 5,
         out_shape=[jax.ShapeDtypeStruct(*v) for v in shapes],
         scratch_shapes=[pltpu.VMEM(*v) for v in scratch]
@@ -823,7 +831,7 @@
             vmem_limit_bytes=63 * MIB, collective_id=0, has_side_effects=True
         ),
         name="front",
-    )(tokens, cot, notes, w_local, out_w, x_w, dt_w, taps, bias, dt_bias, rate)
+    )(tokens, cot, notes, w_local, out_w, x_w, dt_w, params)
 
 
 class RowScatter:
@@ -1002,7 +1010,7 @@
                         value = -value
                     for way in ways:
                         value = value + self.land[way, n].astype(jnp.float32)
-                    total[n] = value.astype(jnp.bfloat16)
+                    total(n, value.astype(jnp.bfloat16))
 
     def run(self, first, last, total):
         def body(step, none):
@@ -1068,13 +1076,13 @@
 
 
 def backward_kernel(size, seq, nr, tt, ct, uu, *refs):
-    delta_in, x_in, gy_in, hist_in, proj_ref, a_ref, carry_ref, last_ref, branch, out_w, gate_w = refs[:11]
-    gdelta_out, gx_out, gate_out, gbc_ref, grate_ref, branch_own, total = refs[11:18]
-    sel, bc, hist, prod, state_ref, after_ref, fold, delta_ref, x_ref, gy_ref, gdelta_ref, gx_ref, gate_s = refs[18:31]
-    sems, out_sems, hist_sems = refs[31:34]
-    scatter = RowScatter(size, branch, *refs[34:40])
-    chain = SeqSum(seq, 3, *refs[40:45])
-    gate_send, gate_recv, gate_sem = refs[45:]
+    delta_in, x_in, gy_in, hist_in, proj_ref, params, carry_ref, last_ref, branch, out_w, gate_w = refs[:11]
+    gdelta_out, gx_out, gate_out, gbc_ref, grate_ref, branch_own, out_sum, gate_sum = refs[11:19]
+    sel, bc, hist, prod, state_ref, after_ref, fold, delta_ref, x_ref, gy_ref, gdelta_ref, gx_ref, gate_s, a_ref = refs[19:33]
+    sems, out_sems, hist_sems = refs[33:36]
+    scatter = RowScatter(size, branch, *refs[36:42])
+    chain = SeqSum(seq, 3, *refs[42:47])
+    gate_send, gate_recv, gate_sem = refs[47:]
     el = a_ref.shape[1]
     blocks = el // LANES
     count = tt // ct
@@ -1099,6 +1107,21 @@
         return gate_s.at[m - early], gate_recv.at[m], gate_send.at[m, 0]
 
     swap_blocks(size, gate_w, slots)
+    a_ref[...] = decay_rates(params) * LOG2E
+    piece = chain.held.shape[1:]
+
+    def total(n, value):
+        @pl.when(n < first)
+        def _():
+            across = out_sum.shape[1] // piece[1]
+            down = pl.multiple_of(lax.div(n, across) * piece[0], piece[0])
+            along = pl.multiple_of(lax.rem(n, across) * piece[1], LANES)
+            out_sum[pl.ds(down, piece[0]), pl.ds(along, piece[1])] = value
+
+        @pl.when(n >= first)
+        def _():
+            gate_sum[n - first] = value
+
     sel[...] = selector(LANES)
     fold_row = lax.broadcasted_iota(jnp.int32, fold.shape, 0) // LANES
     fold_col = lax.broadcasted_iota(jnp.int32, fold.shape, 1)
@@ -1201,9 +1224,9 @@
         copy.wait()
 
 
-def scan_backward(delta, x, gy, hist, proj, rate, carry, last, branch, out_w, gate_w, size, seq):
+def scan_backward(delta, x, gy, hist, proj, params, carry, last, branch, out_w, gate_w, size, seq):
     nr, tt, width = branch.shape
-    el = rate.shape[1]
+    el = params.shape[1]
     blocks = el // LANES
     ct = math.gcd(tt, 32)
     here = pl.BlockSpec(memory_space=pltpu.VMEM)
@@ -1214,9 +1237,9 @@
     early = early_blocks(size)
     chunks = out_w.size // math.prod(piece) + 2 * early
     return pl.pallas_call(
-        functools.partial(backward_kernel, size, seq, nr, tt, ct, ct),
+        functools.partial(backward_kernel, size, seq, nr, tt, ct, max(1, ct * 8 // size)),
         in_specs=[away] * 4 + [here] * 4 + [away] * 3,
-        out_specs=[away] * 3 + [here] * 4,
+        out_specs=[away] * 3 + [here] * 5,
         out_shape=[
             jax.ShapeDtypeStruct(scan, f32),
             jax.ShapeDtypeStruct(scan, f32),
@@ -1224,7 +1247,8 @@
             jax.ShapeDtypeStruct((tt * nr, LANES), f32),
             jax.ShapeDtypeStruct((NS, nr, el), f32),
             jax.ShapeDtypeStruct((tt, width), bf16),
-            jax.ShapeDtypeStruct((chunks,) + piece, bf16),
+            jax.ShapeDtypeStruct(out_w.shape, bf16),
+            jax.ShapeDtypeStruct((2 * early,) + piece, bf16),
         ],
         scratch_shapes=[
             pltpu.VMEM((LANES, 2 * NS * LANES), bf16),
@@ -1238,6 +1262,7 @@
         + [pltpu.VMEM(scan, f32)] * 5
         + [
             pltpu.VMEM((size - early,) + gate_w.shape[1:], bf16),
+            pltpu.VMEM((NS, el), f32),
             pltpu.SemaphoreType.DMA((3,)),
             pltpu.SemaphoreType.DMA((2,)),
             pltpu.SemaphoreType.DMA((2,)),
@@ -1249,7 +1274,7 @@
             vmem_limit_bytes=62 * MIB, collective_id=3, has_side_effects=True
         ),
         name="scan_backward",
-    )(delta, x, gy, hist, proj, rate, carry, last, branch, out_w, gate_w)
+    )(delta, x, gy, hist, proj, params, carry, last, branch, out_w, gate_w)
 
 
 def small_rows(piece_rows):
@@ -1259,17 +1284,18 @@
 
 def back_kernel(size, seq, *refs):
     gdelta_in, gx_in, delta_in, normed_in, w_in, cext_in, ggp_in, gbc_in, gate_w = refs[:9]
-    rank_ref, dt_w, x_w, taps_ref, bias_ref, rate_ref, grate_ref = refs[9:16]
-    own, sums = refs[16:18]
+    rank_ref, dt_in, x_w, params, grate_ref, gate_sum = refs[9:15]
+    own, in_sum, small_sum = refs[15:18]
+    taps_ref, bias_ref = params.at[0:KC], params.at[KC : KC + 1]
     (
         gdelta, gx, delta, normed, wv, cext, gmix, gbc, low, gcp, turned, w_stage, acc_x, acc_dt, acc,
-        small, hmail, hland, stage, gco,
-    ) = refs[18:38]
-    part, near, total, mail, far, out, sems = refs[38:45]
-    scatter = RowScatter(size, None, *refs[45:51])
-    chain = SeqSum(seq, 4, *refs[51:56])
+        small, hmail, hland, stage, gco, dt_w,
+    ) = refs[18:39]
+    part, near, total, mail, far, out, sems = refs[39:46]
+    scatter = RowScatter(size, None, *refs[46:52])
+    chain = SeqSum(seq, 4, *refs[52:57])
     held, fill_sem = chain.held, chain.fill_sem
-    swap_send, in_sems, halo_send, halo_recv = refs[56:]
+    swap_send, in_sems, halo_send, halo_recv = refs[57:]
     me, parity, partner, others = row_peers(size)
     place = lax.axis_index("seq")
     share, el = w_stage.shape[1:]
@@ -1292,6 +1318,34 @@
     for copy in copies[:3]:
         copy.wait()
 
+    dt_w[0:R, :] = dt_in[...]
+    dt_w[R:, :] = jnp.zeros((LANES - R, el), bf16)
+    rows = held.shape[1]
+    halves = share // rows
+    first = small_rows(rows) // rows
+    before = early_blocks(size)
+
+    def place_in(m, i, gate, value):
+        along = pl.multiple_of((gate * size + crossed(me, m, size)) * el, LANES)
+        in_sum[pl.ds(pl.multiple_of(i * rows, rows), rows), pl.ds(along, el)] = value
+
+    def sums(n, value):
+        @pl.when(n < early)
+        def _():
+            place_in(before + lax.div(n, halves), lax.rem(n, halves), 1, value)
+
+        @pl.when((n >= early) & (n < early + first))
+        def _():
+            small_sum[pl.ds(pl.multiple_of((n - early) * rows, rows), rows), :] = value
+
+        @pl.when(n >= early + first)
+        def _():
+            k = n - early - first
+            place_in(lax.div(k, halves), lax.rem(k, halves), 0, value)
+
+    for n in range(before * halves):
+        place_in(n // halves, n % halves, 1, gate_sum[n])
+
     def fold8(value):
         return jnp.sum(value.reshape(value.shape[0] // 8, 8, value.shape[1]), axis=0)
 
@@ -1419,15 +1473,14 @@
         return none
 
     lax.fori_loop(0, width // 384, weights, 0)
-    rows = 2 * LANES
+    top = 2 * LANES
     small[0:LANES, :] = acc_x[...].astype(bf16)
-    small[LANES:rows, :] = acc_dt[...].astype(bf16)
-    rate_sum = jnp.sum(grate_ref[...], axis=1) * rate_ref[...]
+    small[LANES:top, :] = acc_dt[...].astype(bf16)
+    rate_sum = jnp.sum(grate_ref[...], axis=1) * decay_rates(params)
     last = [rate_sum] + [jnp.sum(acc[k], axis=0, keepdims=True) for k in range(KC + 2)]
     last.append(jnp.zeros((16 - KC - 2, el), f32))
-    small[rows : rows + 32, :] = jnp.concatenate(last, axis=0).astype(bf16)
+    small[top : top + 32, :] = jnp.concatenate(last, axis=0).astype(bf16)
     late = fill_chunks(held, fill_sem, small, early)
-    halves = share // held.shape[1]
 
     def slots(m, i):
         n = late + m * halves + i
@@ -1476,7 +1529,7 @@
 
 
 def back(
-    gdelta, gx, delta, normed, w_in, cext, ggp, gbc, rank, dt_w, x_w, taps, bias, rate, grate, gate_w, size, seq
+    gdelta, gx, delta, normed, w_in, cext, ggp, gbc, gate_w, rank, dt_w, x_w, params, grate, gate_sum, size, seq
 ):
     away = pl.BlockSpec(memory_space=pl.ANY)
     here = pl.BlockSpec(memory_space=pltpu.VMEM)
@@ -1493,14 +1546,16 @@
         ((size, tt + 8, el), f32), ((el, size * tt), bf16), ((size, share, el), bf16), ((LANES, el), f32),
         ((LANES, el), f32), ((KC + 2, 8, el), f32), ((low, el), bf16), ((size, 16, el), bf16),
         ((size, 16, el), bf16), ((size // 2, tt, width), bf16), ((tt, el), f32),
+        ((LANES, el), bf16),
     ]
     return pl.pallas_call(
         functools.partial(back_kernel, size, seq),
-        in_specs=[away] * 9 + [here] * 7,
-        out_specs=[here] * 2,
+        in_specs=[away] * 9 + [here] * 6,
+        out_specs=[here] * 3,
         out_shape=[
             jax.ShapeDtypeStruct((tt, width), bf16),
-            jax.ShapeDtypeStruct((chunks,) + piece, bf16),
+            jax.ShapeDtypeStruct((share, 2 * size * el), bf16),
+            jax.ShapeDtypeStruct((low, el), bf16),
         ],
         scratch_shapes=[pltpu.VMEM(*v) for v in scratch]
         + sum_scratch(size, tt)
@@ -1516,7 +1571,7 @@
             vmem_limit_bytes=63 * MIB, collective_id=4, has_side_effects=True
         ),
         name="back",
-    )(gdelta, gx, delta, normed, w_in, cext, ggp, gbc, gate_w, rank, dt_w, x_w, taps, bias, rate, grate)
+    )(gdelta, gx, delta, normed, w_in, cext, ggp, gbc, gate_w, rank, dt_w, x_w, params, grate, gate_sum)
 
 
 def local(
@@ -1547,39 +1602,28 @@
         w_local = jnp.moveaxis(in_proj.reshape(share, 2, size, el), 2, 0)
         w_local = widen(w_local, 3).reshape(size, share, 2 * elp)
     out_proj, x_proj = widen(out_proj, 0), widen(x_proj, 0)
-    dt_pad = widen(jnp.pad(dt_proj, ((0, LANES - R), (0, 0))), 1)
-    taps = widen(conv_weight.astype(f32), 1)
-    bias = widen(conv_bias.astype(f32), 0)[None]
-    rate = widen(-jnp.exp(a_log.astype(f32)), 1)
+    dt_proj = widen(dt_proj, 1)
+    params = [conv_weight, conv_bias[None], dt_bias[None], jnp.zeros((8 - KC - 2, el), bf16), a_log]
+    params = widen(jnp.concatenate(params, axis=0).astype(f32), 1)
     notes = jnp.zeros((16, -(-share // 256) * 256), bf16)
     notes = notes.at[0, :share].set(norm_gain).at[1].set(1.0 - resets[0, 0].astype(bf16))
     (
         normed, w_in, x_t, delta_t, gy_t, conv_ext, hist, branch, grad_out_proj, grad_in_gate, grad_gate_pre, proj_t,
         rank_all, all_notes, last, carry_back,
     ) = front(
-        tokens[0], cotangent[0], notes, w_local, out_proj, x_proj, dt_pad, taps, bias,
-        widen(dt_bias.astype(f32), 0)[None], rate * LOG2E, size, seq, direct,
+        tokens[0], cotangent[0], notes, w_local, out_proj, x_proj, dt_proj, params, size, seq, direct
     )
     gain = all_notes[:, 0, :share].reshape(D).astype(f32)
-    grad_delta, grad_input, gate_blocks, grad_bc, grate, branch_own, summed_out = scan_backward(
-        delta_t, x_t, gy_t, hist, proj_t, rate * LOG2E, carry_back, last, branch,
-        grad_out_proj[:el], grad_in_gate, size, seq,
+    grad_delta, grad_input, gate_blocks, grad_bc, grate, branch_own, sum_out, gate_sum = scan_backward(
+        delta_t, x_t, gy_t, hist, proj_t, params, carry_back, last, branch, grad_out_proj[:el], grad_in_gate, size, seq
     )
-    grad_normed, summed = back(
-        grad_delta, grad_input, delta_t, normed.reshape(count, D), w_in, conv_ext, grad_gate_pre, grad_bc, rank_all,
-        dt_pad, x_proj, taps, bias, rate, grate, gate_blocks, size, seq,
+    grad_normed, sum_in, small = back(
+        grad_delta, grad_input, delta_t, normed.reshape(count, D), w_in, conv_ext, grad_gate_pre, grad_bc, gate_blocks,
+        rank_all, dt_proj, x_proj, params, grate, gate_sum, size, seq,
     )
-    block = (share, elp)
-    early = 2 * early_blocks(size)
-    out_rows, out_cols = 2 * el // share, D // elp
-    sum_out = summed_out[:-early].reshape(out_rows, out_cols, share // 2, elp)
-    sum_out = jnp.swapaxes(sum_out, 1, 2).reshape(el, D).astype(f32)
-    rest = 2 * size - early
-    small = summed[rest : -2 * size].reshape(-1, elp)[:, :el].astype(f32)
-    order = jnp.array(range(size)) ^ lax.axis_index("rows")
-    sum_gate = jnp.concatenate([summed_out[-early:], summed[:rest]])
-    sum_in = [part.reshape((size,) + block)[order] for part in (summed[-2 * size :], sum_gate)]
-    sum_in = jnp.transpose(jnp.stack(sum_in)[..., :el].astype(f32), (2, 0, 1, 3)).reshape(share, 2 * E)
+    sum_in = sum_in.reshape(share, 2, size, elp)[..., :el].reshape(share, 2 * E).astype(f32)
+    sum_out = sum_out.astype(f32)
+    small = small[:, :el].astype(f32)
     block_out = (tokens.astype(jnp.float32) + branch_own[None].astype(jnp.float32)).astype(jnp.bfloat16)
     grad_normed = grad_normed[None].astype(jnp.float32)
 

time: 363 us -> 333 us (0.917)
  Pallas kernels: 331 us -> 310 us
  local copies, waits for them, and re-layouts: 21.3 us -> 8.89 us
  other arithmetic: 7.52 us -> 12.3 us
    pallas_call x1, Pallas kernels: 178 us -> 158 us  [front(): pl.pallas_call(functools.partial(front_kernel, size, seq, direct, ct, max...]
    slice x5 -> x0, local copies, waits for them, and re-layouts: 4.72 us -> none  [the longest x2 2.25 us: local(): sum_gate = jnp.concatenate([summed_out[-early:], summed[:rest]])]
    unnamed x21 -> x17, local copies, waits for them, and re-layouts: 4.95 us -> 0.85 us
where the time goes in v6:
time: 333 us
  Pallas kernels  310 us (93%)
  other arithmetic  12.3 us (4%)
  local copies, waits for them, and re-layouts  8.89 us (3%)
    pallas_call x1, Pallas kernels, front(): pl.pallas_call(functools.partial(front_kernel, size, seq, direct, ct, max...  158 us
    pallas_call x1, Pallas kernels, back(): pl.pallas_call(functools.partial(back_kernel, size, seq), in_specs=[away]...  93 us
    pallas_call x1, Pallas kernels, scan_backward(): pl.pallas_call(functools.partial(backward_kernel, size, seq, nr, tt, ct,...  59.3 us

profile of v6, /device:TPU:0, one launch (start us, length us, event | category | flops | bytes accessed | tf_op | source)
XLA Modules:
  0.0 332.8 jit_solution(4163074490848580074)
XLA Ops:
  0.6 1.2 slice.69
  2.5 0.7 reshape.120
  3.1 0.7 broadcast_in_dim.6
  3.8 0.7 broadcast_in_dim.7
  4.6 0.0 copy-start.6
  4.6 1.4 concatenate.7
  6.0 0.6 convert_element_type.54.refs_7_.refs_5_.refs_12_
  6.6 0.0 copy-done.6
  6.6 157.8 %front.1 = (bf16[8,256,1536]{2,1,0:T(8,128)(2,1)}, bf16[8,192,768]{2,1,0:T(8,128)(2,1)}, f32[3,2048,128]{2,1,0:T(8,128)}, f32[3,2048,128]{2,1,0:T(8,128)}, f32[3...) custom-call(bf16[256,1536]{1,0:T(8,128)(2,1)} %bitcast.12, ...), custom_call_target="tpu_custom_call" | custom-call | tf_op jit(solution)/shard_map/front/pallas_call | solution.py:813
  164.5 59.3 %scan_backward.1 = (f32[3,2048,128]{2,1,0:T(8,128)}, f32[3,2048,128]{2,1,0:T(8,128)}, bf16[6,192,384]{2,1,0:T(8,128)(2,1)}, f32[2048,128]{1,0:T(8,128)}, f32[16,...) custom-call(f32[3,2048,128]{2,1,0:T(8,128)} %get-tuple-element.62.refs_0_.r, ...), custom_call_target="tpu_custom_call" | custom-call | tf_op jit(solution)/shard_map/scan_backward/pallas_call | solution.py:1239
  223.8 0.0 copy-start.1
  223.8 93.0 %back.1 = (bf16[256,1536]{1,0:T(8,128)(2,1)}, bf16[192,6144]{1,0:T(8,128)(2,1)}, bf16[288,384]{1,0:T(8,128)(2,1)}) custom-call(f32[3,2048,128]{2,1,0:T(8,128)} %get-tuple-element.73.refs_0_, f32[3,2048,128]{2,1,0:T(8,128)} %get-tuple-element.74.refs_1_, f32[3,2048,128]{2,1,0:T(8,128)} %get-tuple-element.62.refs_0_.refs_2_, bf16[2048,1536]{1,0:T(8,128)(2,1)} %bitcast.13, ...), custom_call_target="tpu_custom_call" | custom-call | tf_op jit(solution)/shard_map/back/pallas_call | solution.py:1551
  316.8 0.0 copy-start.2
  316.8 0.0 copy-start.3
  316.8 1.4 slice.72
  318.2 0.8 convert_reduce_fusion
  319.0 0.1 reshape.123
  319.1 0.0 copy-done.1
  319.1 1.6 fusion.1
  320.7 0.0 copy-done.2
  320.7 0.0 copy-done.3
  320.7 0.0 copy-start.5
  320.7 2.9 fusion.6
  323.6 0.0 copy-done.5
  323.6 0.6 slice.75
  324.2 0.7 slice.71
  324.8 0.0 copy-start.4
  324.9 0.6 slice_reduce_fusion
  325.5 0.8 copy.23
  326.3 0.0 copy-start
  326.3 3.1 convert_element_type.67
  329.4 0.0 copy-done.4
  329.4 0.0 copy-done
  329.4 0.0 copy-start.7
  329.4 2.8 multiply_reduce_fusion
  332.2 0.0 copy-done.7
  332.2 0.6 convert_divide_fusion
  (7 shorter events, 0.1 us)
Async XLA Ops:
  4.6 2.1 copy-start.6
  223.8 95.3 %copy-start.1 = (bf16[1,256,1536]{2,1,0:T(8,128)(2,1)S(1)}, bf16[1,256,1536]{2,1,0:T(8,128)(2,1)}, u32[]{:S(2)}) copy-start(bf16[1,256,1536]{2,1,0:T(8,128)(2,1)} %param.16) | copy-start | bytes 2359300
  316.8 3.9 %copy-start.2 = (bf16[1,256,1536]{2,1,0:T(8,128)(2,1)S(1)}, bf16[1,256,1536]{2,1,0:T(8,128)(2,1)}, u32[]{:S(2)}) copy-start(bf16[1,256,1536]{2,1,0:T(8,128)(2,1)} %param.27) | copy-start | bytes 2359300
  316.8 3.9 %copy-start.3 = (bf16[256,1536]{1,0:T(8,128)(2,1)S(1)}, bf16[256,1536]{1,0:T(8,128)(2,1)}, u32[]{:S(2)}) copy-start(bf16[256,1536]{1,0:T(8,128)(2,1)} %get-tuple-element.84) | copy-start | bytes 2359300
  320.7 2.9 copy-start.5
  324.8 4.6 %copy-start.4 = (bf16[192,6144]{1,0:T(8,128)(2,1)S(1)}, bf16[192,6144]{1,0:T(8,128)(2,1)}, u32[]{:S(2)}) copy-start(bf16[192,6144]{1,0:T(8,128)(2,1)} %get-tuple-element.86) | copy-start | bytes 7077892
  326.3 3.1 copy-start
  329.4 2.8 copy-start.7

commit v7 on v6

--- a/solution.py
+++ b/solution.py
@@ -330,10 +330,10 @@
     (tokens, cot, notes, w_local, out_w, x_w, dt_in, params) = refs[:8]
     (
         normed_out, w_out, x_out, delta_out, gy_out, cext_out, hist_out, branch_out, dout_out, dwg_out, ggp_out,
-        proj_ref, rank_ref, all_notes, last_ref, leaving_ref,
+        proj_ref, rank_ref, last_ref, leaving_ref, gain_ref,
     ) = refs[8:24]
     (
-        tok, cot_s, wc, wg, cext, xb, x_s, delta_s, gy_s, gate_s, gg_s, gain_ref, alive_ref, sel, bc, ends, entered,
+        tok, cot_s, wc, wg, cext, xb, x_s, delta_s, gy_s, gate_s, gg_s, all_notes, alive_ref, sel, bc, ends, entered,
         delta_sum, hist, y_s, gated, ggp, branch_s, turned, d_stage, w_stage, gate_b, dt_w, a_ref,
     ) = refs[24:53]
     token_sems, cot_sems = refs[53:56], refs[56:59]
@@ -352,7 +352,7 @@
     blocks = el // LANES
     half = size // 2
     f32, bf16 = jnp.float32, jnp.bfloat16
-    tile = 32
+    tile = 64
     stores = []
 
     def put(source, target):
@@ -798,12 +798,12 @@
     shapes = [
         (rows, bf16), ((size, share, 2 * el), bf16), (scan, f32), (scan, f32), (scan, f32), (ext, bf16),
         ((tt, blocks, NS * size, LANES), bf16), (rows, bf16), ((el, width), bf16), (weights, bf16), (channels, bf16),
-        ((tt * size, LANES), f32), ((size, tt, LANES), bf16), ((size,) + notes.shape, bf16), (states, f32),
-        (states, f32),
+        ((tt * size, LANES), f32), ((size, tt, LANES), bf16), (states, f32), (states, f32),
+        ((1, width), f32),
     ]
     scratch = [
         (rows, bf16), (rows, bf16), (weights, bf16), (weights, bf16), (ext, bf16), ((tt, el), bf16), (scan, f32),
-        (scan, f32), (scan, f32), ((tt, el), f32), ((tt, el), f32), ((1, width), f32), ((size, LANES), f32),
+        (scan, f32), (scan, f32), ((tt, el), f32), ((tt, el), f32), ((size,) + notes.shape, bf16), ((size, LANES), f32),
         ((LANES, 2 * NS * LANES), bf16), ((ct * size, 2 * NS * LANES), f32), ((4,) + states, f32), ((2,) + states, f32),
         ((blocks, size, LANES), f32), ((2, ct, blocks, NS * size, LANES), bf16), (scan, f32), ((tt, el), bf16), (channels, bf16),
         ((2, tt, width), bf16), ((el, size * tt), bf16), ((el, width), bf16), (weights, bf16),
@@ -1358,14 +1358,14 @@
         def body(span):
             for b in range(blocks):
                 lanes = slice(b * LANES, (b + 1) * LANES)
-                there = pl.ds(p + span.start * size, 32, stride=size)
+                there = pl.ds(p + span.start * size, 64, stride=size)
                 dl = delta[b, there, :]
                 near_zero = dl * (1.0 - dl * (0.5 - dl * (1.0 / 6.0)))
                 value = gdelta[b, there, :] * jnp.where(dl < 0.01, near_zero, 1.0 - jnp.exp(-dl))
                 low[span, lanes] = value.astype(bf16)
                 acc[KC + 1, :, lanes] = acc[KC + 1, :, lanes] + fold8(value)
 
-        by_tiles(tt, 32, body)
+        by_tiles(tt, 64, body)
         value = lax.dot_general(low[...], dt_w[...], nt, preferred_element_type=f32)
         value = value + gbc[pl.ds(p, tt, stride=size), :]
         acc_dt[...] += lax.dot_general(rank_ref[p], low[...], tn, preferred_element_type=f32)
@@ -1387,36 +1387,32 @@
     lax.fori_loop(0, size, steps_back, 0)
     for copy in copies[3:]:
         copy.wait()
-    exchange_sums(size, near, total, mail, far, out, sems, lambda p: None)
-    for j in range(half):
-        wait_for(near.at[j], sems.at[0, j])
-
     def halo(p):
         return pltpu.make_async_remote_copy(
             src_ref=hmail.at[p], dst_ref=hland.at[p], send_sem=halo_send.at[p], recv_sem=halo_recv.at[p],
             device_id=(jnp.maximum(place - 1, 0), me), device_id_type=MESH,
         )
 
-    def conv_back(p, none):
+    def conv_back(p, step):
         gco[...] = lax.dot_general(out[p], x_w[...], nt, preferred_element_type=f32)
 
         def body(span):
             value = gco[span, :]
-            there = pl.ds(p + span.start * size, 32, stride=size)
+            there = pl.ds(p + span.start * size, 64, stride=size)
             value = value + jnp.concatenate([gx[b, there, :] for b in range(blocks)], axis=1)
-            ext = cext[p, pl.ds(span.start, 48), :].astype(f32)
+            ext = cext[p, pl.ds(span.start, 80), :].astype(f32)
             here = bias_ref[...]
             for k in range(KC):
-                here = here + taps_ref[k : k + 1, :] * ext[16 - KC + 1 + k : 16 - KC + 1 + k + 32]
+                here = here + taps_ref[k : k + 1, :] * ext[16 - KC + 1 + k : 16 - KC + 1 + k + 64]
             sig = 1.0 / (1.0 + jnp.exp(-here))
             low[span, :] = (here * sig).astype(bf16)
             value = value * sig * (1.0 + here * (1.0 - sig))
             gcp[p, span, :] = value
             acc[KC] = acc[KC] + fold8(value)
             for k in range(KC):
-                acc[k] = acc[k] + fold8(value * ext[16 - KC + 1 + k : 16 - KC + 1 + k + 32])
-
-        by_tiles(tt, 32, body)
+                acc[k] = acc[k] + fold8(value * ext[16 - KC + 1 + k : 16 - KC + 1 + k + 64])
+
+        by_tiles(tt, 64, body)
         acc_x[...] += lax.dot_general(out[p], low[...], tn, preferred_element_type=f32)
         hmail[p] = gcp[p, 0:16, :].astype(bf16)
 
@@ -1424,13 +1420,13 @@
         def _():
             halo(p).start()
 
-        @pl.when(p < early)
-        def _():
-            chain.advance(p, sums)
-
-        return none
-
-    lax.fori_loop(0, size, conv_back, 0)
+        if step < early:
+            chain.advance(step, sums)
+
+    steps_done = iter(range(size))
+    exchange_sums(size, near, total, mail, far, out, sems, lambda p: conv_back(p, next(steps_done)))
+    for j in range(half):
+        wait_for(near.at[j], sems.at[0, j])
 
     def turn(p, none):
         @pl.when(place < seq - 1)
@@ -1443,13 +1439,13 @@
             gcp[p, tt : tt + 8, :] = jnp.zeros((8, el), f32)
 
         def body(span):
-            ext = gcp[p, pl.ds(span.start, 40), :]
-            value = taps_ref[KC - 1 : KC, :] * ext[0:32]
+            ext = gcp[p, pl.ds(span.start, 72), :]
+            value = taps_ref[KC - 1 : KC, :] * ext[0:64]
             for k in range(KC - 1):
-                value = value + taps_ref[k : k + 1, :] * ext[KC - 1 - k : KC - 1 - k + 32]
+                value = value + taps_ref[k : k + 1, :] * ext[KC - 1 - k : KC - 1 - k + 64]
             gmix[p, span, 0:el] = value.astype(bf16)
 
-        by_tiles(tt, 32, body)
+        by_tiles(tt, 64, body)
         columns = pl.ds(pl.multiple_of(p * tt, tt), tt)
         turned[:, columns] = jnp.transpose(gmix[p, :, 0:el].astype(f32)).astype(bf16)
 
@@ -1609,11 +1605,10 @@
     notes = notes.at[0, :share].set(norm_gain).at[1].set(1.0 - resets[0, 0].astype(bf16))
     (
         normed, w_in, x_t, delta_t, gy_t, conv_ext, hist, branch, grad_out_proj, grad_in_gate, grad_gate_pre, proj_t,
-        rank_all, all_notes, last, carry_back,
+        rank_all, last, carry_back, gain,
     ) = front(
         tokens[0], cotangent[0], notes, w_local, out_proj, x_proj, dt_proj, params, size, seq, direct
     )
-    gain = all_notes[:, 0, :share].reshape(D).astype(f32)
     grad_delta, grad_input, gate_blocks, grad_bc, grate, branch_own, sum_out, gate_sum = scan_backward(
         delta_t, x_t, gy_t, hist, proj_t, params, carry_back, last, branch, grad_out_proj[:el], grad_in_gate, size, seq
     )
@@ -1621,7 +1616,7 @@
         grad_delta, grad_input, delta_t, normed.reshape(count, D), w_in, conv_ext, grad_gate_pre, grad_bc, gate_blocks,
         rank_all, dt_proj, x_proj, params, grate, gate_sum, size, seq,
     )
-    sum_in = sum_in.reshape(share, 2, size, elp)[..., :el].reshape(share, 2 * E).astype(f32)
+    sum_in = sum_in.reshape(share, 2, size, elp)[..., :el].reshape(share, 2 * E)
     sum_out = sum_out.astype(f32)
     small = small[:, :el].astype(f32)
     block_out = (tokens.astype(jnp.float32) + branch_own[None].astype(jnp.float32)).astype(jnp.bfloat16)
@@ -1629,7 +1624,7 @@
 
     own = tokens.astype(jnp.float32)
     inv = lax.rsqrt(jnp.mean(own * own, axis=2, keepdims=True) + epsilon)
-    gain_own = jnp.sum(in_proj.astype(jnp.float32) * sum_in, axis=1) / norm_gain.astype(jnp.float32)
+    gain_own = jnp.sum(in_proj.astype(f32) * sum_in.astype(f32), axis=1) / norm_gain.astype(jnp.float32)
     grad_hat = grad_normed * gain
     grad_norm_in = inv * (
         grad_hat - own * (inv * inv) * jnp.mean(grad_hat * own, axis=2, keepdims=True)
@@ -1641,7 +1636,7 @@
         block_out,
         d_tokens,
         gain_own,
-        sum_in,
+        sum_in.astype(f32),
         small[:LANES].T,
         small[LANES : LANES + R],
         more[NS : NS + KC],

time: 333 us -> 326 us (0.979)
  Pallas kernels: 310 us -> 304 us
    pallas_call x1, Pallas kernels: 93 us -> 87.8 us  [back(): pl.pallas_call(functools.partial(back_kernel, size, seq), in_specs=[away]...]
where the time goes in v7:
time: 326 us
  Pallas kernels  304 us (93%)
  other arithmetic  11.6 us (4%)
  local copies, waits for them, and re-layouts  8.82 us (3%)
    pallas_call x1, Pallas kernels, front(): pl.pallas_call(functools.partial(front_kernel, size, seq, direct, ct, max...  157 us
    pallas_call x1, Pallas kernels, back(): pl.pallas_call(functools.partial(back_kernel, size, seq), in_specs=[away]...  87.8 us
    pallas_call x1, Pallas kernels, scan_backward(): pl.pallas_call(functools.partial(backward_kernel, size, seq, nr, tt, ct,...  59.2 us

profile of v7, /device:TPU:0, one launch (start us, length us, event | category | flops | bytes accessed | tf_op | source)
XLA Modules:
  0.0 325.8 jit_solution(4495307246291065964)
XLA Ops:
  0.6 1.2 slice.65
  2.5 0.7 reshape.114
  3.1 0.7 broadcast_in_dim.6
  3.8 0.7 broadcast_in_dim.7
  4.6 0.0 copy-start.6
  4.6 1.4 concatenate.7
  6.0 0.6 convert_element_type.45.refs_7_.refs_5_.refs_12_
  6.6 0.0 copy-done.6
  6.6 156.9 %front.1 = (bf16[8,256,1536]{2,1,0:T(8,128)(2,1)}, bf16[8,192,768]{2,1,0:T(8,128)(2,1)}, f32[3,2048,128]{2,1,0:T(8,128)}, f32[3,2048,128]{2,1,0:T(8,128)}, f32[3...) custom-call(bf16[256,1536]{1,0:T(8,128)(2,1)} %bitcast.12, ...), custom_call_target="tpu_custom_call" | custom-call | tf_op jit(solution)/shard_map/front/pallas_call | solution.py:813
  163.5 59.2 %scan_backward.1 = (f32[3,2048,128]{2,1,0:T(8,128)}, f32[3,2048,128]{2,1,0:T(8,128)}, bf16[6,192,384]{2,1,0:T(8,128)(2,1)}, f32[2048,128]{1,0:T(8,128)}, f32[16,...) custom-call(f32[3,2048,128]{2,1,0:T(8,128)} %get-tuple-element.62.refs_0_.r, ...), custom_call_target="tpu_custom_call" | custom-call | tf_op jit(solution)/shard_map/scan_backward/pallas_call | solution.py:1239
  222.8 0.0 copy-start.7
  222.8 0.0 copy-start.1
  222.8 87.8 %back.1 = (bf16[256,1536]{1,0:T(8,128)(2,1)}, bf16[192,6144]{1,0:T(8,128)(2,1)}, bf16[288,384]{1,0:T(8,128)(2,1)}) custom-call(f32[3,2048,128]{2,1,0:T(8,128)} %get-tuple-element.73.refs_0_, f32[3,2048,128]{2,1,0:T(8,128)} %get-tuple-element.74.refs_1_, f32[3,2048,128]{2,1,0:T(8,128)} %get-tuple-element.62.refs_0_.refs_2_, bf16[2048,1536]{1,0:T(8,128)(2,1)} %bitcast.13, ...), custom_call_target="tpu_custom_call" | custom-call | tf_op jit(solution)/shard_map/back/pallas_call | solution.py:1547
  310.6 0.0 copy-start.2
  310.6 0.0 copy-start.3
  310.6 1.4 slice.68
  312.0 0.0 copy-done.7
  312.1 0.0 copy-done.1
  312.1 1.6 fusion.1
  313.7 0.0 copy-done.2
  313.7 0.0 copy-done.3
  313.7 0.0 copy-start.5
  313.7 2.9 fusion.6
  316.6 0.0 copy-done.5
  316.6 0.6 slice.71
  317.2 0.7 slice.67
  317.8 0.0 copy-start.4
  317.9 0.6 slice_reduce_fusion
  318.5 0.8 copy.23
  319.3 0.0 copy-start
  319.3 3.1 convert_element_type.56
  322.4 0.0 copy-done.4
  322.4 0.0 copy-done
  322.4 0.0 copy-start.8
  322.4 2.8 multiply_reduce_fusion
  325.2 0.0 copy-done.8
  325.2 0.6 convert_divide_fusion
  (8 shorter events, 0.1 us)
Async XLA Ops:
  4.6 2.1 copy-start.6
  222.8 89.3 %copy-start.7 = (f32[1,1536]{1,0:T(1,128)S(1)}, f32[1,1536]{1,0:T(1,128)}, u32[]{:S(2)}) copy-start(f32[1,1536]{1,0:T(1,128)} %get-tuple-element.85) | copy-start | bytes 18436
  222.8 89.3 %copy-start.1 = (bf16[1,256,1536]{2,1,0:T(8,128)(2,1)S(1)}, bf16[1,256,1536]{2,1,0:T(8,128)(2,1)}, u32[]{:S(2)}) copy-start(bf16[1,256,1536]{2,1,0:T(8,128)(2,1)} %param.16) | copy-start | bytes 2359300
  310.6 3.1 copy-start.2
  310.6 3.0 copy-start.3
  313.7 2.9 copy-start.5
  317.8 4.6 %copy-start.4 = (bf16[192,6144]{1,0:T(8,128)(2,1)S(1)}, bf16[192,6144]{1,0:T(8,128)(2,1)}, u32[]{:S(2)}) copy-start(bf16[192,6144]{1,0:T(8,128)(2,1)} %get-tuple-element.86) | copy-start | bytes 7077892
  319.3 3.1 copy-start
  322.4 2.8 copy-start.8

commit v8 on v7

--- a/solution.py
+++ b/solution.py
@@ -1601,8 +1601,11 @@
     dt_proj = widen(dt_proj, 1)
     params = [conv_weight, conv_bias[None], dt_bias[None], jnp.zeros((8 - KC - 2, el), bf16), a_log]
     params = widen(jnp.concatenate(params, axis=0).astype(f32), 1)
-    notes = jnp.zeros((16, -(-share // 256) * 256), bf16)
-    notes = notes.at[0, :share].set(norm_gain).at[1].set(1.0 - resets[0, 0].astype(bf16))
+    across = -(-share // 256) * 256
+    line = lax.broadcasted_iota(jnp.int32, (16, across), 0)
+    fresh = 1.0 - resets[:, :1].astype(bf16)
+    notes = jnp.where(line == 0, jnp.pad(norm_gain, (0, across - share))[None], jnp.where(line == 1, fresh, 0.0))
+    notes = notes.astype(bf16)
     (
         normed, w_in, x_t, delta_t, gy_t, conv_ext, hist, branch, grad_out_proj, grad_in_gate, grad_gate_pre, proj_t,
         rank_all, last, carry_back, gain,
@@ -1618,7 +1621,6 @@
     )
     sum_in = sum_in.reshape(share, 2, size, elp)[..., :el].reshape(share, 2 * E)
     sum_out = sum_out.astype(f32)
-    small = small[:, :el].astype(f32)
     block_out = (tokens.astype(jnp.float32) + branch_own[None].astype(jnp.float32)).astype(jnp.bfloat16)
     grad_normed = grad_normed[None].astype(jnp.float32)
 
@@ -1631,18 +1633,22 @@
     )
     d_tokens = (cotangent.astype(jnp.float32) + grad_norm_in).astype(jnp.bfloat16)
 
-    more = small[2 * LANES :]
+
+    def rows(first, last):
+        return small[first:last, :el].astype(f32)
+
+    top = 2 * LANES + NS
     return (
         block_out,
         d_tokens,
         gain_own,
         sum_in.astype(f32),
-        small[:LANES].T,
-        small[LANES : LANES + R],
-        more[NS : NS + KC],
-        more[NS + KC],
-        more[NS + KC + 1],
-        more[:NS],
+        rows(0, LANES).T,
+        rows(LANES, LANES + R),
+        rows(top, top + KC),
+        rows(top + KC, top + KC + 1)[0],
+        rows(top + KC + 1, top + KC + 2)[0],
+        rows(2 * LANES, top),
         sum_out,
     )
 

time: 326 us -> 329 us (level)
  other arithmetic: 11.6 us -> 17.9 us
  local copies, waits for them, and re-layouts: 8.82 us -> 5.47 us
where the time goes in v8:
time: 329 us
  Pallas kernels  304 us (92%)
  other arithmetic  17.9 us (5%)
  local copies, waits for them, and re-layouts  5.47 us (2%)
    pallas_call x1, Pallas kernels, front(): pl.pallas_call(functools.partial(front_kernel, size, seq, direct, ct, max...  157 us
    pallas_call x1, Pallas kernels, back(): pl.pallas_call(functools.partial(back_kernel, size, seq), in_specs=[away]...  87.8 us
    pallas_call x1, Pallas kernels, scan_backward(): pl.pallas_call(functools.partial(backward_kernel, size, seq, nr, tt, ct,...  59.2 us

profile of v8, /device:TPU:0, one launch (start us, length us, event | category | flops | bytes accessed | tf_op | source)
XLA Modules:
  0.0 328.8 jit_solution(101425433577472873)
XLA Ops:
  0.6 1.2 slice.29
  2.5 0.7 pad.4
  3.2 0.7 broadcast_in_dim.41
  3.8 0.7 broadcast_in_dim.42
  4.5 0.7 broadcast_select_fusion.refs_2_
  5.2 1.4 concatenate.3
  6.6 0.6 convert_element_type.57.refs_7_.refs_5_.refs_12_
  7.2 156.9 %front.1 = (bf16[8,256,1536]{2,1,0:T(8,128)(2,1)}, bf16[8,192,768]{2,1,0:T(8,128)(2,1)}, f32[3,2048,128]{2,1,0:T(8,128)}, f32[3,2048,128]{2,1,0:T(8,128)}, f32[3...) custom-call(bf16[256,1536]{1,0:T(8,128)(2,1)} %bitcast.12, ...), custom_call_target="tpu_custom_call" | custom-call | tf_op jit(solution)/shard_map/front/pallas_call | solution.py:813
  164.1 59.2 %scan_backward.1 = (f32[3,2048,128]{2,1,0:T(8,128)}, f32[3,2048,128]{2,1,0:T(8,128)}, bf16[6,192,384]{2,1,0:T(8,128)(2,1)}, f32[2048,128]{1,0:T(8,128)}, f32[16,...) custom-call(f32[3,2048,128]{2,1,0:T(8,128)} %get-tuple-element.38.refs_0_.r, ...), custom_call_target="tpu_custom_call" | custom-call | tf_op jit(solution)/shard_map/scan_backward/pallas_call | solution.py:1239
  223.4 0.0 copy-start.5
  223.4 0.0 copy-start.1
  223.4 87.8 %back.1 = (bf16[256,1536]{1,0:T(8,128)(2,1)}, bf16[192,6144]{1,0:T(8,128)(2,1)}, bf16[288,384]{1,0:T(8,128)(2,1)}) custom-call(f32[3,2048,128]{2,1,0:T(8,128)} %get-tuple-element.49.refs_0_, f32[3,2048,128]{2,1,0:T(8,128)} %get-tuple-element.50.refs_1_, f32[3,2048,128]{2,1,0:T(8,128)} %get-tuple-element.38.refs_0_.refs_2_, bf16[2048,1536]{1,0:T(8,128)(2,1)} %bitcast.13, ...), custom_call_target="tpu_custom_call" | custom-call | tf_op jit(solution)/shard_map/back/pallas_call | solution.py:1547
  311.2 0.0 copy-start.2
  311.2 0.0 copy-start.3
  311.2 1.4 convert_reduce_fusion
  312.7 1.3 slice_convert_fusion.2
  314.0 0.0 copy-done.5
  314.0 0.0 copy-done.1
  314.0 1.6 fusion.1
  315.6 0.0 copy-done.2
  315.6 0.0 copy-done.3
  315.6 0.0 copy-start.4
  315.6 2.9 fusion.6
  318.5 0.0 copy-done.4
  318.5 0.6 slice_convert_fusion.1
  319.1 0.7 slice_convert_fusion
  319.8 0.8 copy.23
  320.6 0.0 copy-start
  320.6 3.1 convert_element_type.70
  323.7 0.0 copy-done
  323.7 0.0 copy-start.6
  323.7 4.5 %multiply_reduce_fusion = (f32[192]{0:T(256)S(1)}, f32[192,6144]{1,0:T(8,128)}) fusion(bf16[192,6144]{1,0:T(8,128)(2,1)S(1)} %copy-done, bf16[192,6144]{1,0:T(8,128)(2,1)} %get-tuple-element.62), kind=kLoop, calls=%fused_computation | loop fusion | flops 4718400 | bytes 9437952 | tf_op jit(solution)/shard_map/reduce_sum | solution.py:1629
  328.2 0.0 copy-done.6
  328.2 0.6 convert_divide_fusion
  (6 shorter events, 0.1 us)
Async XLA Ops:
  223.4 90.6 %copy-start.5 = (f32[1,1536]{1,0:T(1,128)S(1)}, f32[1,1536]{1,0:T(1,128)}, u32[]{:S(2)}) copy-start(f32[1,1536]{1,0:T(1,128)} %get-tuple-element.61) | copy-start | bytes 18436
  223.4 90.6 %copy-start.1 = (bf16[1,256,1536]{2,1,0:T(8,128)(2,1)S(1)}, bf16[1,256,1536]{2,1,0:T(8,128)(2,1)}, u32[]{:S(2)}) copy-start(bf16[1,256,1536]{2,1,0:T(8,128)(2,1)} %param.12) | copy-start | bytes 2359300
  311.2 4.4 %copy-start.2 = (bf16[1,256,1536]{2,1,0:T(8,128)(2,1)S(1)}, bf16[1,256,1536]{2,1,0:T(8,128)(2,1)}, u32[]{:S(2)}) copy-start(bf16[1,256,1536]{2,1,0:T(8,128)(2,1)} %param.23) | copy-start | bytes 2359300
  311.2 4.4 %copy-start.3 = (bf16[256,1536]{1,0:T(8,128)(2,1)S(1)}, bf16[256,1536]{1,0:T(8,128)(2,1)}, u32[]{:S(2)}) copy-start(bf16[256,1536]{1,0:T(8,128)(2,1)} %get-tuple-element.60) | copy-start | bytes 2359300
  315.6 2.9 copy-start.4
  320.6 3.1 copy-start
  323.7 4.5 %copy-start.6 = (bf16[192]{0:T(256)(128)(2,1)S(1)}, bf16[192]{0:T(256)(128)(2,1)}, u32[]{:S(2)}) copy-start(bf16[192]{0:T(256)(128)(2,1)} %param.14) | copy-start | bytes 1156
